TPU v7x, 32 devices: a whole 2x2x4 slice. The times are simulated.
32 devices in a mesh: groups: 2 (over y), tensor: 4 (over z), dp: 2 (over x), pipe: 2 (over core).
Axes of the slice: x: 2, y: 2, z: 4, core: 2. Of those that a mesh axis runs over, the one named last changes fastest.
Arguments:
- queries: bfloat16 [2048, 8192], P(('groups', 'dp', 'pipe'), 'tensor'), parts along dimension 0, may hold values from -192 to 192
- incoming_key_value: bfloat16 [2048, 2048], P(('groups', 'dp', 'pipe'), 'tensor'), parts along dimension 0, may hold values from -6 to 6
- prefix_key_value_cache: bfloat16 [16, 2048, 2048], P(('groups', 'dp', 'pipe'), None, 'tensor'), parts along dimension 0, may hold values from -6 to 6
- prefix_length: int32 [16], P(('groups', 'dp', 'pipe')), parts along dimension 0, may hold values from 1 to 2048, as said below
- adapter: int32 [16], P(('groups', 'dp', 'pipe')), parts along dimension 0, may hold values from 0 to 3
- output_weight: bfloat16 [8192, 8192], P('tensor', ('dp', 'pipe')), may hold values from -0.0625 to 0.0625
- adapter_down_weight: bfloat16 [8192, 4, 64], P('tensor'), may hold values from -0.0625 to 0.0625
- adapter_up_weight: bfloat16 [4, 64, 8192], P(None, None, 'tensor'), may hold values from -0.75 to 0.75
- residual: bfloat16 [2048, 8192], P(('groups', 'dp', 'pipe'), 'tensor'), parts along dimension 0, may hold values from -1.5 to 1.5
- norm_scale_weight: bfloat16 [8192], P('tensor'), may hold values from 0.5 to 1.5
Outputs:
- hidden: bfloat16 [2048, 8192], P(('groups', 'dp', 'pipe'), 'tensor'), parts along dimension 0
- normed: bfloat16 [2048, 8192], P(('groups', 'dp', 'pipe'), 'tensor'), parts along dimension 0
There are 2 independent parts, one for each index of `groups`. A program takes and returns all parts, laid end to end along the dimension named above; an argument that names none is the same for every part. Nothing has to cross between parts.
Inputs may be any that keep to these rules, and one draw needn't show every extreme that they name: `prefix_length`: some request's prefix fills all 2048 slots.
All inputs are finite; a program needn't handle non-finite values.
Results may differ from a plain program's by a relative error of at most 0.012.
Values may be sent and summed in bfloat16 or wider, within the bound.
A program may use at most 192 MiB of HBM per device.

v0:
```python
import math

import jax
import jax.numpy as jnp
from jax import lax
from jax.sharding import PartitionSpec as P

MODEL_WIDTH = 8192
HEAD_SIZE = 128
ADAPTER_RANK = 64
ADAPTER_COUNT = 4
NEW = 128
PRE = 2048


neg_large = -1e30
eps_norm = 1e-05


def partner(block, axis, distance):
    count = lax.axis_size(axis)
    route = []
    for low in range(count):
        high = low | 1 << distance
        if high != low and high < count:
            route += [(low, high), (high, low)]
    return lax.ppermute(block, axis, route)


def shards(
    queries,
    incoming_key_value,
    prefix_key_value_cache,
    prefix_length,
    adapter,
    output_weight,
    adapter_down_weight,
    adapter_up_weight,
    residual,
    norm_scale_weight,
):
    requests = prefix_length.shape[0]
    tokens = queries.shape[0]
    heads_dev = queries.shape[1] // HEAD_SIZE
    block_heads = incoming_key_value.shape[1] // HEAD_SIZE
    scaling = 1.0 / math.sqrt(HEAD_SIZE)
    partner_new, partner_past = partner((incoming_key_value, prefix_key_value_cache), "tensor", 0)
    parity = lax.axis_index("tensor") % 2
    holds_keys = parity == 0
    fresh_keys = jnp.where(holds_keys, incoming_key_value, partner_new).reshape(
        requests, NEW, block_heads, HEAD_SIZE
    )
    fresh_values = jnp.where(holds_keys, partner_new, incoming_key_value).reshape(
        requests, NEW, block_heads, HEAD_SIZE
    )
    past_keys = jnp.where(holds_keys, prefix_key_value_cache, partner_past).reshape(
        requests, PRE, block_heads, HEAD_SIZE
    )
    past_values = jnp.where(holds_keys, partner_past, prefix_key_value_cache).reshape(
        requests, PRE, block_heads, HEAD_SIZE
    )
    slots_dev = max(1, block_heads // 2)
    offset = parity * (block_heads - slots_dev)
    fresh_kv = jnp.stack(
        [
            lax.dynamic_slice_in_dim(fresh_keys, offset, slots_dev, 2),
            lax.dynamic_slice_in_dim(fresh_values, offset, slots_dev, 2),
        ],
        axis=3,
    )
    past_kv = jnp.stack(
        [
            lax.dynamic_slice_in_dim(past_keys, offset, slots_dev, 2),
            lax.dynamic_slice_in_dim(past_values, offset, slots_dev, 2),
        ],
        axis=3,
    )
    grouped = heads_dev // slots_dev
    query_view = queries.reshape(requests, NEW, slots_dev, grouped, HEAD_SIZE)
    scores = (
        jnp.einsum(
            "rnsgd,rksd->rnsgk",
            query_view,
            fresh_kv[:, :, :, 0, :],
            preferred_element_type=jnp.float32,
        )
        * scaling
    )
    causal = jnp.arange(NEW)[None, :] <= jnp.arange(NEW)[:, None]
    scores = jnp.where(causal[None, :, None, None, :], scores, neg_large)
    running_max = jnp.max(scores, axis=-1)
    weights = jnp.exp(scores - running_max[..., None])
    denominator = jnp.sum(weights, axis=-1)
    weighted = jnp.einsum(
        "rnsgk,rksd->rnsgd",
        weights.astype(jnp.bfloat16),
        fresh_kv[:, :, :, 1, :],
        preferred_element_type=jnp.float32,
    )
    key_width = min(PRE, 512)

    def key_step(block_index, state_carry):
        old_max, old_denominator, old_weighted = state_carry
        key_block = lax.dynamic_slice_in_dim(past_kv, block_index * key_width, key_width, 1)
        block_scores = (
            jnp.einsum(
                "rnsgd,rksd->rnsgk",
                query_view,
                key_block[:, :, :, 0, :],
                preferred_element_type=jnp.float32,
            )
            * scaling
        )
        position = block_index * key_width + jnp.arange(key_width)
        live_mask = position[None, :] < prefix_length[:, None]
        block_scores = jnp.where(live_mask[:, None, None, None, :], block_scores, neg_large)
        new_max = jnp.maximum(old_max, jnp.max(block_scores, axis=-1))
        shrink = jnp.exp(old_max - new_max)
        block_weights = jnp.exp(block_scores - new_max[..., None])
        new_denominator = old_denominator * shrink + jnp.sum(block_weights, axis=-1)
        new_weighted = old_weighted * shrink[..., None] + jnp.einsum(
            "rnsgk,rksd->rnsgd",
            block_weights.astype(jnp.bfloat16),
            key_block[:, :, :, 1, :],
            preferred_element_type=jnp.float32,
        )
        return (new_max, new_denominator, new_weighted)

    block_count = PRE // key_width
    running_max, denominator, weighted = lax.fori_loop(
        0, block_count, key_step, (running_max, denominator, weighted)
    )
    attention_output = (
        (weighted / denominator[..., None])
        .astype(jnp.bfloat16)
        .reshape(tokens, heads_dev * HEAD_SIZE)
    )
    partial_value = jnp.dot(
        attention_output,
        lax.all_gather(output_weight, ("dp", "pipe"), axis=1, tiled=True),
        preferred_element_type=jnp.float32,
    )
    projected_output = lax.psum_scatter(
        partial_value.astype(jnp.bfloat16), "tensor", scatter_dimension=1, tiled=True
    ).astype(jnp.float32)
    adapter_rows = jnp.repeat(adapter, NEW)
    selector = (adapter_rows[:, None] == jnp.arange(ADAPTER_COUNT)[None, :]).astype(jnp.float32)
    flattened_rank = jnp.dot(
        attention_output,
        adapter_down_weight.reshape(adapter_down_weight.shape[0], ADAPTER_COUNT * ADAPTER_RANK),
        preferred_element_type=jnp.float32,
    ).reshape(tokens, ADAPTER_COUNT, ADAPTER_RANK)
    partial_rank = jnp.sum(flattened_rank * selector[:, :, None], axis=1)
    pieces = lax.all_gather(partial_rank.astype(jnp.bfloat16), "tensor", axis=1, tiled=True).astype(
        partial_rank.dtype
    )
    rank_total = jnp.sum(pieces.reshape(tokens, -1, ADAPTER_RANK), axis=1)
    shrunk = rank_total.astype(jnp.bfloat16)
    spread_heads = (shrunk[:, None, :] * selector.astype(jnp.bfloat16)[:, :, None]).reshape(
        tokens, ADAPTER_COUNT * ADAPTER_RANK
    )
    adapter_output = jnp.dot(
        spread_heads,
        adapter_up_weight.reshape(ADAPTER_COUNT * ADAPTER_RANK, adapter_up_weight.shape[2]),
        preferred_element_type=jnp.float32,
    )
    combined_output = residual.astype(jnp.float32) + projected_output + adapter_output
    hidden = combined_output.astype(jnp.bfloat16)
    widened = hidden.astype(jnp.float32)
    squares = lax.psum(jnp.sum(widened * widened, axis=1), "tensor")
    inverse = lax.rsqrt(squares / MODEL_WIDTH + eps_norm)
    normed = (widened * inverse[:, None] * norm_scale_weight.astype(jnp.float32)[None, :]).astype(
        jnp.bfloat16
    )
    return (hidden, normed)


def solution(mesh):
    return jax.shard_map(
        shards,
        mesh=mesh,
        in_specs=(
            P(("groups", "dp", "pipe"), "tensor"),
            P(("groups", "dp", "pipe"), "tensor"),
            P(("groups", "dp", "pipe"), None, "tensor"),
            P(("groups", "dp", "pipe")),
            P(("groups", "dp", "pipe")),
            P("tensor", ("dp", "pipe")),
            P("tensor", None, None),
            P(None, None, "tensor"),
            P(("groups", "dp", "pipe"), "tensor"),
            P("tensor"),
        ),
        out_specs=(P(("groups", "dp", "pipe"), "tensor"), P(("groups", "dp", "pipe"), "tensor")),
        check_vma=False,
    )
```

profile of v0, /device:TPU:0, one launch (start us, length us, event | category | flops | bytes accessed | tf_op | source)
XLA Modules:
  0.0 330.6 jit_solution(2847375499403472246)
XLA Ops:
  7.2 0.0 copy-start
  7.2 0.0 all-gather.2.cloned.1.call-start
  7.2 0.7 all-gather.2.cloned.1.call-update
  7.9 0.0 reduce-scatter.2.cloned.1.call-start
  8.0 3.1 collective-permute-start.1
  11.1 0.2 collective-permute-start
  11.2 0.2 copy.39
  11.5 1.2 copy.20
  12.7 94.8 %collective-permute-done = bf16[256,512]{1,0:T(8,128)(2,1)} collective-permute-done((bf16[256,512]{1,0:T(8,128)(2,1)S(1)}, bf16[256,512]{1,0:T(8,128)(2,1)}, u32[]{:S(2)}, u32[]{:S(2)}) %collective-permute-start) | collective-permute-done | bytes 262176 | tf_op jit(solution)/shard_map/ppermute | solution.py:27
  107.6 1.0 broadcast_select_fusion.2
  108.6 0.1 reshape.134
  108.6 0.1 reshape.132
  108.7 0.3 constant_dynamic-slice_fusion.2
  109.0 0.1 copy.36
  109.1 0.0 copy-start.2
  109.1 0.5 fusion.34
  109.7 0.4 fusion.22
  110.1 0.5 convolution_bitcast_fusion.1
  110.6 0.8 copy-done.2
  111.3 5.1 %broadcast_select_fusion.1 = (bf16[2,2048,512]{2,1,0:T(8,128)(2,1)}, bf16[2,2048,512]{2,1,0:T(8,128)(2,1)}) fusion(bf16[2,2048,512]{2,1,0:T(8,128)(2,1)S(1)} %copy-done.2, bf16[2,2048,512]{2,1,0:T(8,128)(2,1)} %collective-permute-done.1, pred[]{:T(512)S(6)} %eq.27), kind=kLoop, calls=%fused_computation.26 | loop fusion | flops 4194304 | bytes 16777216 | tf_op jit(solution)/shard_map/jit(_where)/select_n | solution.py:56
  116.4 6.9 %reshape.136 = bf16[2,2048,4,128]{3,2,1,0:T(4,128)(2,1)} reshape(bf16[2,2048,512]{2,1,0:T(8,128)(2,1)} %get-tuple-element.155) | data formatting | bytes 8388608 | tf_op jit(solution)/shard_map/reshape | solution.py:59
  123.4 6.9 %reshape.135 = bf16[2,2048,4,128]{3,2,1,0:T(4,128)(2,1)} reshape(bf16[2,2048,512]{2,1,0:T(8,128)(2,1)} %get-tuple-element.154) | data formatting | bytes 8388608 | tf_op jit(solution)/shard_map/reshape | solution.py:56
  130.2 6.5 %constant_dynamic-slice_fusion = (bf16[2,2048,2,128]{3,2,1,0:T(2,128)(2,1)S(1)}, bf16[2,2048,2,128]{3,2,1,0:T(2,128)(2,1)S(1)}) fusion(bf16[2,2048,4,128]{3,2,1,0:T(4,128)(2,1)} %reshape.136, s32[]{:T(128)S(6)} %select_n.62, bf16[2,2048,4,128]{3,2,1,0:T(4,128)(2,1)} %reshape.135), kind=kLoop, calls=%fused_computation.58 | loop fusion | bytes 8388612 | tf_op jit(solution)/shard_map/dynamic_slice | solution.py:74
  136.7 0.3 copy.50
  137.0 0.3 copy.51
  137.3 0.0 copy-start.6
  137.3 2.3 pad_maximum_fusion
  139.6 48.3 %while.17 = (s32[]{:T(128)}, f32[2,128,2,8]{1,3,2,0:T(8,128)S(1)}, f32[2,128,2,8]{1,3,2,0:T(8,128)S(1)}, f32[2,128,2,8,128]{1,4,3,2,0:T(8,128)S(1)}, s32[2]{0:T(...) while((s32[]{:T(128)}, f32[2,128,2,8]{1,3,2,0:T(8,128)S(1)}, ...), condition=%wide.region_5.6_spmd, body=%wide.region_2.5_spmd.sunk | while | flops 1097868800 | bytes 65282284 | solution.py:130
  139.6 0.1 broadcast_compare_fusion.2
  139.7 2.7 bitcast_reduce_fusion.2
  142.4 1.9 fusion.45
  144.3 1.3 copy-done.1
  145.6 6.0 %bitcast_add_fusion.2 = f32[2,128,2,8,128]{1,4,3,2,0:T(8,128)S(1)} fusion(f32[2,128,2,8,128]{1,4,3,2,0:T(8,128)S(1)} %get-tuple-element.234, f32[2,2,512,128,8]{3,2,4,1,0:T(8,128)} %copy-done.1, f32[2,128,2,8]{1,3,2,0:T(8,128)S(1)} %max.8, pred[2,512]{1,0:T(4,128)(4,1)S(1)} %broadcast_compare_fusion.2, f32[2,128,2,8]{1,3,2,0:T(8,128)S(1)} %get-tuple-element.218, ...), kind=kOutput, calls=%fused_computation.11.clone.1 | convolution fusion | flops 546308096 | bytes 13141000 | tf_op jit(solution)/shard_map/while/body/eval_jaxpr/rnsgk,rksd->rnsgd/dot_general | solution.py:121
  151.7 0.1 broadcast_compare_fusion.2
  151.7 2.7 bitcast_reduce_fusion.2
  154.5 1.9 fusion.45
  156.4 1.3 copy-done.1
  157.7 6.0 %bitcast_add_fusion.2 = f32[2,128,2,8,128]{1,4,3,2,0:T(8,128)S(1)} fusion(f32[2,128,2,8,128]{1,4,3,2,0:T(8,128)S(1)} %get-tuple-element.234, f32[2,2,512,128,8]{3,2,4,1,0:T(8,128)} %copy-done.1, f32[2,128,2,8]{1,3,2,0:T(8,128)S(1)} %max.8, pred[2,512]{1,0:T(4,128)(4,1)S(1)} %broadcast_compare_fusion.2, f32[2,128,2,8]{1,3,2,0:T(8,128)S(1)} %get-tuple-element.218, ...), kind=kOutput, calls=%fused_computation.11.clone.1 | convolution fusion | flops 546308096 | bytes 13141000 | tf_op jit(solution)/shard_map/while/body/eval_jaxpr/rnsgk,rksd->rnsgd/dot_general | solution.py:121
  163.7 0.1 broadcast_compare_fusion.2
  163.8 2.7 bitcast_reduce_fusion.2
  166.6 1.9 fusion.45
  168.5 1.3 copy-done.1
  169.8 6.0 %bitcast_add_fusion.2 = f32[2,128,2,8,128]{1,4,3,2,0:T(8,128)S(1)} fusion(f32[2,128,2,8,128]{1,4,3,2,0:T(8,128)S(1)} %get-tuple-element.234, f32[2,2,512,128,8]{3,2,4,1,0:T(8,128)} %copy-done.1, f32[2,128,2,8]{1,3,2,0:T(8,128)S(1)} %max.8, pred[2,512]{1,0:T(4,128)(4,1)S(1)} %broadcast_compare_fusion.2, f32[2,128,2,8]{1,3,2,0:T(8,128)S(1)} %get-tuple-element.218, ...), kind=kOutput, calls=%fused_computation.11.clone.1 | convolution fusion | flops 546308096 | bytes 13141000 | tf_op jit(solution)/shard_map/while/body/eval_jaxpr/rnsgk,rksd->rnsgd/dot_general | solution.py:121
  175.8 0.1 broadcast_compare_fusion.2
  175.9 2.7 bitcast_reduce_fusion.2
  178.6 1.9 fusion.45
  180.5 1.3 copy-done.1
  181.8 6.0 %bitcast_add_fusion.2 = f32[2,128,2,8,128]{1,4,3,2,0:T(8,128)S(1)} fusion(f32[2,128,2,8,128]{1,4,3,2,0:T(8,128)S(1)} %get-tuple-element.234, f32[2,2,512,128,8]{3,2,4,1,0:T(8,128)} %copy-done.1, f32[2,128,2,8]{1,3,2,0:T(8,128)S(1)} %max.8, pred[2,512]{1,0:T(4,128)(4,1)S(1)} %broadcast_compare_fusion.2, f32[2,128,2,8]{1,3,2,0:T(8,128)S(1)} %get-tuple-element.218, ...), kind=kOutput, calls=%fused_computation.11.clone.1 | convolution fusion | flops 546308096 | bytes 13141000 | tf_op jit(solution)/shard_map/while/body/eval_jaxpr/rnsgk,rksd->rnsgd/dot_general | solution.py:121
  187.9 1.2 divide_convert_fusion
  189.1 2.0 copy.26
  191.1 0.5 reshape.137
  191.6 22.3 %all-gather.2.cloned.1.call-done = bf16[2048,8192]{1,0:T(8,128)(2,1)} async-done(((bf16[2048,2048]{1,0:T(8,128)(2,1)}), bf16[2048,8192]{1,0:T(8,128)(2,1)}) %all-gather.2.cloned.1.call-update) | async-done | bytes 33554448 | tf_op jit(solution)/shard_map/all_gather | solution.py:140
  213.9 16.4 %convolution_convert_fusion = bf16[256,8192]{1,0:T(8,128)(2,1)} fusion(bf16[256,2048]{1,0:T(8,128)(2,1)S(1)} %reshape.137, bf16[2048,8192]{1,0:T(8,128)(2,1)} %all-gather.2.cloned.1.call-done), kind=kOutput, calls=%fused_computation.23 | convolution fusion | flops 8592031744 | bytes 38797312 | tf_op jit(solution)/shard_map/dot_general | solution.py:138
  230.2 0.0 reduce-scatter.2.cloned.1.call-update
  230.3 0.7 copy-done.7
  230.9 0.1 broadcast_bitcast_fusion
  231.0 0.5 reshape.145
  231.5 1.7 fusion.23
  233.2 14.1 %all_gather.7 = bf16[256,256]{0,1:T(8,128)(2,1)S(1)} all-gather(bf16[256,64]{0,1:T(8,128)(2,1)S(1)} %fusion.23), channel_id=1, replica_groups=mesh['groups'=2,'tensor'=4,'dp'=2,'pipe'=2] {'tensor'}, dimensions={1}, use_global_device_ids=true | all-gather | bytes 163840 | tf_op jit(solution)/shard_map/all_gather | solution.py:154
  247.4 61.7 %reduce-scatter.2.cloned.1.call-done = bf16[256,2048]{1,0:T(8,128)(2,1)} async-done(((bf16[256,8192]{1,0:T(8,128)(2,1)}), bf16[256,2048]{1,0:T(8,128)(2,1)}) %reduce-scatter.2.cloned.1.call-update) | async-done | bytes 1048592 | tf_op jit(solution)/shard_map/reduce_scatter | solution.py:143
  309.1 2.2 fusion.18
  311.3 0.0 copy-start.4
  311.3 11.1 %psum.7 = f32[256]{0:T(256)S(1)} all-reduce(f32[256]{0:T(256)S(1)} %get-tuple-element.162), channel_id=1, replica_groups=mesh['groups'=2,'tensor'=4,'dp'=2,'pipe'=2] {'tensor'}, use_global_device_ids=true, to_apply=%region_10.11 | all-reduce | flops 256 | bytes 2048 | tf_op jit(solution)/shard_map/psum | solution.py:170
  322.4 1.3 fusion.20
  (36 shorter events, 0.2 us)
Async XLA Ops:
  7.2 301.9 %copy-start = (bf16[4,64,2048]{2,1,0:T(8,128)(2,1)S(1)}, bf16[4,64,2048]{2,1,0:T(8,128)(2,1)}, u32[]{:S(2)}) copy-start(bf16[4,64,2048]{2,1,0:T(8,128)(2,1)} %param.19) | copy-start | bytes 3145732
  7.2 3.9 %copy-start.5 = (bf16[256,512]{1,0:T(8,128)(2,1)S(1)}, bf16[256,512]{1,0:T(8,128)(2,1)}, u32[]{:S(2)}) copy-start(bf16[256,512]{1,0:T(8,128)(2,1)} %param.13) | copy-start | bytes 786436
  7.2 4.1 %copy-start.3 = (bf16[256,2048]{1,0:T(8,128)(2,1)S(1)}, bf16[256,2048]{1,0:T(8,128)(2,1)}, u32[]{:S(2)}) copy-start(bf16[256,2048]{1,0:T(8,128)(2,1)} %param.12) | copy-start | bytes 3145732
  7.2 206.7 %all-gather.2.cloned.1.call-start = ((), (), s32[]{:S(2)}) async-start(), calls=%async_computation.1 | async-start | bytes 41943040 | tf_op jit(solution)/shard_map/all_gather | solution.py:140
  7.9 301.1 %reduce-scatter.2.cloned.1.call-start = ((), (), s32[]{:S(2)}) async-start(), calls=%async_computation.2 | async-start | bytes 5242880 | tf_op jit(solution)/shard_map/reduce_scatter | solution.py:143
  8.0 102.6 %collective-permute-start.1 = (bf16[2,2048,512]{2,1,0:T(8,128)(2,1)}, bf16[2,2048,512]{2,1,0:T(8,128)(2,1)}, u32[]{:S(2)}, u32[]{:S(2)}) collective-permute-start(bf16[2,2048,512]{2,1,0:T(8,128)(2,1)} %param.14), channel_id=1, source_target_pairs={{0,4},{4,0},{8,12},{12,8},{1,5},{5,1},{9,13},{13,9},{2,6},{6,2},{1... | collective-permute-start | bytes 12582920 | tf_op jit(solution)/shard_map/ppermute | solution.py:27
  11.1 96.5 %collective-permute-start = (bf16[256,512]{1,0:T(8,128)(2,1)S(1)}, bf16[256,512]{1,0:T(8,128)(2,1)}, u32[]{:S(2)}, u32[]{:S(2)}) collective-permute-start(bf16[256,512]{1,0:T(8,128)(2,1)S(1)} %copy-done.5), channel_id=1, source_target_pairs={{0,4},{4,0},{8,12},{12,8},{1,5},{5,1},{9,13},{13,9},{2,6},{6,2},{1... | collective-permute-start | bytes 786440 | tf_op jit(solution)/shard_map/ppermute | solution.py:27
  109.1 2.2 copy-start.2
  137.3 2.3 copy-start.6
  142.4 3.2 copy-start.1
  154.5 3.2 copy-start.1
  166.5 3.2 copy-start.1
  178.6 3.2 copy-start.1
  230.2 0.7 copy-start.7
  230.2 0.7 copy-start.8
  311.3 12.4 %copy-start.4 = (bf16[256,2048]{1,0:T(8,128)(2,1)}, bf16[256,2048]{1,0:T(8,128)(2,1)S(1)}, u32[]{:S(2)}) copy-start(bf16[256,2048]{1,0:T(8,128)(2,1)S(1)} %get-tuple-element.163) | copy-start | bytes 3145732
Sparse Core Ops, SparseCore 0:
  9.6 204.2 all-gather.1
  230.4 78.6 reduce-scatter.1
where the time goes:
time: 331 us
  waiting for transfers between devices  180 us (54%)
  matrix products  56.2 us (17%)
  local copies, waits for them, and re-layouts  32.5 us (10%)
  blocking collectives  25.2 us (8%)
  other arithmetic  19.3 us (6%)
  between operations  14.2 us (4%)
  starting transfers between devices  3.33 us (1%)
    ppermute x2, waiting for transfers between devices, partner(): return lax.ppermute(block, axis, route)  94.8 us
    reduce_scatter x1, waiting for transfers between devices, shards(): lax.psum_scatter(partial_value.astype(jnp.bfloat16), 'tensor', scatter_di...  61.7 us
    dot_general x4, matrix products, key_step(): jnp.einsum('rnsgk,rksd->rnsgd', block_weights.astype(jnp.bfloat16), key_b...  24 us
    all_gather x1, waiting for transfers between devices, shards(): lax.all_gather(output_weight, ('dp', 'pipe'), axis=1, tiled=True)  22.3 us
    dot_general x1, matrix products, shards(): jnp.dot(attention_output, lax.all_gather(output_weight, ('dp', 'pipe'), a...  16.4 us
    all_gather x1, blocking collectives, shards(): lax.all_gather(partial_rank.astype(jnp.bfloat16), 'tensor', axis=1, tiled...  14.1 us
    psum x1, blocking collectives, shards(): squares = lax.psum(jnp.sum(widened * widened, axis=1), 'tensor')  11.1 us
    dot_general x4, matrix products, key_step(): jnp.einsum('rnsgd,rksd->rnsgk', query_view, key_block[:, :, :, 0, :], pre...  10.8 us
  transfers between devices with their start and end apart: 4, of which 3 were waited for; matrix products, arithmetic and copies ran while one was open for 25% of the time, Pallas kernels for 0%

commit v1 on v0

--- a/solution.py
+++ b/solution.py
@@ -1,8 +1,11 @@
+import functools
 import math
 
 import jax
 import jax.numpy as jnp
 from jax import lax
+from jax.experimental import pallas as pl
+from jax.experimental.pallas import tpu as pltpu
 from jax.sharding import PartitionSpec as P
 
 MODEL_WIDTH = 8192
@@ -27,7 +30,7 @@
     return lax.ppermute(block, axis, route)
 
 
-def shards(
+def shards_any(
     queries,
     incoming_key_value,
     prefix_key_value_cache,
@@ -175,7 +178,193 @@
     return (hidden, normed)
 
 
+def attend_kernel(
+    heads_tile, length_ref, parity_ref, q_ref, own_past, own_new, recv, out_ref, keys, values
+):
+    request = pl.program_id(0)
+    row_tile = 2
+    past, new = own_past.shape[1], own_new.shape[0]
+
+    @pl.when((pl.program_id(2) == 0) & (parity_ref[0] == 0))
+    def _():
+        keys[:past] = own_past[0]
+        keys[past:] = own_new[...]
+        values[...] = recv[...]
+
+    @pl.when((pl.program_id(2) == 0) & (parity_ref[0] != 0))
+    def _():
+        values[:past] = own_past[0]
+        values[past:] = own_new[...]
+        keys[...] = recv[...]
+
+    factor = math.log2(math.e) / math.sqrt(HEAD_SIZE)
+    length = length_ref[request + parity_ref[1]]
+    live = lax.broadcasted_iota(jnp.int32, (1, past), 1) < length
+    bias = jnp.where(live, 0.0, neg_large)
+    rows = row_tile * new
+    row = lax.broadcasted_iota(jnp.int32, (rows, new), 0) % new
+    causal = lax.broadcasted_iota(jnp.int32, (rows, new), 1) <= row
+    for first in range(0, heads_tile, row_tile):
+        q = jnp.concatenate(
+            [
+                q_ref[:, h * HEAD_SIZE : (h + 1) * HEAD_SIZE]
+                for h in range(first, first + row_tile)
+            ],
+            axis=0,
+        )
+        scores = lax.dot_general(
+            q, keys[...], (((1,), (1,)), ((), ())), preferred_element_type=jnp.float32
+        )
+        old = scores[:, :past] + bias
+        fresh = jnp.where(causal, scores[:, past:], neg_large)
+        peak = jnp.maximum(
+            jnp.max(old, axis=1, keepdims=True), jnp.max(fresh, axis=1, keepdims=True)
+        )
+        old = jnp.exp2((old - peak) * factor)
+        fresh = jnp.exp2((fresh - peak) * factor)
+        denominator = jnp.sum(old, axis=1, keepdims=True) + jnp.sum(fresh, axis=1, keepdims=True)
+        mixed = jnp.dot(
+            old.astype(jnp.bfloat16), values[:past], preferred_element_type=jnp.float32
+        ) + jnp.dot(
+            fresh.astype(jnp.bfloat16), values[past:], preferred_element_type=jnp.float32
+        )
+        mixed = (mixed / denominator).astype(jnp.bfloat16)
+        for i in range(row_tile):
+            h = first + i
+            out_ref[:, h * HEAD_SIZE : (h + 1) * HEAD_SIZE] = mixed[i * new : (i + 1) * new]
+
+
+def attend(request, lengths, parity, queries, cache, incoming, recv):
+    slots = recv.shape[1] // HEAD_SIZE
+    heads = queries.shape[1] // HEAD_SIZE
+    grouped = heads // slots
+    heads_tile = min(4, grouped)
+    tiles = grouped // heads_tile
+    past = cache.shape[1]
+    whole = past + NEW
+    meta = jnp.stack([parity, jnp.int32(request)])
+    width = heads_tile * HEAD_SIZE
+    return pl.pallas_call(
+        functools.partial(attend_kernel, heads_tile),
+        out_shape=jax.ShapeDtypeStruct((NEW, heads * HEAD_SIZE), jnp.bfloat16),
+        grid_spec=pltpu.PrefetchScalarGridSpec(
+            num_scalar_prefetch=2,
+            grid=(1, slots, tiles),
+            in_specs=[
+                pl.BlockSpec((NEW, width), lambda r, s, t, n, p: (request, s * tiles + t)),
+                pl.BlockSpec(
+                    (1, past, HEAD_SIZE), lambda r, s, t, n, p: (request, 0, slots * p[0] + s)
+                ),
+                pl.BlockSpec((NEW, HEAD_SIZE), lambda r, s, t, n, p: (request, slots * p[0] + s)),
+                pl.BlockSpec((whole, HEAD_SIZE), lambda r, s, t, n, p: (0, s)),
+            ],
+            out_specs=pl.BlockSpec((NEW, width), lambda r, s, t, n, p: (0, s * tiles + t)),
+            scratch_shapes=[
+                pltpu.VMEM((whole, HEAD_SIZE), jnp.bfloat16),
+                pltpu.VMEM((whole, HEAD_SIZE), jnp.bfloat16),
+            ],
+        ),
+        compiler_params=pltpu.CompilerParams(vmem_limit_bytes=40 * 2**20),
+        cost_estimate=pl.CostEstimate(
+            flops=4 * NEW * heads * whole * HEAD_SIZE,
+            bytes_accessed=4 * whole * slots * HEAD_SIZE + 4 * NEW * heads * HEAD_SIZE,
+            transcendentals=NEW * heads * whole,
+        ),
+        name="attend",
+    )(lengths, meta, queries, cache, incoming, recv)
+
+
+def from_others(block, axis):
+    count = lax.axis_size(axis)
+    return [
+        lax.ppermute(block, axis, [(i, (i + shift) % count) for i in range(count)])
+        for shift in range(1, count)
+    ]
+
+
+def shards_fast(
+    queries,
+    incoming_key_value,
+    prefix_key_value_cache,
+    prefix_length,
+    adapter,
+    output_weight,
+    adapter_down_weight,
+    adapter_up_weight,
+    residual,
+    norm_scale_weight,
+):
+    requests = prefix_length.shape[0]
+    half = incoming_key_value.shape[1] // 2
+    past = prefix_key_value_cache.shape[1]
+    width = output_weight.shape[1]
+    place = lax.axis_index("tensor")
+    parity = place % 2
+    upper = place // 2
+    x = lax.axis_index("dp")
+    core = lax.axis_index("pipe")
+    send_at = (1 - parity) * half
+    outgoing = []
+    for r in range(requests):
+        a = lax.dynamic_slice(prefix_key_value_cache, (r, 0, send_at), (1, past, half))[0]
+        b = lax.dynamic_slice(incoming_key_value, (r * NEW, send_at), (NEW, half))
+        outgoing.append(jnp.concatenate([a, b], axis=0))
+    arrived = [partner(block, "tensor", 0) for block in outgoing]
+    weight_partner = partner(output_weight, "pipe", 0)
+    down = adapter_down_weight.reshape(adapter_down_weight.shape[0], ADAPTER_COUNT * ADAPTER_RANK)
+
+    keep_own = parity == core
+    hidden, squares = [], []
+    for r in range(requests):
+        attended = attend(
+            r, prefix_length, parity, queries, prefix_key_value_cache, incoming_key_value, arrived[r]
+        )
+        both = jnp.concatenate([attended, partner(attended, "dp", 0)], axis=0)
+        own = jnp.dot(both, output_weight, preferred_element_type=jnp.float32).astype(jnp.bfloat16)
+        other = jnp.dot(both, weight_partner, preferred_element_type=jnp.float32).astype(
+            jnp.bfloat16
+        )
+        kept = jnp.where(keep_own, own, other)
+        sent = jnp.where(keep_own, other, own)
+        got = partner(sent, "tensor", 0)
+        pair = (kept.astype(jnp.float32) + got.astype(jnp.float32)).astype(jnp.bfloat16)
+        mine = pair[:NEW]
+        theirs = partner(pair[NEW:], "dp", 0)
+        last_kept = jnp.where(x == upper, mine, theirs)
+        last_sent = jnp.where(x == upper, theirs, mine)
+        last_got = partner(last_sent, "tensor", 1)
+        projected = last_kept.astype(jnp.float32) + last_got.astype(jnp.float32)
+
+        flat = jnp.dot(attended, down, preferred_element_type=jnp.float32)
+        partial = lax.dynamic_slice(flat, (0, adapter[r] * ADAPTER_RANK), (NEW, ADAPTER_RANK))
+        partial = partial.astype(jnp.bfloat16)
+        rank_total = partial.astype(jnp.float32)
+        for piece in from_others(partial, "tensor"):
+            rank_total = rank_total + piece.astype(jnp.float32)
+        up = lax.dynamic_slice(
+            adapter_up_weight, (adapter[r], 0, 0), (1, ADAPTER_RANK, width)
+        )[0]
+        adapter_output = jnp.dot(
+            rank_total.astype(jnp.bfloat16), up, preferred_element_type=jnp.float32
+        )
+        rows = residual[r * NEW : (r + 1) * NEW].astype(jnp.float32)
+        hidden.append((rows + projected + adapter_output).astype(jnp.bfloat16))
+    hidden = jnp.concatenate(hidden, axis=0)
+    widened = hidden.astype(jnp.float32)
+    own_squares = jnp.sum(widened * widened, axis=1)
+    squares = own_squares
+    for piece in from_others(own_squares, "tensor"):
+        squares = squares + piece
+    inverse = lax.rsqrt(squares / MODEL_WIDTH + eps_norm)
+    normed = (widened * inverse[:, None] * norm_scale_weight.astype(jnp.float32)[None, :]).astype(
+        jnp.bfloat16
+    )
+    return (hidden, normed)
+
+
 def solution(mesh):
+    sizes = tuple(mesh.shape[name] for name in ("tensor", "dp", "pipe"))
+    shards = shards_fast if sizes == (4, 2, 2) else shards_any
     return jax.shard_map(
         shards,
         mesh=mesh,

time: 331 us -> 204 us (0.62)
  waiting for transfers between devices: 180 us -> 111 us
  matrix products: 56.2 us -> 21.9 us
  starting transfers between devices: 3.33 us -> 30.5 us
  local copies, waits for them, and re-layouts: 32.5 us -> 6.88 us
  blocking collectives: 25.2 us -> 0 us
  Pallas kernels: 0 us -> 20.1 us
  other arithmetic: 19.3 us -> 6.58 us
  between operations: 14.2 us -> 6.18 us
    reduce_scatter x1 -> x0, waiting for transfers between devices: 61.7 us -> none  [shards(): lax.psum_scatter(partial_value.astype(jnp.bfloat16), 'tensor', scatter_di...]
    dot_general x13 -> x8, matrix products: 56.2 us -> 21.9 us  [the longest x2 14.3 us: shards_fast(): jnp.dot(both, weight_partner, preferred_element_type=jnp.float32)]
    ppermute x0 -> x9, waiting for transfers between devices: none -> 23.9 us  [from_others(): lax.ppermute(block, axis, [(i, (i + shift) % count) for i in range(count)])]
    all_gather x1 -> x0, waiting for transfers between devices: 22.3 us -> none  [shards(): lax.all_gather(output_weight, ('dp', 'pipe'), axis=1, tiled=True)]
    pallas_call x0 -> x2, Pallas kernels: none -> 20.1 us  [attend(): pl.pallas_call(functools.partial(attend_kernel, heads_tile), out_shape=ja...]
    reshape x7 -> x0, local copies, waits for them, and re-layouts: 16.2 us -> none  [the longest x1 6.94 us: shards(): jnp.where(holds_keys, partner_past, prefix_key_value_cache)]
    ppermute x0 -> x9, starting transfers between devices: none -> 16 us  [from_others(): lax.ppermute(block, axis, [(i, (i + shift) % count) for i in range(count)])]
    all_gather x1 -> x0, blocking collectives: 14.1 us -> none  [shards(): lax.all_gather(partial_rank.astype(jnp.bfloat16), 'tensor', axis=1, tiled...]
  transfers between devices with their start and end apart: 4 -> 20, of which waited for: 3 -> 11; matrix products, arithmetic and copies ran while one was open for 25% -> 11% of each run, Pallas kernels for 0% -> 10%
where the time goes in v1:
time: 204 us
  waiting for transfers between devices  111 us (54%)
  starting transfers between devices  30.5 us (15%)
  matrix products  21.9 us (11%)
  Pallas kernels  20.1 us (10%)
  local copies, waits for them, and re-layouts  6.88 us (3%)
  other arithmetic  6.58 us (3%)
  between operations  6.18 us (3%)
    ppermute x11, waiting for transfers between devices, partner(): return lax.ppermute(block, axis, route)  87.5 us
    ppermute x9, waiting for transfers between devices, from_others(): lax.ppermute(block, axis, [(i, (i + shift) % count) for i in range(count)])  23.9 us
    pallas_call x2, Pallas kernels, attend(): pl.pallas_call(functools.partial(attend_kernel, heads_tile), out_shape=ja...  20.1 us
    ppermute x9, starting transfers between devices, from_others(): lax.ppermute(block, axis, [(i, (i + shift) % count) for i in range(count)])  16 us
    ppermute x11, starting transfers between devices, partner(): return lax.ppermute(block, axis, route)  14.6 us
    dot_general x2, matrix products, shards_fast(): jnp.dot(both, weight_partner, preferred_element_type=jnp.float32)  14.3 us
    dot_general x2, matrix products, shards_fast(): jnp.dot(both, output_weight, preferred_element_type=jnp.float32)  5.87 us
  transfers between devices with their start and end apart: 20, of which 11 were waited for; matrix products, arithmetic and copies ran while one was open for 11% of the time, Pallas kernels for 10%

profile of v1, /device:TPU:0, one launch (start us, length us, event | category | flops | bytes accessed | tf_op | source)
XLA Modules:
  0.0 203.5 jit_solution(6869281944016648759)
XLA Ops:
  0.6 0.0 copy-start
  0.6 0.5 collective-permute-start.2
  1.2 0.9 constant_dynamic-slice_fusion
  2.0 0.0 copy-start.4
  2.1 1.8 dynamic-slice_bitcast_fusion.1
  3.8 0.0 copy-start.1
  3.8 0.0 copy-start.3
  3.9 0.0 copy-start.6
  3.9 0.1 pad_maximum_fusion
  3.9 2.7 %collective-permute-start = (bf16[2176,256]{1,0:T(8,128)(2,1)S(1)}, bf16[2176,256]{1,0:T(8,128)(2,1)S(1)}, u32[]{:S(2)}, u32[]{:S(2)}) collective-permute-start(bf16[2176,256]{1,0:T(8,128)(2,1)S(1)} %pad_maximum_fusion), channel_id=1, source_target_pairs={{0,4},{4,0},{8,12},{12,8},{1,5},{5,1},{9,13},{13,9},{2,6},{6,2},{1... | collective-permute-start | bytes 3342344 | tf_op jit(solution)/shard_map/ppermute | solution.py:30
  6.7 1.1 pad_maximum_fusion.1
  7.8 0.0 collective-permute-start.9
  7.8 0.1 pad_add_fusion.parity_ref
  7.9 24.3 %collective-permute-done.recv = bf16[2176,256]{1,0:T(8,128)(2,1)S(1)} collective-permute-done((bf16[2176,256]{1,0:T(8,128)(2,1)S(1)}, bf16[2176,256]{1,0:T(8,128)(2,1)S(1)}, u32[]{:S(2)}, u32[]{:S(2)}) %collective-permute-start) | collective-permute-done | bytes 1114144 | tf_op jit(solution)/shard_map/ppermute | solution.py:30
  32.1 9.9 %attend.2 = bf16[128,2048]{1,0:T(8,128)(2,1)S(1)} custom-call(s32[2]{0:T(128)S(1)} %copy-done.6, s32[2]{0:T(128)S(1)} %pad_add_fusion.parity_ref, bf16[256,2048]{1,0:T(8,128)(2,1)S(1)} %copy-done.4, bf16[2,2048,512]{2,1,0:T(8,128)(2,1)S(1)} %copy-done.1, bf16[256,512]{1,0:T(8,128)(2,1)S(1)} %copy-done.3, bf16[2176,256]{1,0:T(8,128)(2,1)S(1)} %collective-permute-done.recv), custom_call_target="tpu_custom_call" | custom-call | flops 2281701376 | bytes 3276800 | tf_op jit(solution)/shard_map/attend/pallas_call | solution.py:247
  42.1 1.9 collective-permute-start.1
  44.0 0.1 pad_add_fusion.1.parity_ref
  44.1 11.6 %collective-permute-done.9.recv = bf16[2176,256]{1,0:T(8,128)(2,1)S(1)} collective-permute-done((bf16[2176,256]{1,0:T(8,128)(2,1)}, bf16[2176,256]{1,0:T(8,128)(2,1)S(1)}, u32[]{:S(2)}, u32[]{:S(2)}) %collective-permute-start.9) | collective-permute-done | bytes 1114144 | tf_op jit(solution)/shard_map/ppermute | solution.py:30
  55.7 2.2 %copy-done.2 = bf16[2,2048,512]{2,1,0:T(8,128)(2,1)S(1)} copy-done((bf16[2,2048,512]{2,1,0:T(8,128)(2,1)S(1)}, bf16[2,2048,512]{2,1,0:T(8,128)(2,1)}, u32[]{:S(2)}) %copy-start.2) | copy-done | bytes 4194328
  57.9 1.2 copy-done.5
  59.1 10.1 %attend.3 = bf16[128,2048]{1,0:T(8,128)(2,1)S(1)} custom-call(s32[2]{0:T(128)S(1)} %copy-done.6, s32[2]{0:T(128)S(1)} %pad_add_fusion.1.parity_ref, bf16[256,2048]{1,0:T(8,128)(2,1)S(1)} %copy-done.5, bf16[2,2048,512]{2,1,0:T(8,128)(2,1)S(1)} %copy-done.2, bf16[256,512]{1,0:T(8,128)(2,1)S(1)} %copy-done.3, bf16[2176,256]{1,0:T(8,128)(2,1)S(1)} %collective-permute-done.9.recv), custom_call_target="tpu_custom_call" | custom-call | flops 2281701376 | bytes 3276800 | tf_op jit(solution)/shard_map/attend/pallas_call | solution.py:247
  69.2 1.7 collective-permute-start.10
  71.0 3.5 %convolution_convert_fusion.3 = bf16[256,2048]{1,0:T(8,128)(2,1)S(1)} fusion(bf16[2048,2048]{1,0:T(8,128)(2,1)S(1)} %copy-done.15, bf16[128,2048]{1,0:T(8,128)(2,1)} %collective-permute-done.1, bf16[128,2048]{1,0:T(8,128)(2,1)S(1)} %attend.2), kind=kOutput, calls=%fused_computation.5 | convolution fusion | flops 2150105088 | bytes 10485760 | tf_op jit(solution)/shard_map/dot_general | solution.py:323
  74.5 8.6 %collective-permute-done.10 = bf16[128,2048]{1,0:T(8,128)(2,1)S(1)} collective-permute-done((bf16[128,2048]{1,0:T(8,128)(2,1)S(1)}, bf16[128,2048]{1,0:T(8,128)(2,1)S(1)}, u32[]{:S(2)}, u32[]{:S(2)}) %collective-permute-start.10) | collective-permute-done | bytes 524320 | tf_op jit(solution)/shard_map/ppermute | solution.py:30
  83.1 2.4 %convolution_convert_fusion.1 = bf16[256,2048]{1,0:T(8,128)(2,1)S(1)} fusion(bf16[2048,2048]{1,0:T(8,128)(2,1)S(1)} %copy-done.15, bf16[128,2048]{1,0:T(8,128)(2,1)S(1)} %collective-permute-done.10, bf16[128,2048]{1,0:T(8,128)(2,1)S(1)} %attend.3), kind=kOutput, calls=%fused_computation.3 | convolution fusion | flops 2150105088 | bytes 10485760 | tf_op jit(solution)/shard_map/dot_general | solution.py:323
  85.5 0.0 collective-permute-done.2
  85.5 7.2 %broadcast_select_fusion.1 = (bf16[256,2048]{1,0:T(8,128)(2,1)}, bf16[256,2048]{1,0:T(8,128)(2,1)}) fusion(bf16[256,2048]{1,0:T(8,128)(2,1)S(1)} %convolution_convert_fusion.3, pred[]{:T(512)S(6)} %eq.12, bf16[2048,2048]{1,0:T(8,128)(2,1)} %collective-permute-done.2, bf16[128,2048]{1,0:T(8,128)(2,1)} %collective-permute-done.1, bf16[128,2048]{1,0:T(8,128)(2,1)S(1)} %attend.2), kind=kOutput, calls=%fused_computation.21 | convolution fusion | flops 2150629376 | bytes 12582913 | tf_op jit(solution)/shard_map/dot_general | solution.py:324
  92.7 1.6 collective-permute-start.3
  94.3 7.0 %broadcast_select_fusion = (bf16[256,2048]{1,0:T(8,128)(2,1)}, bf16[256,2048]{1,0:T(8,128)(2,1)}) fusion(bf16[256,2048]{1,0:T(8,128)(2,1)S(1)} %convolution_convert_fusion.1, pred[]{:T(512)S(6)} %eq.12, bf16[2048,2048]{1,0:T(8,128)(2,1)} %collective-permute-done.2, bf16[128,2048]{1,0:T(8,128)(2,1)S(1)} %collective-permute-done.10, ...), kind=kOutput, calls=%fused_computation.20 | convolution fusion | flops 2150629376 | bytes 12582913 | tf_op jit(solution)/shard_map/dot_general | solution.py:324
  101.4 0.4 collective-permute-start.11
  101.8 0.6 fusion.19
  107.7 0.4 fusion.20
  108.2 10.9 %collective-permute-done.3 = bf16[256,2048]{1,0:T(8,128)(2,1)} collective-permute-done((bf16[256,2048]{1,0:T(8,128)(2,1)}, bf16[256,2048]{1,0:T(8,128)(2,1)}, u32[]{:S(2)}, u32[]{:S(2)}) %collective-permute-start.3) | collective-permute-done | bytes 1048608 | tf_op jit(solution)/shard_map/ppermute | solution.py:30
  119.1 1.8 add_convert_fusion.1
  121.0 1.6 collective-permute-start.4
  122.6 17.0 %collective-permute-done.11 = bf16[256,2048]{1,0:T(8,128)(2,1)} collective-permute-done((bf16[256,2048]{1,0:T(8,128)(2,1)}, bf16[256,2048]{1,0:T(8,128)(2,1)}, u32[]{:S(2)}, u32[]{:S(2)}) %collective-permute-start.11) | collective-permute-done | bytes 1048608 | tf_op jit(solution)/shard_map/ppermute | solution.py:30
  139.6 1.7 add_convert_fusion
  141.4 1.4 collective-permute-start.12
  142.8 1.6 collective-permute-start.6
  144.4 2.6 %collective-permute-start.7 = (bf16[128,64]{0,1:T(8,128)(2,1)S(1)}, bf16[128,64]{0,1:T(8,128)(2,1)S(1)}, u32[]{:S(2)}, u32[]{:S(2)}) collective-permute-start(bf16[128,64]{0,1:T(8,128)(2,1)S(1)} %dynamic-slice_convert_fusion.1), channel_id=1, source_target_pairs={{0,8},{4,12},{8,0},{12,4},{1,9},{5,13},{9,1},{13,5},{2,10},{6,14},... | collective-permute-start | bytes 49160 | tf_op jit(solution)/shard_map/ppermute | solution.py:280
  147.0 1.3 collective-permute-start.8
  148.3 0.0 collective-permute-done.4
  148.3 0.1 broadcast_select_fusion.3
  148.4 0.4 collective-permute-start.5
  148.8 4.7 %collective-permute-done.12 = bf16[128,2048]{1,0:T(8,128)(2,1)S(1)} collective-permute-done((bf16[128,2048]{1,0:T(8,128)(2,1)S(1)}, bf16[128,2048]{1,0:T(8,128)(2,1)S(1)}, u32[]{:S(2)}, u32[]{:S(2)}) %collective-permute-start.12) | collective-permute-done | bytes 524320 | tf_op jit(solution)/shard_map/ppermute | solution.py:30
  153.5 0.1 broadcast_select_fusion.2
  153.5 2.3 %collective-permute-start.13 = (bf16[128,2048]{1,0:T(8,128)(2,1)S(1)}, bf16[128,2048]{1,0:T(8,128)(2,1)S(1)}, u32[]{:S(2)}, u32[]{:S(2)}) collective-permute-start(bf16[128,2048]{1,0:T(8,128)(2,1)S(1)} %broadcast_select_fusion.2), channel_id=1, source_target_pairs={{0,8},{8,0},{4,12},{12,4},{1,9},{9,1},{5,13},{13,5},{2,10},{10,2},... | collective-permute-start | bytes 1572872 | tf_op jit(solution)/shard_map/ppermute | solution.py:30
  155.8 0.4 fusion.21
  156.3 0.0 collective-permute-done.6
  156.3 1.6 collective-permute-start.14
  157.8 11.0 %collective-permute-done.7 = bf16[128,64]{0,1:T(8,128)(2,1)S(1)} collective-permute-done((bf16[128,64]{0,1:T(8,128)(2,1)S(1)}, bf16[128,64]{0,1:T(8,128)(2,1)S(1)}, u32[]{:S(2)}, u32[]{:S(2)}) %collective-permute-start.7) | collective-permute-done | bytes 16416 | tf_op jit(solution)/shard_map/ppermute | solution.py:280
  168.8 5.0 %collective-permute-start.16 = (bf16[128,64]{0,1:T(8,128)(2,1)S(1)}, bf16[128,64]{0,1:T(8,128)(2,1)S(1)}, u32[]{:S(2)}, u32[]{:S(2)}) collective-permute-start(bf16[128,64]{0,1:T(8,128)(2,1)S(1)} %dynamic-slice_convert_fusion), channel_id=1, source_target_pairs={{0,12},{4,0},{8,4},{12,8},{1,13},{5,1},{9,5},{13,9},{2,14},{6,2},{... | collective-permute-start | bytes 49160 | tf_op jit(solution)/shard_map/ppermute | solution.py:280
  173.8 10.4 %collective-permute-done.5 = bf16[128,2048]{1,0:T(8,128)(2,1)S(1)} collective-permute-done((bf16[128,2048]{1,0:T(8,128)(2,1)S(1)}, bf16[128,2048]{1,0:T(8,128)(2,1)S(1)}, u32[]{:S(2)}, u32[]{:S(2)}) %collective-permute-start.5) | collective-permute-done | bytes 524320 | tf_op jit(solution)/shard_map/ppermute | solution.py:30
  184.2 0.4 add_convert_fusion.3
  184.7 0.0 copy-start.13
  184.7 10.8 %collective-permute-done.15 = bf16[128,64]{0,1:T(8,128)(2,1)S(1)} collective-permute-done((bf16[128,64]{0,1:T(8,128)(2,1)S(1)}, bf16[128,64]{0,1:T(8,128)(2,1)S(1)}, u32[]{:S(2)}, u32[]{:S(2)}) %collective-permute-start.15) | collective-permute-done | bytes 16416 | tf_op jit(solution)/shard_map/ppermute | solution.py:280
  195.5 0.4 add_convert_fusion.2
  196.0 0.3 fusion
  196.3 0.8 collective-permute-start.17
  197.1 0.8 collective-permute-start.18
  197.8 2.3 %collective-permute-start.19 = (f32[256]{0:T(256)S(1)}, f32[256]{0:T(256)S(1)}, u32[]{:S(2)}, u32[]{:S(2)}) collective-permute-start(f32[256]{0:T(256)S(1)} %get-tuple-element.2), channel_id=1, source_target_pairs={{0,12},{4,0},{8,4},{12,8},{1,13},{5,1},{9,5},{13,9},{2,14},{6,2},{... | collective-permute-start | bytes 3080 | tf_op jit(solution)/shard_map/ppermute | solution.py:280
  200.2 1.5 collective-permute-done.17
  201.7 0.6 collective-permute-done.19
  202.3 1.3 fusion.2
  (37 shorter events, 0.2 us)
Async XLA Ops:
  0.6 107.1 %copy-start = (bf16[2048,4,64]{0,2,1:T(8,128)(2,1)S(1)}, bf16[2048,4,64]{0,2,1:T(8,128)(2,1)}, u32[]{:S(2)}) copy-start(bf16[2048,4,64]{0,2,1:T(8,128)(2,1)} %param.16) | copy-start | bytes 3145732
  0.6 84.8 %collective-permute-start.2 = (bf16[2048,2048]{1,0:T(8,128)(2,1)}, bf16[2048,2048]{1,0:T(8,128)(2,1)}, u32[]{:S(2)}, u32[]{:S(2)}) collective-permute-start(bf16[2048,2048]{1,0:T(8,128)(2,1)} %param.15), channel_id=1, source_target_pairs={{0,1},{1,0},{2,3},{3,2},{4,5},{5,4},{6,7},{7,6},{8,9},{9,8},{10,11... | collective-permute-start | bytes 25165832 | tf_op jit(solution)/shard_map/ppermute | solution.py:30
  2.0 30.1 %copy-start.4 = (bf16[256,2048]{1,0:T(8,128)(2,1)S(1)}, bf16[256,2048]{1,0:T(8,128)(2,1)}, u32[]{:S(2)}) copy-start(bf16[256,2048]{1,0:T(8,128)(2,1)} %q_ref.3) | copy-start | bytes 3145732
  3.8 28.3 %copy-start.1 = (bf16[2,2048,512]{2,1,0:T(8,128)(2,1)S(1)}, bf16[2,2048,512]{2,1,0:T(8,128)(2,1)}, u32[]{:S(2)}) copy-start(bf16[2,2048,512]{2,1,0:T(8,128)(2,1)} %own_past.3) | copy-start | bytes 12582916
  3.8 28.3 %copy-start.3 = (bf16[256,512]{1,0:T(8,128)(2,1)S(1)}, bf16[256,512]{1,0:T(8,128)(2,1)}, u32[]{:S(2)}) copy-start(bf16[256,512]{1,0:T(8,128)(2,1)} %own_new.3) | copy-start | bytes 786436
  3.9 28.3 %copy-start.6 = (s32[2]{0:T(128)S(1)}, s32[2]{0:T(128)}, u32[]{:S(2)}) copy-start(s32[2]{0:T(128)} %length_ref.3) | copy-start | bytes 28
  3.9 28.2 %collective-permute-start = (bf16[2176,256]{1,0:T(8,128)(2,1)S(1)}, bf16[2176,256]{1,0:T(8,128)(2,1)S(1)}, u32[]{:S(2)}, u32[]{:S(2)}) collective-permute-start(bf16[2176,256]{1,0:T(8,128)(2,1)S(1)} %pad_maximum_fusion), channel_id=1, source_target_pairs={{0,4},{4,0},{8,12},{12,8},{1,5},{5,1},{9,13},{13,9},{2,6},{6,2},{1... | collective-permute-start | bytes 3342344 | tf_op jit(solution)/shard_map/ppermute | solution.py:30
  7.8 47.9 %collective-permute-start.9 = (bf16[2176,256]{1,0:T(8,128)(2,1)}, bf16[2176,256]{1,0:T(8,128)(2,1)S(1)}, u32[]{:S(2)}, u32[]{:S(2)}) collective-permute-start(bf16[2176,256]{1,0:T(8,128)(2,1)} %pad_maximum_fusion.1), channel_id=1, source_target_pairs={{0,4},{4,0},{8,12},{12,8},{1,5},{5,1},{9,13},{13,9},{2,6},{6,2},{1... | collective-permute-start | bytes 3342344 | tf_op jit(solution)/shard_map/ppermute | solution.py:30
  42.1 28.9 %collective-permute-start.1 = (bf16[128,2048]{1,0:T(8,128)(2,1)S(1)}, bf16[128,2048]{1,0:T(8,128)(2,1)}, u32[]{:S(2)}, u32[]{:S(2)}) collective-permute-start(bf16[128,2048]{1,0:T(8,128)(2,1)S(1)} %attend.2), channel_id=1, source_target_pairs={{0,2},{2,0},{1,3},{3,1},{4,6},{6,4},{5,7},{7,5},{8,10},{10,8},{9,1... | collective-permute-start | bytes 1572872 | tf_op jit(solution)/shard_map/ppermute | solution.py:30
  55.7 2.2 %copy-start.2 = (bf16[2,2048,512]{2,1,0:T(8,128)(2,1)S(1)}, bf16[2,2048,512]{2,1,0:T(8,128)(2,1)}, u32[]{:S(2)}) copy-start(bf16[2,2048,512]{2,1,0:T(8,128)(2,1)} %own_past.3) | copy-start | bytes 12582916
  57.9 1.2 copy-start.5
  59.1 11.9 %copy-start.15 = (bf16[2048,2048]{1,0:T(8,128)(2,1)S(1)}, bf16[2048,2048]{1,0:T(8,128)(2,1)}, u32[]{:S(2)}) copy-start(bf16[2048,2048]{1,0:T(8,128)(2,1)} %param.15) | copy-start | bytes 25165828
  69.2 13.8 %collective-permute-start.10 = (bf16[128,2048]{1,0:T(8,128)(2,1)S(1)}, bf16[128,2048]{1,0:T(8,128)(2,1)S(1)}, u32[]{:S(2)}, u32[]{:S(2)}) collective-permute-start(bf16[128,2048]{1,0:T(8,128)(2,1)S(1)} %attend.3), channel_id=1, source_target_pairs={{0,2},{2,0},{1,3},{3,1},{4,6},{6,4},{5,7},{7,5},{8,10},{10,8},{9,1... | collective-permute-start | bytes 1572872 | tf_op jit(solution)/shard_map/ppermute | solution.py:30
  74.5 11.0 %copy-start.8 = (bf16[256,2048]{1,0:T(8,128)(2,1)}, bf16[256,2048]{1,0:T(8,128)(2,1)S(1)}, u32[]{:S(2)}) copy-start(bf16[256,2048]{1,0:T(8,128)(2,1)S(1)} %convolution_convert_fusion.3) | copy-start | bytes 3145732
  92.7 9.1 %copy-start.14 = (s32[2]{0:T(128)S(1)}, s32[2]{0:T(128)}, u32[]{:S(2)}) copy-start(s32[2]{0:T(128)} %param.14) | copy-start | bytes 28
  92.7 26.4 %collective-permute-start.3 = (bf16[256,2048]{1,0:T(8,128)(2,1)}, bf16[256,2048]{1,0:T(8,128)(2,1)}, u32[]{:S(2)}, u32[]{:S(2)}) collective-permute-start(bf16[256,2048]{1,0:T(8,128)(2,1)} %get-tuple-element.12), channel_id=1, source_target_pairs={{0,4},{4,0},{8,12},{12,8},{1,5},{5,1},{9,13},{13,9},{2,6},{6,2},{1... | collective-permute-start | bytes 3145736 | tf_op jit(solution)/shard_map/ppermute | solution.py:30
  101.4 38.3 %collective-permute-start.11 = (bf16[256,2048]{1,0:T(8,128)(2,1)}, bf16[256,2048]{1,0:T(8,128)(2,1)}, u32[]{:S(2)}, u32[]{:S(2)}) collective-permute-start(bf16[256,2048]{1,0:T(8,128)(2,1)} %get-tuple-element.10), channel_id=1, source_target_pairs={{0,4},{4,0},{8,12},{12,8},{1,5},{5,1},{9,13},{13,9},{2,6},{6,2},{1... | collective-permute-start | bytes 3145736 | tf_op jit(solution)/shard_map/ppermute | solution.py:30
  107.7 11.4 %copy-start.9 = (bf16[256,2048]{1,0:T(8,128)(2,1)S(1)}, bf16[256,2048]{1,0:T(8,128)(2,1)}, u32[]{:S(2)}) copy-start(bf16[256,2048]{1,0:T(8,128)(2,1)} %copy-done.8) | copy-start | bytes 3145732
  119.1 20.5 %copy-start.10 = (bf16[256,2048]{1,0:T(8,128)(2,1)S(1)}, bf16[256,2048]{1,0:T(8,128)(2,1)}, u32[]{:S(2)}) copy-start(bf16[256,2048]{1,0:T(8,128)(2,1)} %get-tuple-element.11) | copy-start | bytes 3145732
  121.0 27.3 %collective-permute-start.4 = (bf16[128,2048]{1,0:T(8,128)(2,1)S(1)}, bf16[128,2048]{1,0:T(8,128)(2,1)S(1)}, u32[]{:S(2)}, u32[]{:S(2)}) collective-permute-start(bf16[128,2048]{1,0:T(8,128)(2,1)S(1)} %slice.35), channel_id=1, source_target_pairs={{0,2},{2,0},{1,3},{3,1},{4,6},{6,4},{5,7},{7,5},{8,10},{10,8},{9,1... | collective-permute-start | bytes 1572872 | tf_op jit(solution)/shard_map/ppermute | solution.py:30
  141.4 12.0 %collective-permute-start.12 = (bf16[128,2048]{1,0:T(8,128)(2,1)S(1)}, bf16[128,2048]{1,0:T(8,128)(2,1)S(1)}, u32[]{:S(2)}, u32[]{:S(2)}) collective-permute-start(bf16[128,2048]{1,0:T(8,128)(2,1)S(1)} %slice.37), channel_id=1, source_target_pairs={{0,2},{2,0},{1,3},{3,1},{4,6},{6,4},{5,7},{7,5},{8,10},{10,8},{9,1... | collective-permute-start | bytes 1572872 | tf_op jit(solution)/shard_map/ppermute | solution.py:30
  142.8 41.4 %copy-start.11 = (bf16[256,2048]{1,0:T(8,128)(2,1)S(1)}, bf16[256,2048]{1,0:T(8,128)(2,1)}, u32[]{:S(2)}) copy-start(bf16[256,2048]{1,0:T(8,128)(2,1)} %param.18) | copy-start | bytes 3145732
  142.8 41.4 %copy-start.12 = (bf16[4,64,2048]{2,1,0:T(8,128)(2,1)S(1)}, bf16[4,64,2048]{2,1,0:T(8,128)(2,1)}, u32[]{:S(2)}) copy-start(bf16[4,64,2048]{2,1,0:T(8,128)(2,1)} %param.17) | copy-start | bytes 3145732
  142.8 13.5 %collective-permute-start.6 = (bf16[128,64]{0,1:T(8,128)(2,1)S(1)}, bf16[128,64]{0,1:T(8,128)(2,1)S(1)}, u32[]{:S(2)}, u32[]{:S(2)}) collective-permute-start(bf16[128,64]{0,1:T(8,128)(2,1)S(1)} %dynamic-slice_convert_fusion.1), channel_id=1, source_target_pairs={{0,4},{4,8},{8,12},{12,0},{1,5},{5,9},{9,13},{13,1},{2,6},{6,10},{... | collective-permute-start | bytes 49160 | tf_op jit(solution)/shard_map/ppermute | solution.py:280
  144.4 24.4 %collective-permute-start.7 = (bf16[128,64]{0,1:T(8,128)(2,1)S(1)}, bf16[128,64]{0,1:T(8,128)(2,1)S(1)}, u32[]{:S(2)}, u32[]{:S(2)}) collective-permute-start(bf16[128,64]{0,1:T(8,128)(2,1)S(1)} %dynamic-slice_convert_fusion.1), channel_id=1, source_target_pairs={{0,8},{4,12},{8,0},{12,4},{1,9},{5,13},{9,1},{13,5},{2,10},{6,14},... | collective-permute-start | bytes 49160 | tf_op jit(solution)/shard_map/ppermute | solution.py:280
  147.0 21.8 %collective-permute-start.8 = (bf16[128,64]{0,1:T(8,128)(2,1)S(1)}, bf16[128,64]{0,1:T(8,128)(2,1)S(1)}, u32[]{:S(2)}, u32[]{:S(2)}) collective-permute-start(bf16[128,64]{0,1:T(8,128)(2,1)S(1)} %dynamic-slice_convert_fusion.1), channel_id=1, source_target_pairs={{0,12},{4,0},{8,4},{12,8},{1,13},{5,1},{9,5},{13,9},{2,14},{6,2},{... | collective-permute-start | bytes 49160 | tf_op jit(solution)/shard_map/ppermute | solution.py:280
  148.4 35.8 %collective-permute-start.5 = (bf16[128,2048]{1,0:T(8,128)(2,1)S(1)}, bf16[128,2048]{1,0:T(8,128)(2,1)S(1)}, u32[]{:S(2)}, u32[]{:S(2)}) collective-permute-start(bf16[128,2048]{1,0:T(8,128)(2,1)S(1)} %broadcast_select_fusion.3), channel_id=1, source_target_pairs={{0,8},{8,0},{4,12},{12,4},{1,9},{9,1},{5,13},{13,5},{2,10},{10,2},... | collective-permute-start | bytes 1572872 | tf_op jit(solution)/shard_map/ppermute | solution.py:30
  153.5 42.0 %collective-permute-start.13 = (bf16[128,2048]{1,0:T(8,128)(2,1)S(1)}, bf16[128,2048]{1,0:T(8,128)(2,1)S(1)}, u32[]{:S(2)}, u32[]{:S(2)}) collective-permute-start(bf16[128,2048]{1,0:T(8,128)(2,1)S(1)} %broadcast_select_fusion.2), channel_id=1, source_target_pairs={{0,8},{8,0},{4,12},{12,4},{1,9},{9,1},{5,13},{13,5},{2,10},{10,2},... | collective-permute-start | bytes 1572872 | tf_op jit(solution)/shard_map/ppermute | solution.py:30
  156.3 28.4 %collective-permute-start.14 = (bf16[128,64]{0,1:T(8,128)(2,1)S(1)}, bf16[128,64]{0,1:T(8,128)(2,1)S(1)}, u32[]{:S(2)}, u32[]{:S(2)}) collective-permute-start(bf16[128,64]{0,1:T(8,128)(2,1)S(1)} %dynamic-slice_convert_fusion), channel_id=1, source_target_pairs={{0,4},{4,8},{8,12},{12,0},{1,5},{5,9},{9,13},{13,1},{2,6},{6,10},{... | collective-permute-start | bytes 49160 | tf_op jit(solution)/shard_map/ppermute | solution.py:280
  168.8 26.7 %collective-permute-start.15 = (bf16[128,64]{0,1:T(8,128)(2,1)S(1)}, bf16[128,64]{0,1:T(8,128)(2,1)S(1)}, u32[]{:S(2)}, u32[]{:S(2)}) collective-permute-start(bf16[128,64]{0,1:T(8,128)(2,1)S(1)} %dynamic-slice_convert_fusion), channel_id=1, source_target_pairs={{0,8},{4,12},{8,0},{12,4},{1,9},{5,13},{9,1},{13,5},{2,10},{6,14},... | collective-permute-start | bytes 49160 | tf_op jit(solution)/shard_map/ppermute | solution.py:280
  168.8 26.7 %collective-permute-start.16 = (bf16[128,64]{0,1:T(8,128)(2,1)S(1)}, bf16[128,64]{0,1:T(8,128)(2,1)S(1)}, u32[]{:S(2)}, u32[]{:S(2)}) collective-permute-start(bf16[128,64]{0,1:T(8,128)(2,1)S(1)} %dynamic-slice_convert_fusion), channel_id=1, source_target_pairs={{0,12},{4,0},{8,4},{12,8},{1,13},{5,1},{9,5},{13,9},{2,14},{6,2},{... | collective-permute-start | bytes 49160 | tf_op jit(solution)/shard_map/ppermute | solution.py:280
  184.7 15.5 %copy-start.13 = (bf16[2048]{0:T(1024)(128)(2,1)S(1)}, bf16[2048]{0:T(1024)(128)(2,1)}, u32[]{:S(2)}) copy-start(bf16[2048]{0:T(1024)(128)(2,1)} %param.19) | copy-start | bytes 12292
  196.3 7.3 %copy-start.7 = (bf16[256,2048]{1,0:T(8,128)(2,1)}, bf16[256,2048]{1,0:T(8,128)(2,1)S(1)}, u32[]{:S(2)}) copy-start(bf16[256,2048]{1,0:T(8,128)(2,1)S(1)} %get-tuple-element.3) | copy-start | bytes 3145732
  196.3 5.4 %collective-permute-start.17 = (f32[256]{0:T(256)S(1)}, f32[256]{0:T(256)S(1)}, u32[]{:S(2)}, u32[]{:S(2)}) collective-permute-start(f32[256]{0:T(256)S(1)} %get-tuple-element.2), channel_id=1, source_target_pairs={{0,4},{4,8},{8,12},{12,0},{1,5},{5,9},{9,13},{13,1},{2,6},{6,10},{... | collective-permute-start | bytes 3080 | tf_op jit(solution)/shard_map/ppermute | solution.py:280
  197.1 4.6 %collective-permute-start.18 = (f32[256]{0:T(256)S(1)}, f32[256]{0:T(256)S(1)}, u32[]{:S(2)}, u32[]{:S(2)}) collective-permute-start(f32[256]{0:T(256)S(1)} %get-tuple-element.2), channel_id=1, source_target_pairs={{0,8},{4,12},{8,0},{12,4},{1,9},{5,13},{9,1},{13,5},{2,10},{6,14},... | collective-permute-start | bytes 3080 | tf_op jit(solution)/shard_map/ppermute | solution.py:280
  197.8 4.4 %collective-permute-start.19 = (f32[256]{0:T(256)S(1)}, f32[256]{0:T(256)S(1)}, u32[]{:S(2)}, u32[]{:S(2)}) collective-permute-start(f32[256]{0:T(256)S(1)} %get-tuple-element.2), channel_id=1, source_target_pairs={{0,12},{4,0},{8,4},{12,8},{1,13},{5,1},{9,5},{13,9},{2,14},{6,2},{... | collective-permute-start | bytes 3080 | tf_op jit(solution)/shard_map/ppermute | solution.py:280

commit v2 on v1

--- a/solution.py
+++ b/solution.py
@@ -314,39 +314,63 @@
     down = adapter_down_weight.reshape(adapter_down_weight.shape[0], ADAPTER_COUNT * ADAPTER_RANK)
 
     keep_own = parity == core
-    hidden, squares = [], []
+    weight_keep = jnp.where(keep_own, output_weight, weight_partner)
+    weight_send = jnp.where(keep_own, weight_partner, output_weight)
+    weight_keep, weight_send, arrived[0] = lax.optimization_barrier(
+        (weight_keep, weight_send, arrived[0])
+    )
+
+    def product(rows, weight):
+        return jnp.dot(rows, weight, preferred_element_type=jnp.float32).astype(jnp.bfloat16)
+
+    state = []
     for r in range(requests):
         attended = attend(
             r, prefix_length, parity, queries, prefix_key_value_cache, incoming_key_value, arrived[r]
         )
-        both = jnp.concatenate([attended, partner(attended, "dp", 0)], axis=0)
-        own = jnp.dot(both, output_weight, preferred_element_type=jnp.float32).astype(jnp.bfloat16)
-        other = jnp.dot(both, weight_partner, preferred_element_type=jnp.float32).astype(
+        across = partner(attended, "dp", 0)
+        flat = jnp.dot(attended, down, preferred_element_type=jnp.float32)
+        rank = lax.dynamic_slice(
+            flat, (0, adapter[r] * ADAPTER_RANK), (NEW, ADAPTER_RANK)
+        ).astype(jnp.bfloat16)
+        rank = jnp.pad(rank, ((0, 0), (0, HEAD_SIZE - ADAPTER_RANK)))
+        payload = jnp.concatenate([product(attended, weight_send), rank], axis=1)
+        got_mine = partner(payload, "tensor", 0)
+        keep_mine = product(attended, weight_keep)
+        sent_theirs = product(across, weight_send)
+        if r + 1 < requests:
+            keep_mine, arrived[r + 1], _ = lax.optimization_barrier(
+                (keep_mine, arrived[r + 1], sent_theirs)
+            )
+        got_theirs = partner(sent_theirs, "tensor", 0)
+        keep_theirs = product(across, weight_keep)
+        keep_mine, keep_theirs = lax.optimization_barrier((keep_mine, keep_theirs))
+        state.append((rank, keep_mine, keep_theirs, got_mine, got_theirs))
+
+    hidden = []
+    for r in range(requests):
+        rank, keep_mine, keep_theirs, got_mine, got_theirs = state[r]
+        theirs_pair = (keep_theirs.astype(jnp.float32) + got_theirs.astype(jnp.float32)).astype(
             jnp.bfloat16
         )
-        kept = jnp.where(keep_own, own, other)
-        sent = jnp.where(keep_own, other, own)
-        got = partner(sent, "tensor", 0)
-        pair = (kept.astype(jnp.float32) + got.astype(jnp.float32)).astype(jnp.bfloat16)
-        mine = pair[:NEW]
-        theirs = partner(pair[NEW:], "dp", 0)
+        theirs = partner(theirs_pair, "dp", 0)
+        mine = (keep_mine.astype(jnp.float32) + got_mine[:, :width].astype(jnp.float32)).astype(
+            jnp.bfloat16
+        )
+        rank_pair = (rank.astype(jnp.float32) + got_mine[:, width:].astype(jnp.float32)).astype(
+            jnp.bfloat16
+        )
         last_kept = jnp.where(x == upper, mine, theirs)
-        last_sent = jnp.where(x == upper, theirs, mine)
+        last_sent = jnp.concatenate([jnp.where(x == upper, theirs, mine), rank_pair], axis=1)
         last_got = partner(last_sent, "tensor", 1)
-        projected = last_kept.astype(jnp.float32) + last_got.astype(jnp.float32)
-
-        flat = jnp.dot(attended, down, preferred_element_type=jnp.float32)
-        partial = lax.dynamic_slice(flat, (0, adapter[r] * ADAPTER_RANK), (NEW, ADAPTER_RANK))
-        partial = partial.astype(jnp.bfloat16)
-        rank_total = partial.astype(jnp.float32)
-        for piece in from_others(partial, "tensor"):
-            rank_total = rank_total + piece.astype(jnp.float32)
+        projected = last_kept.astype(jnp.float32) + last_got[:, :width].astype(jnp.float32)
+        shrunk = (rank_pair.astype(jnp.float32) + last_got[:, width:].astype(jnp.float32)).astype(
+            jnp.bfloat16
+        )
         up = lax.dynamic_slice(
             adapter_up_weight, (adapter[r], 0, 0), (1, ADAPTER_RANK, width)
         )[0]
-        adapter_output = jnp.dot(
-            rank_total.astype(jnp.bfloat16), up, preferred_element_type=jnp.float32
-        )
+        adapter_output = jnp.dot(shrunk[:, :ADAPTER_RANK], up, preferred_element_type=jnp.float32)
         rows = residual[r * NEW : (r + 1) * NEW].astype(jnp.float32)
         hidden.append((rows + projected + adapter_output).astype(jnp.bfloat16))
     hidden = jnp.concatenate(hidden, axis=0)

time: 204 us -> 169 us (0.83)
  waiting for transfers between devices: 111 us -> 75.5 us
  other arithmetic: 6.58 us -> 15.4 us
  starting transfers between devices: 30.5 us -> 25.1 us
    ppermute x9 -> x3, waiting for transfers between devices: 23.9 us -> 3.56 us  [from_others(): lax.ppermute(block, axis, [(i, (i + shift) % count) for i in range(count)])]
    ppermute x11 -> x13, waiting for transfers between devices: 87.5 us -> 71.9 us  [partner(): return lax.ppermute(block, axis, route)]
    ppermute x9 -> x3, starting transfers between devices: 16 us -> 4.11 us  [from_others(): lax.ppermute(block, axis, [(i, (i + shift) % count) for i in range(count)])]
    select_n x2 -> x3, other arithmetic: 0.13 us -> 9.43 us  [the longest x1 9.03 us: shards_fast(): weight_send = jnp.where(keep_own, weight_partner, output_weight)]
    ppermute x11 -> x13, starting transfers between devices: 14.6 us -> 21 us  [partner(): return lax.ppermute(block, axis, route)]
    unnamed x32 -> x36, local copies, waits for them, and re-layouts: 3.48 us -> 0.08 us
    convert_element_type x2 -> x4, other arithmetic: 3.58 us -> 0.28 us  [the longest x2 0.25 us: shards_fast(): (keep_theirs.astype(jnp.float32) + got_theirs.astype(jnp.float32)).astype...]
    dot_general x6 -> x10, matrix products: 21 us -> 20.3 us  [the longest x8 17 us: product(): jnp.dot(rows, weight, preferred_element_type=jnp.float32)]
  transfers between devices with their start and end apart: 20 -> 16, of which waited for: 11 -> 12; matrix products, arithmetic and copies ran while one was open for 11% -> 22% of each run, Pallas kernels for 10% -> 12%
where the time goes in v2:
time: 169 us
  waiting for transfers between devices  75.5 us (45%)
  starting transfers between devices  25.1 us (15%)
  matrix products  21.3 us (13%)
  Pallas kernels  20.1 us (12%)
  other arithmetic  15.4 us (9%)
  between operations  6.25 us (4%)
  local copies, waits for them, and re-layouts  4.97 us (3%)
    ppermute x13, waiting for transfers between devices, partner(): return lax.ppermute(block, axis, route)  71.9 us
    ppermute x13, starting transfers between devices, partner(): return lax.ppermute(block, axis, route)  21 us
    pallas_call x2, Pallas kernels, attend(): pl.pallas_call(functools.partial(attend_kernel, heads_tile), out_shape=ja...  20.1 us
    dot_general x8, matrix products, product(): jnp.dot(rows, weight, preferred_element_type=jnp.float32)  17 us
    select_n x1, other arithmetic, shards_fast(): weight_send = jnp.where(keep_own, weight_partner, output_weight)  9.03 us
    ppermute x3, starting transfers between devices, from_others(): lax.ppermute(block, axis, [(i, (i + shift) % count) for i in range(count)])  4.11 us
    ppermute x3, waiting for transfers between devices, from_others(): lax.ppermute(block, axis, [(i, (i + shift) % count) for i in range(count)])  3.56 us
  transfers between devices with their start and end apart: 16, of which 12 were waited for; matrix products, arithmetic and copies ran while one was open for 22% of the time, Pallas kernels for 12%

profile of v2, /device:TPU:0, one launch (start us, length us, event | category | flops | bytes accessed | tf_op | source)
XLA Modules:
  0.0 168.6 jit_solution(16651593048828591199)
XLA Ops:
  0.6 0.0 copy-start
  0.6 0.5 collective-permute-start
  1.2 0.9 constant_dynamic-slice_fusion.1
  2.0 1.7 dynamic-slice_bitcast_fusion
  3.7 0.0 copy-start.12
  3.7 1.1 pad_maximum_fusion
  4.8 2.7 %collective-permute-start.1 = (bf16[2176,256]{1,0:T(8,128)(2,1)}, bf16[2176,256]{1,0:T(8,128)(2,1)S(1)}, u32[]{:S(2)}, u32[]{:S(2)}) collective-permute-start(bf16[2176,256]{1,0:T(8,128)(2,1)} %pad_maximum_fusion), channel_id=1, source_target_pairs={{0,4},{4,0},{8,12},{12,8},{1,5},{5,1},{9,13},{13,9},{2,6},{6,2},{1... | collective-permute-start | bytes 3342344 | tf_op jit(solution)/shard_map/ppermute | solution.py:30
  7.5 1.1 pad_maximum_fusion.1
  8.6 0.6 fusion.19
  10.6 0.1 pad_add_fusion.parity_ref
  10.6 0.1 pad_add_fusion.1.parity_ref
  10.7 3.6 %collective-permute-done = bf16[2048,2048]{1,0:T(8,128)(2,1)} collective-permute-done((bf16[2048,2048]{1,0:T(8,128)(2,1)}, bf16[2048,2048]{1,0:T(8,128)(2,1)}, u32[]{:S(2)}, u32[]{:S(2)}) %collective-permute-start) | collective-permute-done | bytes 8388640 | tf_op jit(solution)/shard_map/ppermute | solution.py:30
  14.3 9.0 %broadcast_select_fusion = (bf16[2048,2048]{1,0:T(8,128)(2,1)}, bf16[2048,2048]{1,0:T(8,128)(2,1)S(1)}) fusion(bf16[2048,2048]{1,0:T(8,128)(2,1)} %collective-permute-done, bf16[2048,2048]{1,0:T(8,128)(2,1)} %param.15, pred[]{:T(512)S(6)} %eq.12), kind=kLoop, calls=%fused_computation | loop fusion | flops 8388608 | bytes 33554432 | tf_op jit(solution)/shard_map/jit(_where)/select_n | solution.py:318
  23.3 9.8 %collective-permute-done.1.recv = bf16[2176,256]{1,0:T(8,128)(2,1)S(1)} collective-permute-done((bf16[2176,256]{1,0:T(8,128)(2,1)}, bf16[2176,256]{1,0:T(8,128)(2,1)S(1)}, u32[]{:S(2)}, u32[]{:S(2)}) %collective-permute-start.1) | collective-permute-done | bytes 1114144 | tf_op jit(solution)/shard_map/ppermute | solution.py:30
  33.2 9.9 %attend.2 = bf16[128,2048]{1,0:T(8,128)(2,1)S(1)} custom-call(s32[2]{0:T(128)S(1)} %copy-done.4, s32[2]{0:T(128)S(1)} %pad_add_fusion.parity_ref, bf16[256,2048]{1,0:T(8,128)(2,1)S(1)} %copy-done.3, bf16[2,2048,512]{2,1,0:T(8,128)(2,1)S(1)} %copy-done.1, bf16[256,512]{1,0:T(8,128)(2,1)S(1)} %copy-done.2, bf16[2176,256]{1,0:T(8,128)(2,1)S(1)} %collective-permute-done.1.recv), custom_call_target="tpu_custom_call" | custom-call | flops 2281701376 | bytes 3276800 | tf_op jit(solution)/shard_map/attend/pallas_call | solution.py:247
  43.1 1.9 %collective-permute-start.3 = (bf16[128,2048]{1,0:T(8,128)(2,1)S(1)}, bf16[128,2048]{1,0:T(8,128)(2,1)S(1)}, u32[]{:S(2)}, u32[]{:S(2)}) collective-permute-start(bf16[128,2048]{1,0:T(8,128)(2,1)S(1)} %attend.2), channel_id=1, source_target_pairs={{0,2},{2,0},{1,3},{3,1},{4,6},{6,4},{5,7},{7,5},{8,10},{10,8},{9,1... | collective-permute-start | bytes 1572872 | tf_op jit(solution)/shard_map/ppermute | solution.py:30
  45.1 4.7 %convolution_convert_fusion.4 = bf16[128,2048]{1,0:T(8,128)(2,1)S(1)} fusion(bf16[128,2048]{1,0:T(8,128)(2,1)S(1)} %attend.2, bf16[2048,2048]{1,0:T(8,128)(2,1)} %get-tuple-element.13), kind=kOutput, calls=%fused_computation.8 | convolution fusion | flops 1074003968 | bytes 9437184 | tf_op jit(solution)/shard_map/dot_general | solution.py:324
  49.7 0.5 fusion.20
  50.2 0.1 dynamic-slice_convert_fusion.1
  50.4 1.6 collective-permute-start.4
  52.1 1.3 convolution_convert_fusion.7
  53.3 3.2 %collective-permute-done.3 = bf16[128,2048]{1,0:T(8,128)(2,1)S(1)} collective-permute-done((bf16[128,2048]{1,0:T(8,128)(2,1)S(1)}, bf16[128,2048]{1,0:T(8,128)(2,1)S(1)}, u32[]{:S(2)}, u32[]{:S(2)}) %collective-permute-start.3) | collective-permute-done | bytes 524320 | tf_op jit(solution)/shard_map/ppermute | solution.py:30
  56.5 1.3 convolution_convert_fusion.6
  57.9 1.7 collective-permute-start.5
  59.5 10.1 %attend.3 = bf16[128,2048]{1,0:T(8,128)(2,1)S(1)} custom-call(s32[2]{0:T(128)S(1)} %copy-done.4, s32[2]{0:T(128)S(1)} %pad_add_fusion.1.parity_ref, bf16[256,2048]{1,0:T(8,128)(2,1)S(1)} %copy-done.3, bf16[2,2048,512]{2,1,0:T(8,128)(2,1)S(1)} %copy-done.1, bf16[256,512]{1,0:T(8,128)(2,1)S(1)} %copy-done.2, bf16[2176,256]{1,0:T(8,128)(2,1)S(1)} %collective-permute-done.2.recv), custom_call_target="tpu_custom_call" | custom-call | flops 2281701376 | bytes 3276800 | tf_op jit(solution)/shard_map/attend/pallas_call | solution.py:247
  69.7 1.5 collective-permute-start.8
  71.2 4.7 %convolution_convert_fusion.1 = bf16[128,2048]{1,0:T(8,128)(2,1)S(1)} fusion(bf16[128,2048]{1,0:T(8,128)(2,1)S(1)} %attend.3, bf16[2048,2048]{1,0:T(8,128)(2,1)} %get-tuple-element.13), kind=kOutput, calls=%fused_computation.5 | convolution fusion | flops 1074003968 | bytes 9437184 | tf_op jit(solution)/shard_map/dot_general | solution.py:324
  75.9 0.5 fusion.21
  76.4 0.1 dynamic-slice_convert_fusion
  76.5 1.3 convolution_convert_fusion.5
  77.8 0.5 collective-permute-start.9
  78.4 1.3 convolution_convert_fusion.3
  79.7 0.5 collective-permute-done.5
  80.2 0.1 add_convert_fusion.4
  80.3 1.9 %collective-permute-start.6 = (bf16[128,2048]{1,0:T(8,128)(2,1)S(1)}, bf16[128,2048]{1,0:T(8,128)(2,1)S(1)}, u32[]{:S(2)}, u32[]{:S(2)}) collective-permute-start(bf16[128,2048]{1,0:T(8,128)(2,1)S(1)} %add_convert_fusion.4), channel_id=1, source_target_pairs={{0,2},{2,0},{1,3},{3,1},{4,6},{6,4},{5,7},{7,5},{8,10},{10,8},{9,1... | collective-permute-start | bytes 1572872 | tf_op jit(solution)/shard_map/ppermute | solution.py:30
  82.3 1.3 convolution_convert_fusion
  83.6 1.6 collective-permute-start.10
  85.3 1.3 convolution_convert_fusion.2
  86.5 6.9 %collective-permute-done.9 = bf16[128,2176]{1,0:T(8,128)(2,1)S(1)} collective-permute-done((bf16[128,2176]{1,0:T(8,128)(2,1)S(1)}, bf16[128,2176]{1,0:T(8,128)(2,1)S(1)}, u32[]{:S(2)}, u32[]{:S(2)}) %collective-permute-start.9) | collective-permute-done | bytes 557088 | tf_op jit(solution)/shard_map/ppermute | solution.py:30
  93.5 9.6 %collective-permute-done.10 = bf16[128,2048]{1,0:T(8,128)(2,1)S(1)} collective-permute-done((bf16[128,2048]{1,0:T(8,128)(2,1)S(1)}, bf16[128,2048]{1,0:T(8,128)(2,1)S(1)}, u32[]{:S(2)}, u32[]{:S(2)}) %collective-permute-start.10) | collective-permute-done | bytes 524320 | tf_op jit(solution)/shard_map/ppermute | solution.py:30
  103.1 0.1 add_convert_fusion.1
  103.2 1.8 %collective-permute-start.11 = (bf16[128,2048]{1,0:T(8,128)(2,1)S(1)}, bf16[128,2048]{1,0:T(8,128)(2,1)S(1)}, u32[]{:S(2)}, u32[]{:S(2)}) collective-permute-start(bf16[128,2048]{1,0:T(8,128)(2,1)S(1)} %add_convert_fusion.1), channel_id=1, source_target_pairs={{0,2},{2,0},{1,3},{3,1},{4,6},{6,4},{5,7},{7,5},{8,10},{10,8},{9,1... | collective-permute-start | bytes 1572872 | tf_op jit(solution)/shard_map/ppermute | solution.py:30
  105.0 0.2 broadcast_select_fusion.3
  105.2 0.9 pad_maximum_fusion.4
  106.0 2.6 %collective-permute-start.7 = (bf16[128,2176]{1,0:T(8,128)(2,1)}, bf16[128,2176]{1,0:T(8,128)(2,1)}, u32[]{:S(2)}, u32[]{:S(2)}) collective-permute-start(bf16[128,2176]{1,0:T(8,128)(2,1)} %pad_maximum_fusion.4), channel_id=1, source_target_pairs={{0,8},{8,0},{4,12},{12,4},{1,9},{9,1},{5,13},{13,5},{2,10},{10,2},... | collective-permute-start | bytes 1671176 | tf_op jit(solution)/shard_map/ppermute | solution.py:30
  108.6 8.1 %collective-permute-done.11 = bf16[128,2048]{1,0:T(8,128)(2,1)S(1)} collective-permute-done((bf16[128,2048]{1,0:T(8,128)(2,1)S(1)}, bf16[128,2048]{1,0:T(8,128)(2,1)S(1)}, u32[]{:S(2)}, u32[]{:S(2)}) %collective-permute-start.11) | collective-permute-done | bytes 524320 | tf_op jit(solution)/shard_map/ppermute | solution.py:30
  116.7 0.2 broadcast_select_fusion.2
  116.9 0.9 pad_maximum_fusion.6
  117.8 2.6 %collective-permute-start.12 = (bf16[128,2176]{1,0:T(8,128)(2,1)}, bf16[128,2176]{1,0:T(8,128)(2,1)}, u32[]{:S(2)}, u32[]{:S(2)}) collective-permute-start(bf16[128,2176]{1,0:T(8,128)(2,1)} %pad_maximum_fusion.6), channel_id=1, source_target_pairs={{0,8},{8,0},{4,12},{12,4},{1,9},{9,1},{5,13},{13,5},{2,10},{10,2},... | collective-permute-start | bytes 1671176 | tf_op jit(solution)/shard_map/ppermute | solution.py:30
  124.3 0.0 copy-start.13
  124.3 21.9 %collective-permute-done.7 = bf16[128,2176]{1,0:T(8,128)(2,1)} collective-permute-done((bf16[128,2176]{1,0:T(8,128)(2,1)}, bf16[128,2176]{1,0:T(8,128)(2,1)}, u32[]{:S(2)}, u32[]{:S(2)}) %collective-permute-start.7) | collective-permute-done | bytes 557088 | tf_op jit(solution)/shard_map/ppermute | solution.py:30
  146.2 0.8 slice.61
  147.0 1.7 %add_convert_fusion.3 = bf16[128,2048]{1,0:T(8,128)(2,1)S(1)} fusion(bf16[128,2176]{1,0:T(8,128)(2,1)} %collective-permute-done.7, bf16[128,2048]{1,0:T(8,128)(2,1)} %copy-done.8, bf16[256,2048]{1,0:T(8,128)(2,1)} %param.18, pred[]{:T(512)S(6)} %eq.6, bf16[4,64,2048]{2,1,0:T(8,128)(2,1)} %param.17, s32[]{:T(128)S(6)} %select_n.71, ...), kind=kOutput, calls=%fused_computation.21 | convolution fusion | flops 36732928 | bytes 3473413 | tf_op jit(solution)/shard_map/dot_general | solution.py:373
  148.7 8.3 %collective-permute-done.12 = bf16[128,2176]{1,0:T(8,128)(2,1)} collective-permute-done((bf16[128,2176]{1,0:T(8,128)(2,1)}, bf16[128,2176]{1,0:T(8,128)(2,1)}, u32[]{:S(2)}, u32[]{:S(2)}) %collective-permute-start.12) | collective-permute-done | bytes 557088 | tf_op jit(solution)/shard_map/ppermute | solution.py:30
  157.0 0.8 slice.67
  157.7 0.0 copy-start.11
  157.7 1.6 add_convert_fusion
  159.3 0.3 fusion
  159.6 0.7 collective-permute-start.13
  160.3 3.4 %collective-permute-start.14 = (f32[256]{0:T(256)S(1)}, f32[256]{0:T(256)S(1)}, u32[]{:S(2)}, u32[]{:S(2)}) collective-permute-start(f32[256]{0:T(256)S(1)} %get-tuple-element.20), channel_id=1, source_target_pairs={{0,8},{4,12},{8,0},{12,4},{1,9},{5,13},{9,1},{13,5},{2,10},{6,14},... | collective-permute-start | bytes 3080 | tf_op jit(solution)/shard_map/ppermute | solution.py:280
  163.7 1.3 collective-permute-done.13
  165.0 0.2 collective-permute-done.14
  165.3 2.0 %collective-permute-done.15 = f32[256]{0:T(256)S(1)} collective-permute-done((f32[256]{0:T(256)S(1)}, f32[256]{0:T(256)S(1)}, u32[]{:S(2)}, u32[]{:S(2)}) %collective-permute-start.15) | collective-permute-done | bytes 1056 | tf_op jit(solution)/shard_map/ppermute | solution.py:280
  167.3 1.3 fusion.2
  (48 shorter events, 0.2 us)
Async XLA Ops:
  0.6 49.1 %copy-start = (bf16[2048,4,64]{0,2,1:T(8,128)(2,1)S(1)}, bf16[2048,4,64]{0,2,1:T(8,128)(2,1)}, u32[]{:S(2)}) copy-start(bf16[2048,4,64]{0,2,1:T(8,128)(2,1)} %param.16) | copy-start | bytes 3145732
  0.6 13.6 %collective-permute-start = (bf16[2048,2048]{1,0:T(8,128)(2,1)}, bf16[2048,2048]{1,0:T(8,128)(2,1)}, u32[]{:S(2)}, u32[]{:S(2)}) collective-permute-start(bf16[2048,2048]{1,0:T(8,128)(2,1)} %param.15), channel_id=1, source_target_pairs={{0,1},{1,0},{2,3},{3,2},{4,5},{5,4},{6,7},{7,6},{8,9},{9,8},{10,11... | collective-permute-start | bytes 25165832 | tf_op jit(solution)/shard_map/ppermute | solution.py:30
  3.7 4.9 %copy-start.12 = (s32[2]{0:T(128)S(1)}, s32[2]{0:T(128)}, u32[]{:S(2)}) copy-start(s32[2]{0:T(128)} %param.14) | copy-start | bytes 28
  4.8 28.3 %collective-permute-start.1 = (bf16[2176,256]{1,0:T(8,128)(2,1)}, bf16[2176,256]{1,0:T(8,128)(2,1)S(1)}, u32[]{:S(2)}, u32[]{:S(2)}) collective-permute-start(bf16[2176,256]{1,0:T(8,128)(2,1)} %pad_maximum_fusion), channel_id=1, source_target_pairs={{0,4},{4,0},{8,12},{12,8},{1,5},{5,1},{9,13},{13,9},{2,6},{6,2},{1... | collective-permute-start | bytes 3342344 | tf_op jit(solution)/shard_map/ppermute | solution.py:30
  8.6 50.9 %collective-permute-start.2 = (bf16[2176,256]{1,0:T(8,128)(2,1)}, bf16[2176,256]{1,0:T(8,128)(2,1)S(1)}, u32[]{:S(2)}, u32[]{:S(2)}) collective-permute-start(bf16[2176,256]{1,0:T(8,128)(2,1)} %pad_maximum_fusion.1), channel_id=1, source_target_pairs={{0,4},{4,0},{8,12},{12,8},{1,5},{5,1},{9,13},{13,9},{2,6},{6,2},{1... | collective-permute-start | bytes 3342344 | tf_op jit(solution)/shard_map/ppermute | solution.py:30
  10.7 22.4 %copy-start.1 = (bf16[2,2048,512]{2,1,0:T(8,128)(2,1)S(1)}, bf16[2,2048,512]{2,1,0:T(8,128)(2,1)}, u32[]{:S(2)}) copy-start(bf16[2,2048,512]{2,1,0:T(8,128)(2,1)} %own_past.3) | copy-start | bytes 12582916
  10.7 22.4 %copy-start.2 = (bf16[256,512]{1,0:T(8,128)(2,1)S(1)}, bf16[256,512]{1,0:T(8,128)(2,1)}, u32[]{:S(2)}) copy-start(bf16[256,512]{1,0:T(8,128)(2,1)} %own_new.3) | copy-start | bytes 786436
  10.7 22.4 %copy-start.3 = (bf16[256,2048]{1,0:T(8,128)(2,1)S(1)}, bf16[256,2048]{1,0:T(8,128)(2,1)}, u32[]{:S(2)}) copy-start(bf16[256,2048]{1,0:T(8,128)(2,1)} %q_ref.3) | copy-start | bytes 3145732
  10.7 22.4 %copy-start.4 = (s32[2]{0:T(128)S(1)}, s32[2]{0:T(128)}, u32[]{:S(2)}) copy-start(s32[2]{0:T(128)} %length_ref.3) | copy-start | bytes 28
  43.1 13.4 %collective-permute-start.3 = (bf16[128,2048]{1,0:T(8,128)(2,1)S(1)}, bf16[128,2048]{1,0:T(8,128)(2,1)S(1)}, u32[]{:S(2)}, u32[]{:S(2)}) collective-permute-start(bf16[128,2048]{1,0:T(8,128)(2,1)S(1)} %attend.2), channel_id=1, source_target_pairs={{0,2},{2,0},{1,3},{3,1},{4,6},{6,4},{5,7},{7,5},{8,10},{10,8},{9,1... | collective-permute-start | bytes 1572872 | tf_op jit(solution)/shard_map/ppermute | solution.py:30
  50.4 6.2 %slice-start = ((s8[8388608]{0:T(1024)(128)(4,1)}), s8[4194304]{0:T(1024)(128)(4,1)S(1)}, s32[]{:S(2)}) async-start(s8[8388608]{0:T(1024)(128)(4,1)} %bitcast.40), calls=%async_computation | async-start | bytes 8388608
  50.4 6.1 %slice-start.1 = ((s8[8388608]{0:T(1024)(128)(4,1)}), s8[4194304]{0:T(1024)(128)(4,1)S(1)}, s32[]{:S(2)}) async-start(s8[8388608]{0:T(1024)(128)(4,1)} %bitcast.40), calls=%async_computation.1 | async-start | bytes 8388608
  50.4 29.2 %collective-permute-start.4 = (bf16[128,2176]{1,0:T(8,128)(2,1)S(1)}, bf16[128,2176]{1,0:T(8,128)(2,1)S(1)}, u32[]{:S(2)}, u32[]{:S(2)}) collective-permute-start(bf16[128,2176]{1,0:T(8,128)(2,1)S(1)} %pad_maximum_fusion.3), channel_id=1, source_target_pairs={{0,4},{4,0},{8,12},{12,8},{1,5},{5,1},{9,13},{13,9},{2,6},{6,2},{1... | collective-permute-start | bytes 1671176 | tf_op jit(solution)/shard_map/ppermute | solution.py:30
  57.9 22.3 %collective-permute-start.5 = (bf16[128,2048]{1,0:T(8,128)(2,1)S(1)}, bf16[128,2048]{1,0:T(8,128)(2,1)S(1)}, u32[]{:S(2)}, u32[]{:S(2)}) collective-permute-start(bf16[128,2048]{1,0:T(8,128)(2,1)S(1)} %convolution_convert_fusion.6), channel_id=1, source_target_pairs={{0,4},{4,0},{8,12},{12,8},{1,5},{5,1},{9,13},{13,9},{2,6},{6,2},{1... | collective-permute-start | bytes 1572872 | tf_op jit(solution)/shard_map/ppermute | solution.py:30
  69.7 12.6 %collective-permute-start.8 = (bf16[128,2048]{1,0:T(8,128)(2,1)S(1)}, bf16[128,2048]{1,0:T(8,128)(2,1)S(1)}, u32[]{:S(2)}, u32[]{:S(2)}) collective-permute-start(bf16[128,2048]{1,0:T(8,128)(2,1)S(1)} %attend.3), channel_id=1, source_target_pairs={{0,2},{2,0},{1,3},{3,1},{4,6},{6,4},{5,7},{7,5},{8,10},{10,8},{9,1... | collective-permute-start | bytes 1572872 | tf_op jit(solution)/shard_map/ppermute | solution.py:30
  77.8 4.5 %slice-start.2 = ((s8[8388608]{0:T(1024)(128)(4,1)}), s8[4194304]{0:T(1024)(128)(4,1)S(1)}, s32[]{:S(2)}) async-start(s8[8388608]{0:T(1024)(128)(4,1)} %bitcast.42), calls=%async_computation.2 | async-start | bytes 8388608
  77.8 4.4 %slice-start.3 = ((s8[8388608]{0:T(1024)(128)(4,1)}), s8[4194304]{0:T(1024)(128)(4,1)S(1)}, s32[]{:S(2)}) async-start(s8[8388608]{0:T(1024)(128)(4,1)} %bitcast.42), calls=%async_computation.3 | async-start | bytes 8388608
  77.8 15.6 %collective-permute-start.9 = (bf16[128,2176]{1,0:T(8,128)(2,1)S(1)}, bf16[128,2176]{1,0:T(8,128)(2,1)S(1)}, u32[]{:S(2)}, u32[]{:S(2)}) collective-permute-start(bf16[128,2176]{1,0:T(8,128)(2,1)S(1)} %pad_maximum_fusion.5), channel_id=1, source_target_pairs={{0,4},{4,0},{8,12},{12,8},{1,5},{5,1},{9,13},{13,9},{2,6},{6,2},{1... | collective-permute-start | bytes 1671176 | tf_op jit(solution)/shard_map/ppermute | solution.py:30
  80.3 24.6 %collective-permute-start.6 = (bf16[128,2048]{1,0:T(8,128)(2,1)S(1)}, bf16[128,2048]{1,0:T(8,128)(2,1)S(1)}, u32[]{:S(2)}, u32[]{:S(2)}) collective-permute-start(bf16[128,2048]{1,0:T(8,128)(2,1)S(1)} %add_convert_fusion.4), channel_id=1, source_target_pairs={{0,2},{2,0},{1,3},{3,1},{4,6},{6,4},{5,7},{7,5},{8,10},{10,8},{9,1... | collective-permute-start | bytes 1572872 | tf_op jit(solution)/shard_map/ppermute | solution.py:30
  83.6 19.5 %collective-permute-start.10 = (bf16[128,2048]{1,0:T(8,128)(2,1)S(1)}, bf16[128,2048]{1,0:T(8,128)(2,1)S(1)}, u32[]{:S(2)}, u32[]{:S(2)}) collective-permute-start(bf16[128,2048]{1,0:T(8,128)(2,1)S(1)} %convolution_convert_fusion), channel_id=1, source_target_pairs={{0,4},{4,0},{8,12},{12,8},{1,5},{5,1},{9,13},{13,9},{2,6},{6,2},{1... | collective-permute-start | bytes 1572872 | tf_op jit(solution)/shard_map/ppermute | solution.py:30
  93.5 23.2 %copy-start.6 = (bf16[128,2176]{1,0:T(8,128)(2,1)}, bf16[128,2176]{1,0:T(8,128)(2,1)S(1)}, u32[]{:S(2)}) copy-start(bf16[128,2176]{1,0:T(8,128)(2,1)S(1)} %collective-permute-done.9) | copy-start | bytes 1671172
  103.2 13.5 %collective-permute-start.11 = (bf16[128,2048]{1,0:T(8,128)(2,1)S(1)}, bf16[128,2048]{1,0:T(8,128)(2,1)S(1)}, u32[]{:S(2)}, u32[]{:S(2)}) collective-permute-start(bf16[128,2048]{1,0:T(8,128)(2,1)S(1)} %add_convert_fusion.1), channel_id=1, source_target_pairs={{0,2},{2,0},{1,3},{3,1},{4,6},{6,4},{5,7},{7,5},{8,10},{10,8},{9,1... | collective-permute-start | bytes 1572872 | tf_op jit(solution)/shard_map/ppermute | solution.py:30
  105.0 11.9 %copy-start.8 = (bf16[128,2048]{1,0:T(8,128)(2,1)}, bf16[128,2048]{1,0:T(8,128)(2,1)S(1)}, u32[]{:S(2)}) copy-start(bf16[128,2048]{1,0:T(8,128)(2,1)S(1)} %collective-permute-done.6) | copy-start | bytes 1572868
  106.0 40.2 %collective-permute-start.7 = (bf16[128,2176]{1,0:T(8,128)(2,1)}, bf16[128,2176]{1,0:T(8,128)(2,1)}, u32[]{:S(2)}, u32[]{:S(2)}) collective-permute-start(bf16[128,2176]{1,0:T(8,128)(2,1)} %pad_maximum_fusion.4), channel_id=1, source_target_pairs={{0,8},{8,0},{4,12},{12,4},{1,9},{9,1},{5,13},{13,5},{2,10},{10,2},... | collective-permute-start | bytes 1671176 | tf_op jit(solution)/shard_map/ppermute | solution.py:30
  116.7 1.1 copy-start.9
  117.8 39.9 %copy-start.7 = (bf16[128,2176]{1,0:T(8,128)(2,1)S(1)}, bf16[128,2176]{1,0:T(8,128)(2,1)}, u32[]{:S(2)}) copy-start(bf16[128,2176]{1,0:T(8,128)(2,1)} %copy-done.6) | copy-start | bytes 1671172
  117.8 39.2 %collective-permute-start.12 = (bf16[128,2176]{1,0:T(8,128)(2,1)}, bf16[128,2176]{1,0:T(8,128)(2,1)}, u32[]{:S(2)}, u32[]{:S(2)}) collective-permute-start(bf16[128,2176]{1,0:T(8,128)(2,1)} %pad_maximum_fusion.6), channel_id=1, source_target_pairs={{0,8},{8,0},{4,12},{12,4},{1,9},{9,1},{5,13},{13,5},{2,10},{10,2},... | collective-permute-start | bytes 1671176 | tf_op jit(solution)/shard_map/ppermute | solution.py:30
  124.3 33.4 %copy-start.10 = (bf16[128,2048]{1,0:T(8,128)(2,1)S(1)}, bf16[128,2048]{1,0:T(8,128)(2,1)}, u32[]{:S(2)}) copy-start(bf16[128,2048]{1,0:T(8,128)(2,1)} %copy-done.9) | copy-start | bytes 1572868
  124.3 33.4 %copy-start.13 = (bf16[256,2048]{1,0:T(8,128)(2,1)S(1)}, bf16[256,2048]{1,0:T(8,128)(2,1)}, u32[]{:S(2)}) copy-start(bf16[256,2048]{1,0:T(8,128)(2,1)} %param.18) | copy-start | bytes 3145732
  157.7 6.0 %copy-start.11 = (bf16[2048]{0:T(1024)(128)(2,1)S(1)}, bf16[2048]{0:T(1024)(128)(2,1)}, u32[]{:S(2)}) copy-start(bf16[2048]{0:T(1024)(128)(2,1)} %param.19) | copy-start | bytes 12292
  159.6 9.0 %copy-start.5 = (bf16[256,2048]{1,0:T(8,128)(2,1)}, bf16[256,2048]{1,0:T(8,128)(2,1)S(1)}, u32[]{:S(2)}) copy-start(bf16[256,2048]{1,0:T(8,128)(2,1)S(1)} %get-tuple-element.21) | copy-start | bytes 3145732
  159.6 5.4 %collective-permute-start.13 = (f32[256]{0:T(256)S(1)}, f32[256]{0:T(256)S(1)}, u32[]{:S(2)}, u32[]{:S(2)}) collective-permute-start(f32[256]{0:T(256)S(1)} %get-tuple-element.20), channel_id=1, source_target_pairs={{0,4},{4,8},{8,12},{12,0},{1,5},{5,9},{9,13},{13,1},{2,6},{6,10},{... | collective-permute-start | bytes 3080 | tf_op jit(solution)/shard_map/ppermute | solution.py:280
  160.3 4.9 %collective-permute-start.14 = (f32[256]{0:T(256)S(1)}, f32[256]{0:T(256)S(1)}, u32[]{:S(2)}, u32[]{:S(2)}) collective-permute-start(f32[256]{0:T(256)S(1)} %get-tuple-element.20), channel_id=1, source_target_pairs={{0,8},{4,12},{8,0},{12,4},{1,9},{5,13},{9,1},{13,5},{2,10},{6,14},... | collective-permute-start | bytes 3080 | tf_op jit(solution)/shard_map/ppermute | solution.py:280
  163.7 3.6 %collective-permute-start.15 = (f32[256]{0:T(256)S(1)}, f32[256]{0:T(256)S(1)}, u32[]{:S(2)}, u32[]{:S(2)}) collective-permute-start(f32[256]{0:T(256)S(1)} %get-tuple-element.20), channel_id=1, source_target_pairs={{0,12},{4,0},{8,4},{12,8},{1,13},{5,1},{9,5},{13,9},{2,14},{6,2},{... | collective-permute-start | bytes 3080 | tf_op jit(solution)/shard_map/ppermute | solution.py:280

commit v3 on v2

--- a/solution.py
+++ b/solution.py
@@ -179,26 +179,37 @@
 
 
 def attend_kernel(
-    heads_tile, length_ref, parity_ref, q_ref, own_past, own_new, recv, out_ref, keys, values
+    heads_tile,
+    length_ref,
+    meta_ref,
+    q_ref,
+    own_past,
+    own_new,
+    recv_past,
+    recv_new,
+    out_ref,
+    keys,
+    values,
 ):
-    request = pl.program_id(0)
     row_tile = 2
     past, new = own_past.shape[1], own_new.shape[0]
 
-    @pl.when((pl.program_id(2) == 0) & (parity_ref[0] == 0))
+    @pl.when((pl.program_id(1) == 0) & (meta_ref[0] == 0))
     def _():
         keys[:past] = own_past[0]
         keys[past:] = own_new[...]
-        values[...] = recv[...]
-
-    @pl.when((pl.program_id(2) == 0) & (parity_ref[0] != 0))
+        values[:past] = recv_past[...]
+        values[past:] = recv_new[...]
+
+    @pl.when((pl.program_id(1) == 0) & (meta_ref[0] != 0))
     def _():
         values[:past] = own_past[0]
         values[past:] = own_new[...]
-        keys[...] = recv[...]
+        keys[:past] = recv_past[...]
+        keys[past:] = recv_new[...]
 
     factor = math.log2(math.e) / math.sqrt(HEAD_SIZE)
-    length = length_ref[request + parity_ref[1]]
+    length = length_ref[meta_ref[1]]
     live = lax.broadcasted_iota(jnp.int32, (1, past), 1) < length
     bias = jnp.where(live, 0.0, neg_large)
     rows = row_tile * new
@@ -234,7 +245,7 @@
             out_ref[:, h * HEAD_SIZE : (h + 1) * HEAD_SIZE] = mixed[i * new : (i + 1) * new]
 
 
-def attend(request, lengths, parity, queries, cache, incoming, recv):
+def attend(request, lengths, parity, queries, cache, incoming, recv, recv_new):
     slots = recv.shape[1] // HEAD_SIZE
     heads = queries.shape[1] // HEAD_SIZE
     grouped = heads // slots
@@ -249,16 +260,17 @@
         out_shape=jax.ShapeDtypeStruct((NEW, heads * HEAD_SIZE), jnp.bfloat16),
         grid_spec=pltpu.PrefetchScalarGridSpec(
             num_scalar_prefetch=2,
-            grid=(1, slots, tiles),
+            grid=(slots, tiles),
             in_specs=[
-                pl.BlockSpec((NEW, width), lambda r, s, t, n, p: (request, s * tiles + t)),
+                pl.BlockSpec((NEW, width), lambda s, t, n, p: (request, s * tiles + t)),
                 pl.BlockSpec(
-                    (1, past, HEAD_SIZE), lambda r, s, t, n, p: (request, 0, slots * p[0] + s)
+                    (1, past, HEAD_SIZE), lambda s, t, n, p: (request, 0, slots * p[0] + s)
                 ),
-                pl.BlockSpec((NEW, HEAD_SIZE), lambda r, s, t, n, p: (request, slots * p[0] + s)),
-                pl.BlockSpec((whole, HEAD_SIZE), lambda r, s, t, n, p: (0, s)),
+                pl.BlockSpec((NEW, HEAD_SIZE), lambda s, t, n, p: (request, slots * p[0] + s)),
+                pl.BlockSpec((past, HEAD_SIZE), lambda s, t, n, p: (0, s)),
+                pl.BlockSpec((NEW, HEAD_SIZE), lambda s, t, n, p: (request, s)),
             ],
-            out_specs=pl.BlockSpec((NEW, width), lambda r, s, t, n, p: (0, s * tiles + t)),
+            out_specs=pl.BlockSpec((NEW, width), lambda s, t, n, p: (0, s * tiles + t)),
             scratch_shapes=[
                 pltpu.VMEM((whole, HEAD_SIZE), jnp.bfloat16),
                 pltpu.VMEM((whole, HEAD_SIZE), jnp.bfloat16),
@@ -271,7 +283,7 @@
             transcendentals=NEW * heads * whole,
         ),
         name="attend",
-    )(lengths, meta, queries, cache, incoming, recv)
+    )(lengths, meta, queries, cache, incoming, recv, recv_new)
 
 
 def from_others(block, axis):
@@ -304,11 +316,14 @@
     x = lax.axis_index("dp")
     core = lax.axis_index("pipe")
     send_at = (1 - parity) * half
-    outgoing = []
-    for r in range(requests):
-        a = lax.dynamic_slice(prefix_key_value_cache, (r, 0, send_at), (1, past, half))[0]
-        b = lax.dynamic_slice(incoming_key_value, (r * NEW, send_at), (NEW, half))
-        outgoing.append(jnp.concatenate([a, b], axis=0))
+    outgoing = [
+        lax.dynamic_slice(prefix_key_value_cache, (r, 0, send_at), (1, past, half))[0]
+        for r in range(requests)
+    ]
+    outgoing_new = lax.dynamic_slice(
+        incoming_key_value, (0, send_at), (incoming_key_value.shape[0], half)
+    )
+    arrived_new = partner(outgoing_new, "tensor", 0)
     arrived = [partner(block, "tensor", 0) for block in outgoing]
     weight_partner = partner(output_weight, "pipe", 0)
     down = adapter_down_weight.reshape(adapter_down_weight.shape[0], ADAPTER_COUNT * ADAPTER_RANK)
@@ -326,7 +341,14 @@
     state = []
     for r in range(requests):
         attended = attend(
-            r, prefix_length, parity, queries, prefix_key_value_cache, incoming_key_value, arrived[r]
+            r,
+            prefix_length,
+            parity,
+            queries,
+            prefix_key_value_cache,
+            incoming_key_value,
+            arrived[r],
+            arrived_new,
         )
         across = partner(attended, "dp", 0)
         flat = jnp.dot(attended, down, preferred_element_type=jnp.float32)
@@ -350,6 +372,8 @@
     hidden = []
     for r in range(requests):
         rank, keep_mine, keep_theirs, got_mine, got_theirs = state[r]
+        if r > 0:
+            got_mine, got_theirs, _ = lax.optimization_barrier((got_mine, got_theirs, got_first))
         theirs_pair = (keep_theirs.astype(jnp.float32) + got_theirs.astype(jnp.float32)).astype(
             jnp.bfloat16
         )
@@ -362,7 +386,12 @@
         )
         last_kept = jnp.where(x == upper, mine, theirs)
         last_sent = jnp.concatenate([jnp.where(x == upper, theirs, mine), rank_pair], axis=1)
-        last_got = partner(last_sent, "tensor", 1)
+        if r + 1 < requests:
+            got_first = partner(last_sent[:, : width // 2], "tensor", 1)
+            got_rest = partner(last_sent[:, width // 2 :], "tensor", 1)
+            last_got = jnp.concatenate([got_first, got_rest], axis=1)
+        else:
+            last_got = partner(last_sent, "tensor", 1)
         projected = last_kept.astype(jnp.float32) + last_got[:, :width].astype(jnp.float32)
         shrunk = (rank_pair.astype(jnp.float32) + last_got[:, width:].astype(jnp.float32)).astype(
             jnp.bfloat16

time: 169 us -> 163 us (0.964)
  waiting for transfers between devices: 75.5 us -> 68.2 us
  starting transfers between devices: 25.1 us -> 29 us
  matrix products: 21.3 us -> 18.3 us
  local copies, waits for them, and re-layouts: 4.97 us -> 7.62 us
  other arithmetic: 15.4 us -> 13.2 us
    ppermute x13 -> x15, waiting for transfers between devices: 71.9 us -> 64.7 us  [partner(): return lax.ppermute(block, axis, route)]
    ppermute x13 -> x15, starting transfers between devices: 21 us -> 24.7 us  [partner(): return lax.ppermute(block, axis, route)]
    dot_general x8, matrix products: 17 us -> 13.7 us  [product(): jnp.dot(rows, weight, preferred_element_type=jnp.float32)]
    concatenate x2 -> x0, other arithmetic: 2.17 us -> none  [shards_fast(): outgoing.append(jnp.concatenate([a, b], axis=0))]
  transfers between devices with their start and end apart: 16 -> 18, of which waited for: 12 -> 14; matrix products, arithmetic and copies ran while one was open for 22% -> 21% of each run, Pallas kernels for 12% -> 12%
where the time goes in v3:
time: 163 us; the launch traced here: 162 us
  waiting for transfers between devices  68.2 us (42%)
  starting transfers between devices  29 us (18%)
  Pallas kernels  20.1 us (12%)
  matrix products  18.3 us (11%)
  other arithmetic  13.2 us (8%)
  local copies, waits for them, and re-layouts  7.62 us (5%)
  between operations  6 us (4%)
    ppermute x15, waiting for transfers between devices, partner(): return lax.ppermute(block, axis, route)  64.7 us
    ppermute x15, starting transfers between devices, partner(): return lax.ppermute(block, axis, route)  24.7 us
    pallas_call x2, Pallas kernels, attend(): pl.pallas_call(functools.partial(attend_kernel, heads_tile), out_shape=ja...  20.1 us
    dot_general x8, matrix products, product(): jnp.dot(rows, weight, preferred_element_type=jnp.float32)  13.7 us
    select_n x1, other arithmetic, shards_fast(): weight_send = jnp.where(keep_own, weight_partner, output_weight)  9.04 us
    ppermute x3, starting transfers between devices, from_others(): lax.ppermute(block, axis, [(i, (i + shift) % count) for i in range(count)])  4.25 us
    dot_general x2, matrix products, shards_fast(): jnp.dot(shrunk[:, :ADAPTER_RANK], up, preferred_element_type=jnp.float32)  3.59 us
    ppermute x3, waiting for transfers between devices, from_others(): lax.ppermute(block, axis, [(i, (i + shift) % count) for i in range(count)])  3.56 us
  transfers between devices with their start and end apart: 18, of which 14 were waited for; matrix products, arithmetic and copies ran while one was open for 21% of the time, Pallas kernels for 12%

profile of v3, /device:TPU:0, one launch (start us, length us, event | category | flops | bytes accessed | tf_op | source)
XLA Modules:
  0.0 162.4 jit_solution(15777872662669573093)
XLA Ops:
  0.6 0.5 collective-permute-start
  1.2 3.0 %dynamic-slice_bitcast_fusion = (bf16[2048,256]{1,0:T(8,128)(2,1)}, bf16[2048,256]{1,0:T(8,128)(2,1)}) fusion(bf16[2,2048,512]{2,1,0:T(8,128)(2,1)} %own_past.3, s32[]{:T(128)S(6)} %select_n.66), kind=kLoop, calls=%fused_computation.22 | loop fusion | bytes 4194308 | tf_op jit(solution)/shard_map/squeeze | solution.py:320
  4.2 2.7 %collective-permute-start.1 = (bf16[2048,256]{1,0:T(8,128)(2,1)}, bf16[2048,256]{1,0:T(8,128)(2,1)S(1)}, u32[]{:S(2)}, u32[]{:S(2)}) collective-permute-start(bf16[2048,256]{1,0:T(8,128)(2,1)} %get-tuple-element.29), channel_id=1, source_target_pairs={{0,4},{4,0},{8,12},{12,8},{1,5},{5,1},{9,13},{13,9},{2,6},{6,2},{1... | collective-permute-start | bytes 3145736 | tf_op jit(solution)/shard_map/ppermute | solution.py:30
  6.8 0.9 constant_dynamic-slice_fusion
  7.8 0.1 collective-permute-start.2
  7.8 2.0 %collective-permute-start.3 = (bf16[2048,256]{1,0:T(8,128)(2,1)}, bf16[2048,256]{1,0:T(8,128)(2,1)S(1)}, u32[]{:S(2)}, u32[]{:S(2)}) collective-permute-start(bf16[2048,256]{1,0:T(8,128)(2,1)} %get-tuple-element.28), channel_id=1, source_target_pairs={{0,4},{4,0},{8,12},{12,8},{1,5},{5,1},{9,13},{13,9},{2,6},{6,2},{1... | collective-permute-start | bytes 3145736 | tf_op jit(solution)/shard_map/ppermute | solution.py:30
  9.8 1.4 fusion.19
  12.5 0.1 pad_add_fusion.meta_ref
  12.6 0.1 pad_add_fusion.1.meta_ref
  12.7 1.6 collective-permute-done
  14.3 9.0 %broadcast_select_fusion = (bf16[2048,2048]{1,0:T(8,128)(2,1)}, bf16[2048,2048]{1,0:T(8,128)(2,1)S(1)}) fusion(bf16[2048,2048]{1,0:T(8,128)(2,1)} %collective-permute-done, bf16[2048,2048]{1,0:T(8,128)(2,1)} %param.15, pred[]{:T(512)S(6)} %eq.12), kind=kLoop, calls=%fused_computation | loop fusion | flops 8388608 | bytes 33554432 | tf_op jit(solution)/shard_map/jit(_where)/select_n | solution.py:333
  23.3 7.7 %collective-permute-done.1.recv_past = bf16[2048,256]{1,0:T(8,128)(2,1)S(1)} collective-permute-done((bf16[2048,256]{1,0:T(8,128)(2,1)}, bf16[2048,256]{1,0:T(8,128)(2,1)S(1)}, u32[]{:S(2)}, u32[]{:S(2)}) %collective-permute-start.1) | collective-permute-done | bytes 1048608 | tf_op jit(solution)/shard_map/ppermute | solution.py:30
  31.1 2.8 %collective-permute-done.2.recv_new = bf16[256,256]{1,0:T(8,128)(2,1)S(1)} collective-permute-done((bf16[256,256]{1,0:T(8,128)(2,1)S(1)}, bf16[256,256]{1,0:T(8,128)(2,1)S(1)}, u32[]{:S(2)}, u32[]{:S(2)}) %collective-permute-start.2) | collective-permute-done | bytes 131104 | tf_op jit(solution)/shard_map/ppermute | solution.py:30
  33.9 10.0 %attend.2 = bf16[128,2048]{1,0:T(8,128)(2,1)S(1)} custom-call(s32[2]{0:T(128)S(1)} %copy-done.4, s32[2]{0:T(128)S(1)} %pad_add_fusion.meta_ref, bf16[256,2048]{1,0:T(8,128)(2,1)S(1)} %copy-done.3, bf16[2,2048,512]{2,1,0:T(8,128)(2,1)S(1)} %copy-done.1, bf16[256,512]{1,0:T(8,128)(2,1)S(1)} %copy-done.2, ...), custom_call_target="tpu_custom_call" | custom-call | flops 2281701376 | bytes 3276800 | tf_op jit(solution)/shard_map/attend/pallas_call | solution.py:258
  43.9 1.9 %collective-permute-start.4 = (bf16[128,2048]{1,0:T(8,128)(2,1)S(1)}, bf16[128,2048]{1,0:T(8,128)(2,1)S(1)}, u32[]{:S(2)}, u32[]{:S(2)}) collective-permute-start(bf16[128,2048]{1,0:T(8,128)(2,1)S(1)} %attend.2), channel_id=1, source_target_pairs={{0,2},{2,0},{1,3},{3,1},{4,6},{6,4},{5,7},{7,5},{8,10},{10,8},{9,1... | collective-permute-start | bytes 1572872 | tf_op jit(solution)/shard_map/ppermute | solution.py:30
  45.8 4.7 %convolution_convert_fusion.4 = bf16[128,2048]{1,0:T(8,128)(2,1)S(1)} fusion(bf16[128,2048]{1,0:T(8,128)(2,1)S(1)} %attend.2, bf16[2048,2048]{1,0:T(8,128)(2,1)} %get-tuple-element.15), kind=kOutput, calls=%fused_computation.8 | convolution fusion | flops 1074003968 | bytes 9437184 | tf_op jit(solution)/shard_map/dot_general | solution.py:339
  50.5 0.5 fusion.20
  51.0 0.1 dynamic-slice_convert_fusion.1
  51.2 1.6 %collective-permute-start.5 = (bf16[128,2176]{1,0:T(8,128)(2,1)S(1)}, bf16[128,2176]{1,0:T(8,128)(2,1)S(1)}, u32[]{:S(2)}, u32[]{:S(2)}) collective-permute-start(bf16[128,2176]{1,0:T(8,128)(2,1)S(1)} %pad_maximum_fusion.1), channel_id=1, source_target_pairs={{0,4},{4,0},{8,12},{12,8},{1,5},{5,1},{9,13},{13,9},{2,6},{6,2},{1... | collective-permute-start | bytes 1671176 | tf_op jit(solution)/shard_map/ppermute | solution.py:30
  52.8 1.3 convolution_convert_fusion.7
  54.1 3.2 %collective-permute-done.4 = bf16[128,2048]{1,0:T(8,128)(2,1)S(1)} collective-permute-done((bf16[128,2048]{1,0:T(8,128)(2,1)S(1)}, bf16[128,2048]{1,0:T(8,128)(2,1)S(1)}, u32[]{:S(2)}, u32[]{:S(2)}) %collective-permute-start.4) | collective-permute-done | bytes 524320 | tf_op jit(solution)/shard_map/ppermute | solution.py:30
  57.3 1.3 convolution_convert_fusion.6
  58.6 1.7 %collective-permute-start.6 = (bf16[128,2048]{1,0:T(8,128)(2,1)S(1)}, bf16[128,2048]{1,0:T(8,128)(2,1)S(1)}, u32[]{:S(2)}, u32[]{:S(2)}) collective-permute-start(bf16[128,2048]{1,0:T(8,128)(2,1)S(1)} %convolution_convert_fusion.6), channel_id=1, source_target_pairs={{0,4},{4,0},{8,12},{12,8},{1,5},{5,1},{9,13},{13,9},{2,6},{6,2},{1... | collective-permute-start | bytes 1572872 | tf_op jit(solution)/shard_map/ppermute | solution.py:30
  60.3 10.1 %attend.3 = bf16[128,2048]{1,0:T(8,128)(2,1)S(1)} custom-call(s32[2]{0:T(128)S(1)} %copy-done.4, s32[2]{0:T(128)S(1)} %pad_add_fusion.1.meta_ref, bf16[256,2048]{1,0:T(8,128)(2,1)S(1)} %copy-done.3, bf16[2,2048,512]{2,1,0:T(8,128)(2,1)S(1)} %copy-done.1, bf16[256,512]{1,0:T(8,128)(2,1)S(1)} %copy-done.2, ...), custom_call_target="tpu_custom_call" | custom-call | flops 2281701376 | bytes 3276800 | tf_op jit(solution)/shard_map/attend/pallas_call | solution.py:258
  70.4 1.6 collective-permute-start.10
  72.0 1.3 convolution_convert_fusion.3
  73.3 1.3 convolution_convert_fusion.1
  74.6 1.3 convolution_convert_fusion.5
  75.9 0.5 fusion.21
  76.4 0.1 dynamic-slice_convert_fusion
  76.6 0.5 collective-permute-start.11
  77.1 2.4 %collective-permute-done.6 = bf16[128,2048]{1,0:T(8,128)(2,1)S(1)} collective-permute-done((bf16[128,2048]{1,0:T(8,128)(2,1)S(1)}, bf16[128,2048]{1,0:T(8,128)(2,1)S(1)}, u32[]{:S(2)}, u32[]{:S(2)}) %collective-permute-start.6) | collective-permute-done | bytes 524320 | tf_op jit(solution)/shard_map/ppermute | solution.py:30
  79.5 0.1 add_convert_fusion.4
  79.6 1.9 %collective-permute-start.7 = (bf16[128,2048]{1,0:T(8,128)(2,1)S(1)}, bf16[128,2048]{1,0:T(8,128)(2,1)S(1)}, u32[]{:S(2)}, u32[]{:S(2)}) collective-permute-start(bf16[128,2048]{1,0:T(8,128)(2,1)S(1)} %add_convert_fusion.4), channel_id=1, source_target_pairs={{0,2},{2,0},{1,3},{3,1},{4,6},{6,4},{5,7},{7,5},{8,10},{10,8},{9,1... | collective-permute-start | bytes 1572872 | tf_op jit(solution)/shard_map/ppermute | solution.py:30
  81.6 1.1 collective-permute-done.10
  82.7 1.3 convolution_convert_fusion
  84.1 0.5 collective-permute-start.12
  84.6 9.0 %collective-permute-done.7 = bf16[128,2048]{1,0:T(8,128)(2,1)S(1)} collective-permute-done((bf16[128,2048]{1,0:T(8,128)(2,1)S(1)}, bf16[128,2048]{1,0:T(8,128)(2,1)S(1)}, u32[]{:S(2)}, u32[]{:S(2)}) %collective-permute-start.7) | collective-permute-done | bytes 524320 | tf_op jit(solution)/shard_map/ppermute | solution.py:30
  93.5 0.2 broadcast_select_fusion.3
  93.8 0.5 copy-done.7
  94.4 2.6 %collective-permute-start.8 = (bf16[128,1024]{1,0:T(8,128)(2,1)S(1)}, bf16[128,1024]{1,0:T(8,128)(2,1)}, u32[]{:S(2)}, u32[]{:S(2)}) collective-permute-start(bf16[128,1024]{1,0:T(8,128)(2,1)S(1)} %slice.67), channel_id=1, source_target_pairs={{0,8},{8,0},{4,12},{12,4},{1,9},{9,1},{5,13},{13,5},{2,10},{10,2},... | collective-permute-start | bytes 786440 | tf_op jit(solution)/shard_map/ppermute | solution.py:30
  96.9 1.3 convolution_convert_fusion.2
  98.2 9.8 %collective-permute-done.12 = bf16[128,2048]{1,0:T(8,128)(2,1)S(1)} collective-permute-done((bf16[128,2048]{1,0:T(8,128)(2,1)S(1)}, bf16[128,2048]{1,0:T(8,128)(2,1)S(1)}, u32[]{:S(2)}, u32[]{:S(2)}) %collective-permute-start.12) | collective-permute-done | bytes 524320 | tf_op jit(solution)/shard_map/ppermute | solution.py:30
  108.0 0.1 add_convert_fusion.1
  108.1 1.8 %collective-permute-start.13 = (bf16[128,2048]{1,0:T(8,128)(2,1)S(1)}, bf16[128,2048]{1,0:T(8,128)(2,1)S(1)}, u32[]{:S(2)}, u32[]{:S(2)}) collective-permute-start(bf16[128,2048]{1,0:T(8,128)(2,1)S(1)} %add_convert_fusion.1), channel_id=1, source_target_pairs={{0,2},{2,0},{1,3},{3,1},{4,6},{6,4},{5,7},{7,5},{8,10},{10,8},{9,1... | collective-permute-start | bytes 1572872 | tf_op jit(solution)/shard_map/ppermute | solution.py:30
  109.9 0.7 pad_maximum_fusion.5
  110.7 2.6 %collective-permute-start.9 = (bf16[128,1152]{1,0:T(8,128)(2,1)}, bf16[128,1152]{1,0:T(8,128)(2,1)}, u32[]{:S(2)}, u32[]{:S(2)}) collective-permute-start(bf16[128,1152]{1,0:T(8,128)(2,1)} %pad_maximum_fusion.5), channel_id=1, source_target_pairs={{0,8},{8,0},{4,12},{12,4},{1,9},{9,1},{5,13},{13,5},{2,10},{10,2},... | collective-permute-start | bytes 884744 | tf_op jit(solution)/shard_map/ppermute | solution.py:30
  113.3 8.4 %collective-permute-done.13 = bf16[128,2048]{1,0:T(8,128)(2,1)S(1)} collective-permute-done((bf16[128,2048]{1,0:T(8,128)(2,1)S(1)}, bf16[128,2048]{1,0:T(8,128)(2,1)S(1)}, u32[]{:S(2)}, u32[]{:S(2)}) %collective-permute-start.13) | collective-permute-done | bytes 524320 | tf_op jit(solution)/shard_map/ppermute | solution.py:30
  121.6 0.2 broadcast_select_fusion.2
  121.8 0.9 pad_maximum_fusion.3
  122.7 2.8 %collective-permute-start.14 = (bf16[128,2176]{1,0:T(8,128)(2,1)}, bf16[128,2176]{1,0:T(8,128)(2,1)}, u32[]{:S(2)}, u32[]{:S(2)}) collective-permute-start(bf16[128,2176]{1,0:T(8,128)(2,1)} %pad_maximum_fusion.3), channel_id=1, source_target_pairs={{0,8},{8,0},{4,12},{12,4},{1,9},{9,1},{5,13},{13,5},{2,10},{10,2},... | collective-permute-start | bytes 1671176 | tf_op jit(solution)/shard_map/ppermute | solution.py:30
  129.3 10.1 %collective-permute-done.9 = bf16[128,1152]{1,0:T(8,128)(2,1)} collective-permute-done((bf16[128,1152]{1,0:T(8,128)(2,1)}, bf16[128,1152]{1,0:T(8,128)(2,1)}, u32[]{:S(2)}, u32[]{:S(2)}) %collective-permute-start.9) | collective-permute-done | bytes 294944 | tf_op jit(solution)/shard_map/ppermute | solution.py:30
  139.4 0.8 slice.69
  140.1 1.7 %add_convert_fusion.3 = bf16[128,2048]{1,0:T(8,128)(2,1)S(1)} fusion(bf16[128,1152]{1,0:T(8,128)(2,1)} %collective-permute-done.9, bf16[128,1024]{1,0:T(8,128)(2,1)} %collective-permute-done.8, bf16[128,2048]{1,0:T(8,128)(2,1)} %copy-done.7, bf16[256,2048]{1,0:T(8,128)(2,1)} %param.18, pred[]{:T(512)S(6)} %eq.6, bf16[4,64,2048]{2,1,0:T(8,128)(2,1)} %param.17, ...), kind=kOutput, calls=%fused_computation.19 | convolution fusion | flops 37519360 | bytes 3506181 | tf_op jit(solution)/shard_map/dot_general | solution.py:402
  141.9 8.5 %collective-permute-done.14 = bf16[128,2176]{1,0:T(8,128)(2,1)} collective-permute-done((bf16[128,2176]{1,0:T(8,128)(2,1)}, bf16[128,2176]{1,0:T(8,128)(2,1)}, u32[]{:S(2)}, u32[]{:S(2)}) %collective-permute-start.14) | collective-permute-done | bytes 557088 | tf_op jit(solution)/shard_map/ppermute | solution.py:30
  150.3 0.8 slice.73
  151.1 1.9 %add_convert_fusion = bf16[128,2048]{1,0:T(8,128)(2,1)S(1)} fusion(bf16[128,2176]{1,0:T(8,128)(2,1)} %collective-permute-done.14, bf16[128,2048]{1,0:T(8,128)(2,1)} %copy-done.8, bf16[256,2048]{1,0:T(8,128)(2,1)} %param.18, pred[]{:T(512)S(6)} %eq.6, bf16[4,64,2048]{2,1,0:T(8,128)(2,1)} %param.17, s32[]{:T(128)S(6)} %select_n.74, ...), kind=kOutput, calls=%fused_computation.16 | convolution fusion | flops 36732928 | bytes 3473413 | tf_op jit(solution)/shard_map/dot_general | solution.py:402
  153.0 0.3 fusion
  153.3 0.7 collective-permute-start.15
  154.0 3.5 %collective-permute-start.16 = (f32[256]{0:T(256)S(1)}, f32[256]{0:T(256)S(1)}, u32[]{:S(2)}, u32[]{:S(2)}) collective-permute-start(f32[256]{0:T(256)S(1)} %get-tuple-element.24), channel_id=1, source_target_pairs={{0,8},{4,12},{8,0},{12,4},{1,9},{5,13},{9,1},{13,5},{2,10},{6,14},... | collective-permute-start | bytes 3080 | tf_op jit(solution)/shard_map/ppermute | solution.py:292
  157.5 1.2 collective-permute-done.15
  158.7 0.4 collective-permute-done.16
  159.1 2.0 %collective-permute-done.17 = f32[256]{0:T(256)S(1)} collective-permute-done((f32[256]{0:T(256)S(1)}, f32[256]{0:T(256)S(1)}, u32[]{:S(2)}, u32[]{:S(2)}) %collective-permute-start.17) | collective-permute-done | bytes 1056 | tf_op jit(solution)/shard_map/ppermute | solution.py:292
  161.1 1.3 fusion.2
  (43 shorter events, 0.2 us)
Async XLA Ops:
  0.6 49.8 %copy-start = (bf16[2048,4,64]{0,2,1:T(8,128)(2,1)S(1)}, bf16[2048,4,64]{0,2,1:T(8,128)(2,1)}, u32[]{:S(2)}) copy-start(bf16[2048,4,64]{0,2,1:T(8,128)(2,1)} %param.16) | copy-start | bytes 3145732
  0.6 13.6 %collective-permute-start = (bf16[2048,2048]{1,0:T(8,128)(2,1)}, bf16[2048,2048]{1,0:T(8,128)(2,1)}, u32[]{:S(2)}, u32[]{:S(2)}) collective-permute-start(bf16[2048,2048]{1,0:T(8,128)(2,1)} %param.15), channel_id=1, source_target_pairs={{0,1},{1,0},{2,3},{3,2},{4,5},{5,4},{6,7},{7,6},{8,9},{9,8},{10,11... | collective-permute-start | bytes 25165832 | tf_op jit(solution)/shard_map/ppermute | solution.py:30
  4.2 26.9 %collective-permute-start.1 = (bf16[2048,256]{1,0:T(8,128)(2,1)}, bf16[2048,256]{1,0:T(8,128)(2,1)S(1)}, u32[]{:S(2)}, u32[]{:S(2)}) collective-permute-start(bf16[2048,256]{1,0:T(8,128)(2,1)} %get-tuple-element.29), channel_id=1, source_target_pairs={{0,4},{4,0},{8,12},{12,8},{1,5},{5,1},{9,13},{13,9},{2,6},{6,2},{1... | collective-permute-start | bytes 3145736 | tf_op jit(solution)/shard_map/ppermute | solution.py:30
  7.8 26.1 %collective-permute-start.2 = (bf16[256,256]{1,0:T(8,128)(2,1)S(1)}, bf16[256,256]{1,0:T(8,128)(2,1)S(1)}, u32[]{:S(2)}, u32[]{:S(2)}) collective-permute-start(bf16[256,256]{1,0:T(8,128)(2,1)S(1)} %constant_dynamic-slice_fusion), channel_id=1, source_target_pairs={{0,4},{4,0},{8,12},{12,8},{1,5},{5,1},{9,13},{13,9},{2,6},{6,2},{1... | collective-permute-start | bytes 393224 | tf_op jit(solution)/shard_map/ppermute | solution.py:30
  7.8 52.5 %collective-permute-start.3 = (bf16[2048,256]{1,0:T(8,128)(2,1)}, bf16[2048,256]{1,0:T(8,128)(2,1)S(1)}, u32[]{:S(2)}, u32[]{:S(2)}) collective-permute-start(bf16[2048,256]{1,0:T(8,128)(2,1)} %get-tuple-element.28), channel_id=1, source_target_pairs={{0,4},{4,0},{8,12},{12,8},{1,5},{5,1},{9,13},{13,9},{2,6},{6,2},{1... | collective-permute-start | bytes 3145736 | tf_op jit(solution)/shard_map/ppermute | solution.py:30
  12.7 21.2 %copy-start.1 = (bf16[2,2048,512]{2,1,0:T(8,128)(2,1)S(1)}, bf16[2,2048,512]{2,1,0:T(8,128)(2,1)}, u32[]{:S(2)}) copy-start(bf16[2,2048,512]{2,1,0:T(8,128)(2,1)} %own_past.3) | copy-start | bytes 12582916
  12.7 21.2 %copy-start.2 = (bf16[256,512]{1,0:T(8,128)(2,1)S(1)}, bf16[256,512]{1,0:T(8,128)(2,1)}, u32[]{:S(2)}) copy-start(bf16[256,512]{1,0:T(8,128)(2,1)} %own_new.3) | copy-start | bytes 786436
  12.7 21.2 %copy-start.3 = (bf16[256,2048]{1,0:T(8,128)(2,1)S(1)}, bf16[256,2048]{1,0:T(8,128)(2,1)}, u32[]{:S(2)}) copy-start(bf16[256,2048]{1,0:T(8,128)(2,1)} %q_ref.3) | copy-start | bytes 3145732
  12.7 21.2 %copy-start.4 = (s32[2]{0:T(128)S(1)}, s32[2]{0:T(128)}, u32[]{:S(2)}) copy-start(s32[2]{0:T(128)} %length_ref.3) | copy-start | bytes 28
  43.9 13.4 %collective-permute-start.4 = (bf16[128,2048]{1,0:T(8,128)(2,1)S(1)}, bf16[128,2048]{1,0:T(8,128)(2,1)S(1)}, u32[]{:S(2)}, u32[]{:S(2)}) collective-permute-start(bf16[128,2048]{1,0:T(8,128)(2,1)S(1)} %attend.2), channel_id=1, source_target_pairs={{0,2},{2,0},{1,3},{3,1},{4,6},{6,4},{5,7},{7,5},{8,10},{10,8},{9,1... | collective-permute-start | bytes 1572872 | tf_op jit(solution)/shard_map/ppermute | solution.py:30
  51.1 6.2 %slice-start = ((s8[8388608]{0:T(1024)(128)(4,1)}), s8[4194304]{0:T(1024)(128)(4,1)S(1)}, s32[]{:S(2)}) async-start(s8[8388608]{0:T(1024)(128)(4,1)} %bitcast.40), calls=%async_computation | async-start | bytes 8388608
  51.2 6.1 %slice-start.1 = ((s8[8388608]{0:T(1024)(128)(4,1)}), s8[4194304]{0:T(1024)(128)(4,1)S(1)}, s32[]{:S(2)}) async-start(s8[8388608]{0:T(1024)(128)(4,1)} %bitcast.40), calls=%async_computation.1 | async-start | bytes 8388608
  51.2 33.4 %collective-permute-start.5 = (bf16[128,2176]{1,0:T(8,128)(2,1)S(1)}, bf16[128,2176]{1,0:T(8,128)(2,1)S(1)}, u32[]{:S(2)}, u32[]{:S(2)}) collective-permute-start(bf16[128,2176]{1,0:T(8,128)(2,1)S(1)} %pad_maximum_fusion.1), channel_id=1, source_target_pairs={{0,4},{4,0},{8,12},{12,8},{1,5},{5,1},{9,13},{13,9},{2,6},{6,2},{1... | collective-permute-start | bytes 1671176 | tf_op jit(solution)/shard_map/ppermute | solution.py:30
  58.6 20.9 %collective-permute-start.6 = (bf16[128,2048]{1,0:T(8,128)(2,1)S(1)}, bf16[128,2048]{1,0:T(8,128)(2,1)S(1)}, u32[]{:S(2)}, u32[]{:S(2)}) collective-permute-start(bf16[128,2048]{1,0:T(8,128)(2,1)S(1)} %convolution_convert_fusion.6), channel_id=1, source_target_pairs={{0,4},{4,0},{8,12},{12,8},{1,5},{5,1},{9,13},{13,9},{2,6},{6,2},{1... | collective-permute-start | bytes 1572872 | tf_op jit(solution)/shard_map/ppermute | solution.py:30
  60.3 13.0 %slice-start.2 = ((s8[8388608]{0:T(1024)(128)(4,1)}), s8[4194304]{0:T(1024)(128)(4,1)S(1)}, s32[]{:S(2)}) async-start(s8[8388608]{0:T(1024)(128)(4,1)} %bitcast.42), calls=%async_computation.2 | async-start | bytes 8388608
  70.4 2.9 %slice-start.3 = ((s8[8388608]{0:T(1024)(128)(4,1)}), s8[4194304]{0:T(1024)(128)(4,1)S(1)}, s32[]{:S(2)}) async-start(s8[8388608]{0:T(1024)(128)(4,1)} %bitcast.42), calls=%async_computation.3 | async-start | bytes 8388608
  70.4 12.3 %collective-permute-start.10 = (bf16[128,2048]{1,0:T(8,128)(2,1)S(1)}, bf16[128,2048]{1,0:T(8,128)(2,1)S(1)}, u32[]{:S(2)}, u32[]{:S(2)}) collective-permute-start(bf16[128,2048]{1,0:T(8,128)(2,1)S(1)} %attend.3), channel_id=1, source_target_pairs={{0,2},{2,0},{1,3},{3,1},{4,6},{6,4},{5,7},{7,5},{8,10},{10,8},{9,1... | collective-permute-start | bytes 1572872 | tf_op jit(solution)/shard_map/ppermute | solution.py:30
  76.6 21.6 %collective-permute-start.11 = (bf16[128,2176]{1,0:T(8,128)(2,1)S(1)}, bf16[128,2176]{1,0:T(8,128)(2,1)S(1)}, u32[]{:S(2)}, u32[]{:S(2)}) collective-permute-start(bf16[128,2176]{1,0:T(8,128)(2,1)S(1)} %pad_maximum_fusion.2), channel_id=1, source_target_pairs={{0,4},{4,0},{8,12},{12,8},{1,5},{5,1},{9,13},{13,9},{2,6},{6,2},{1... | collective-permute-start | bytes 1671176 | tf_op jit(solution)/shard_map/ppermute | solution.py:30
  79.6 13.9 %collective-permute-start.7 = (bf16[128,2048]{1,0:T(8,128)(2,1)S(1)}, bf16[128,2048]{1,0:T(8,128)(2,1)S(1)}, u32[]{:S(2)}, u32[]{:S(2)}) collective-permute-start(bf16[128,2048]{1,0:T(8,128)(2,1)S(1)} %add_convert_fusion.4), channel_id=1, source_target_pairs={{0,2},{2,0},{1,3},{3,1},{4,6},{6,4},{5,7},{7,5},{8,10},{10,8},{9,1... | collective-permute-start | bytes 1572872 | tf_op jit(solution)/shard_map/ppermute | solution.py:30
  84.1 24.0 %collective-permute-start.12 = (bf16[128,2048]{1,0:T(8,128)(2,1)S(1)}, bf16[128,2048]{1,0:T(8,128)(2,1)S(1)}, u32[]{:S(2)}, u32[]{:S(2)}) collective-permute-start(bf16[128,2048]{1,0:T(8,128)(2,1)S(1)} %convolution_convert_fusion), channel_id=1, source_target_pairs={{0,4},{4,0},{8,12},{12,8},{1,5},{5,1},{9,13},{13,9},{2,6},{6,2},{1... | collective-permute-start | bytes 1572872 | tf_op jit(solution)/shard_map/ppermute | solution.py:30
  93.5 0.8 copy-start.7
  94.4 13.7 %collective-permute-start.8 = (bf16[128,1024]{1,0:T(8,128)(2,1)S(1)}, bf16[128,1024]{1,0:T(8,128)(2,1)}, u32[]{:S(2)}, u32[]{:S(2)}) collective-permute-start(bf16[128,1024]{1,0:T(8,128)(2,1)S(1)} %slice.67), channel_id=1, source_target_pairs={{0,8},{8,0},{4,12},{12,4},{1,9},{9,1},{5,13},{13,5},{2,10},{10,2},... | collective-permute-start | bytes 786440 | tf_op jit(solution)/shard_map/ppermute | solution.py:30
  98.2 59.3 %copy-start.9 = (bf16[2048]{0:T(1024)(128)(2,1)S(1)}, bf16[2048]{0:T(1024)(128)(2,1)}, u32[]{:S(2)}) copy-start(bf16[2048]{0:T(1024)(128)(2,1)} %param.19) | copy-start | bytes 12292
  98.2 24.5 %copy-start.6 = (bf16[128,2176]{1,0:T(8,128)(2,1)}, bf16[128,2176]{1,0:T(8,128)(2,1)S(1)}, u32[]{:S(2)}) copy-start(bf16[128,2176]{1,0:T(8,128)(2,1)S(1)} %collective-permute-done.11) | copy-start | bytes 1671172
  108.1 13.5 %collective-permute-start.13 = (bf16[128,2048]{1,0:T(8,128)(2,1)S(1)}, bf16[128,2048]{1,0:T(8,128)(2,1)S(1)}, u32[]{:S(2)}, u32[]{:S(2)}) collective-permute-start(bf16[128,2048]{1,0:T(8,128)(2,1)S(1)} %add_convert_fusion.1), channel_id=1, source_target_pairs={{0,2},{2,0},{1,3},{3,1},{4,6},{6,4},{5,7},{7,5},{8,10},{10,8},{9,1... | collective-permute-start | bytes 1572872 | tf_op jit(solution)/shard_map/ppermute | solution.py:30
  110.7 28.7 %collective-permute-start.9 = (bf16[128,1152]{1,0:T(8,128)(2,1)}, bf16[128,1152]{1,0:T(8,128)(2,1)}, u32[]{:S(2)}, u32[]{:S(2)}) collective-permute-start(bf16[128,1152]{1,0:T(8,128)(2,1)} %pad_maximum_fusion.5), channel_id=1, source_target_pairs={{0,8},{8,0},{4,12},{12,4},{1,9},{9,1},{5,13},{13,5},{2,10},{10,2},... | collective-permute-start | bytes 884744 | tf_op jit(solution)/shard_map/ppermute | solution.py:30
  121.6 1.1 copy-start.8
  122.7 27.6 %collective-permute-start.14 = (bf16[128,2176]{1,0:T(8,128)(2,1)}, bf16[128,2176]{1,0:T(8,128)(2,1)}, u32[]{:S(2)}, u32[]{:S(2)}) collective-permute-start(bf16[128,2176]{1,0:T(8,128)(2,1)} %pad_maximum_fusion.3), channel_id=1, source_target_pairs={{0,8},{8,0},{4,12},{12,4},{1,9},{9,1},{5,13},{13,5},{2,10},{10,2},... | collective-permute-start | bytes 1671176 | tf_op jit(solution)/shard_map/ppermute | solution.py:30
  153.3 9.1 %copy-start.5 = (bf16[256,2048]{1,0:T(8,128)(2,1)}, bf16[256,2048]{1,0:T(8,128)(2,1)S(1)}, u32[]{:S(2)}) copy-start(bf16[256,2048]{1,0:T(8,128)(2,1)S(1)} %get-tuple-element.25) | copy-start | bytes 3145732
  153.3 5.4 %collective-permute-start.15 = (f32[256]{0:T(256)S(1)}, f32[256]{0:T(256)S(1)}, u32[]{:S(2)}, u32[]{:S(2)}) collective-permute-start(f32[256]{0:T(256)S(1)} %get-tuple-element.24), channel_id=1, source_target_pairs={{0,4},{4,8},{8,12},{12,0},{1,5},{5,9},{9,13},{13,1},{2,6},{6,10},{... | collective-permute-start | bytes 3080 | tf_op jit(solution)/shard_map/ppermute | solution.py:292
  154.0 5.1 %collective-permute-start.16 = (f32[256]{0:T(256)S(1)}, f32[256]{0:T(256)S(1)}, u32[]{:S(2)}, u32[]{:S(2)}) collective-permute-start(f32[256]{0:T(256)S(1)} %get-tuple-element.24), channel_id=1, source_target_pairs={{0,8},{4,12},{8,0},{12,4},{1,9},{5,13},{9,1},{13,5},{2,10},{6,14},... | collective-permute-start | bytes 3080 | tf_op jit(solution)/shard_map/ppermute | solution.py:292
  157.5 3.6 %collective-permute-start.17 = (f32[256]{0:T(256)S(1)}, f32[256]{0:T(256)S(1)}, u32[]{:S(2)}, u32[]{:S(2)}) collective-permute-start(f32[256]{0:T(256)S(1)} %get-tuple-element.24), channel_id=1, source_target_pairs={{0,12},{4,0},{8,4},{12,8},{1,13},{5,1},{9,5},{13,9},{2,14},{6,2},{... | collective-permute-start | bytes 3080 | tf_op jit(solution)/shard_map/ppermute | solution.py:292

commit v4 on v3

--- a/solution.py
+++ b/solution.py
@@ -338,6 +338,7 @@
     def product(rows, weight):
         return jnp.dot(rows, weight, preferred_element_type=jnp.float32).astype(jnp.bfloat16)
 
+    cuts = [slice(0, width // 2), slice(width // 2, width)]
     state = []
     for r in range(requests):
         attended = attend(
@@ -360,48 +361,55 @@
         got_mine = partner(payload, "tensor", 0)
         keep_mine = product(attended, weight_keep)
         sent_theirs = product(across, weight_send)
+        sent_theirs = [sent_theirs[:, cut] for cut in cuts]
         if r + 1 < requests:
             keep_mine, arrived[r + 1], _ = lax.optimization_barrier(
                 (keep_mine, arrived[r + 1], sent_theirs)
             )
-        got_theirs = partner(sent_theirs, "tensor", 0)
+        got_theirs = [partner(block, "tensor", 0) for block in sent_theirs]
         keep_theirs = product(across, weight_keep)
         keep_mine, keep_theirs = lax.optimization_barrier((keep_mine, keep_theirs))
         state.append((rank, keep_mine, keep_theirs, got_mine, got_theirs))
 
+    def pair_sum(kept, got):
+        return (kept.astype(jnp.float32) + got.astype(jnp.float32)).astype(jnp.bfloat16)
+
     hidden = []
+    before = None
     for r in range(requests):
         rank, keep_mine, keep_theirs, got_mine, got_theirs = state[r]
-        if r > 0:
-            got_mine, got_theirs, _ = lax.optimization_barrier((got_mine, got_theirs, got_first))
-        theirs_pair = (keep_theirs.astype(jnp.float32) + got_theirs.astype(jnp.float32)).astype(
-            jnp.bfloat16
-        )
-        theirs = partner(theirs_pair, "dp", 0)
-        mine = (keep_mine.astype(jnp.float32) + got_mine[:, :width].astype(jnp.float32)).astype(
-            jnp.bfloat16
-        )
-        rank_pair = (rank.astype(jnp.float32) + got_mine[:, width:].astype(jnp.float32)).astype(
-            jnp.bfloat16
-        )
-        last_kept = jnp.where(x == upper, mine, theirs)
-        last_sent = jnp.concatenate([jnp.where(x == upper, theirs, mine), rank_pair], axis=1)
-        if r + 1 < requests:
-            got_first = partner(last_sent[:, : width // 2], "tensor", 1)
-            got_rest = partner(last_sent[:, width // 2 :], "tensor", 1)
-            last_got = jnp.concatenate([got_first, got_rest], axis=1)
-        else:
-            last_got = partner(last_sent, "tensor", 1)
-        projected = last_kept.astype(jnp.float32) + last_got[:, :width].astype(jnp.float32)
-        shrunk = (rank_pair.astype(jnp.float32) + last_got[:, width:].astype(jnp.float32)).astype(
-            jnp.bfloat16
-        )
+        if before is not None:
+            got_mine, got_theirs[0], _ = lax.optimization_barrier(
+                (got_mine, got_theirs[0], (before[0], payload))
+            )
+            got_theirs[1], _ = lax.optimization_barrier((got_theirs[1], before[1]))
+        rank_pair = pair_sum(rank, got_mine[:, width:])
+        kept, before = [], []
+        for i, cut in enumerate(cuts):
+            if i > 0:
+                got_theirs[i], _ = lax.optimization_barrier((got_theirs[i], crossing))
+            crossing = pair_sum(keep_theirs[:, cut], got_theirs[i])
+            theirs = partner(crossing, "dp", 0)
+            if i > 0:
+                theirs, _ = lax.optimization_barrier((theirs, payload))
+            mine = pair_sum(keep_mine[:, cut], got_mine[:, cut])
+            kept.append(jnp.where(x == upper, mine, theirs))
+            payload = jnp.where(x == upper, theirs, mine)
+            if i == 0:
+                payload = jnp.concatenate([payload, rank_pair], axis=1)
+            before.append(partner(payload, "tensor", 1))
+        shrunk = pair_sum(rank_pair, before[0][:, width // 2 :])[:, :ADAPTER_RANK]
         up = lax.dynamic_slice(
             adapter_up_weight, (adapter[r], 0, 0), (1, ADAPTER_RANK, width)
         )[0]
-        adapter_output = jnp.dot(shrunk[:, :ADAPTER_RANK], up, preferred_element_type=jnp.float32)
-        rows = residual[r * NEW : (r + 1) * NEW].astype(jnp.float32)
-        hidden.append((rows + projected + adapter_output).astype(jnp.bfloat16))
+        pieces = []
+        for i, cut in enumerate(cuts):
+            got = before[i][:, : width // 2].astype(jnp.float32)
+            projected = kept[i].astype(jnp.float32) + got
+            adapter_output = jnp.dot(shrunk, up[:, cut], preferred_element_type=jnp.float32)
+            rows = residual[r * NEW : (r + 1) * NEW, cut].astype(jnp.float32)
+            pieces.append((rows + projected + adapter_output).astype(jnp.bfloat16))
+        hidden.append(jnp.concatenate(pieces, axis=1))
     hidden = jnp.concatenate(hidden, axis=0)
     widened = hidden.astype(jnp.float32)
     own_squares = jnp.sum(widened * widened, axis=1)

time: 163 us -> 157 us (0.963)
  waiting for transfers between devices: 68.2 us -> 56.7 us
  starting transfers between devices: 29 us -> 36.1 us
  matrix products: 18.3 us -> 15.9 us
    ppermute x15 -> x20, waiting for transfers between devices: 64.7 us -> 52 us  [partner(): return lax.ppermute(block, axis, route)]
    ppermute x15 -> x20, starting transfers between devices: 24.7 us -> 31.9 us  [partner(): return lax.ppermute(block, axis, route)]
    dot_general x2 -> x4, matrix products: 3.59 us -> 1.03 us  [shards_fast(): jnp.dot(shrunk, up[:, cut], preferred_element_type=jnp.float32)]
    squeeze x0 -> x1, local copies, waits for them, and re-layouts: none -> 1.77 us  [shards_fast(): lax.dynamic_slice(adapter_up_weight, (adapter[r], 0, 0), (1, ADAPTER_RANK...]
  transfers between devices with their start and end apart: 18 -> 23, of which waited for: 14 -> 13; matrix products, arithmetic and copies ran while one was open for 21% -> 23% of each run, Pallas kernels for 12% -> 13%
where the time goes in v4:
time: 157 us
  waiting for transfers between devices  56.7 us (36%)
  starting transfers between devices  36.1 us (23%)
  Pallas kernels  20.1 us (13%)
  matrix products  15.9 us (10%)
  other arithmetic  12.6 us (8%)
  local copies, waits for them, and re-layouts  8.92 us (6%)
  between operations  6.32 us (4%)
    ppermute x20, waiting for transfers between devices, partner(): return lax.ppermute(block, axis, route)  52 us
    ppermute x20, starting transfers between devices, partner(): return lax.ppermute(block, axis, route)  31.9 us
    pallas_call x2, Pallas kernels, attend(): pl.pallas_call(functools.partial(attend_kernel, heads_tile), out_shape=ja...  20.1 us
    dot_general x8, matrix products, product(): jnp.dot(rows, weight, preferred_element_type=jnp.float32)  13.8 us
    select_n x1, other arithmetic, shards_fast(): weight_send = jnp.where(keep_own, weight_partner, output_weight)  9.98 us
    ppermute x3, waiting for transfers between devices, from_others(): lax.ppermute(block, axis, [(i, (i + shift) % count) for i in range(count)])  4.72 us
    ppermute x3, starting transfers between devices, from_others(): lax.ppermute(block, axis, [(i, (i + shift) % count) for i in range(count)])  4.23 us
  transfers between devices with their start and end apart: 23, of which 13 were waited for; matrix products, arithmetic and copies ran while one was open for 23% of the time, Pallas kernels for 13%

profile of v4, /device:TPU:0, one launch (start us, length us, event | category | flops | bytes accessed | tf_op | source)
XLA Modules:
  0.0 156.6 jit_solution(6108272866601201725)
XLA Ops:
  0.6 0.5 collective-permute-start
  1.2 3.0 %dynamic-slice_bitcast_fusion = (bf16[2048,256]{1,0:T(8,128)(2,1)}, bf16[2048,256]{1,0:T(8,128)(2,1)}) fusion(bf16[2,2048,512]{2,1,0:T(8,128)(2,1)} %own_past.3, s32[]{:T(128)S(6)} %select_n.82), kind=kLoop, calls=%fused_computation.16 | loop fusion | bytes 4194308 | tf_op jit(solution)/shard_map/squeeze | solution.py:320
  4.2 2.7 %collective-permute-start.1 = (bf16[2048,256]{1,0:T(8,128)(2,1)}, bf16[2048,256]{1,0:T(8,128)(2,1)S(1)}, u32[]{:S(2)}, u32[]{:S(2)}) collective-permute-start(bf16[2048,256]{1,0:T(8,128)(2,1)} %get-tuple-element.39), channel_id=1, source_target_pairs={{0,4},{4,0},{8,12},{12,8},{1,5},{5,1},{9,13},{13,9},{2,6},{6,2},{1... | collective-permute-start | bytes 3145736 | tf_op jit(solution)/shard_map/ppermute | solution.py:30
  6.8 1.6 constant_dynamic-slice_fusion
  8.4 2.0 %collective-permute-start.3 = (bf16[2048,256]{1,0:T(8,128)(2,1)}, bf16[2048,256]{1,0:T(8,128)(2,1)S(1)}, u32[]{:S(2)}, u32[]{:S(2)}) collective-permute-start(bf16[2048,256]{1,0:T(8,128)(2,1)} %get-tuple-element.38), channel_id=1, source_target_pairs={{0,4},{4,0},{8,12},{12,8},{1,5},{5,1},{9,13},{13,9},{2,6},{6,2},{1... | collective-permute-start | bytes 3145736 | tf_op jit(solution)/shard_map/ppermute | solution.py:30
  10.4 1.4 fusion.21
  17.2 1.8 %dynamic-slice_bitcast_fusion.3 = (bf16[64,2048]{1,0:T(8,128)(2,1)}, bf16[64,2048]{1,0:T(8,128)(2,1)S(1)}) fusion(bf16[4,64,2048]{2,1,0:T(8,128)(2,1)} %param.17, s32[]{:T(128)S(6)} %select_n.86, s32[]{:T(128)S(6)} %select_n.92), kind=kLoop, calls=%fused_computation.35 | loop fusion | bytes 1048584 | tf_op jit(solution)/shard_map/squeeze | solution.py:402
  19.0 10.0 %broadcast_select_fusion = (bf16[2048,2048]{1,0:T(8,128)(2,1)}, bf16[2048,2048]{1,0:T(8,128)(2,1)S(1)}) fusion(bf16[2048,2048]{1,0:T(8,128)(2,1)} %collective-permute-done, bf16[2048,2048]{1,0:T(8,128)(2,1)} %param.15, pred[]{:T(512)S(6)} %eq.7), kind=kLoop, calls=%fused_computation | loop fusion | flops 8388608 | bytes 33554432 | tf_op jit(solution)/shard_map/jit(_where)/select_n | solution.py:333
  29.0 2.1 %collective-permute-done.1.recv_past = bf16[2048,256]{1,0:T(8,128)(2,1)S(1)} collective-permute-done((bf16[2048,256]{1,0:T(8,128)(2,1)}, bf16[2048,256]{1,0:T(8,128)(2,1)S(1)}, u32[]{:S(2)}, u32[]{:S(2)}) %collective-permute-start.1) | collective-permute-done | bytes 1048608 | tf_op jit(solution)/shard_map/ppermute | solution.py:30
  31.1 2.8 %collective-permute-done.2.recv_new = bf16[256,256]{1,0:T(8,128)(2,1)S(1)} collective-permute-done((bf16[256,256]{1,0:T(8,128)(2,1)}, bf16[256,256]{1,0:T(8,128)(2,1)S(1)}, u32[]{:S(2)}, u32[]{:S(2)}) %collective-permute-start.2) | collective-permute-done | bytes 131104 | tf_op jit(solution)/shard_map/ppermute | solution.py:30
  33.9 10.0 %attend.2 = bf16[128,2048]{1,0:T(8,128)(2,1)S(1)} custom-call(s32[2]{0:T(128)S(1)} %copy-done.4, s32[2]{0:T(128)S(1)} %pad_add_fusion.meta_ref, bf16[256,2048]{1,0:T(8,128)(2,1)S(1)} %copy-done.3, bf16[2,2048,512]{2,1,0:T(8,128)(2,1)S(1)} %copy-done.1, bf16[256,512]{1,0:T(8,128)(2,1)S(1)} %copy-done.2, ...), custom_call_target="tpu_custom_call" | custom-call | flops 2281701376 | bytes 3276800 | tf_op jit(solution)/shard_map/attend/pallas_call | solution.py:258
  43.9 1.9 %collective-permute-start.4 = (bf16[128,2048]{1,0:T(8,128)(2,1)S(1)}, bf16[128,2048]{1,0:T(8,128)(2,1)S(1)}, u32[]{:S(2)}, u32[]{:S(2)}) collective-permute-start(bf16[128,2048]{1,0:T(8,128)(2,1)S(1)} %attend.2), channel_id=1, source_target_pairs={{0,2},{2,0},{1,3},{3,1},{4,6},{6,4},{5,7},{7,5},{8,10},{10,8},{9,1... | collective-permute-start | bytes 1572872 | tf_op jit(solution)/shard_map/ppermute | solution.py:30
  45.8 1.3 convolution_convert_fusion.7
  47.1 0.1 copy-done.5
  47.2 1.3 convolution_convert_fusion.4
  48.6 0.5 fusion.22
  49.1 0.1 dynamic-slice_convert_fusion.1
  49.2 2.0 %collective-permute-start.5 = (bf16[128,2176]{1,0:T(8,128)(2,1)S(1)}, bf16[128,2176]{1,0:T(8,128)(2,1)S(1)}, u32[]{:S(2)}, u32[]{:S(2)}) collective-permute-start(bf16[128,2176]{1,0:T(8,128)(2,1)S(1)} %pad_maximum_fusion), channel_id=1, source_target_pairs={{0,4},{4,0},{8,12},{12,8},{1,5},{5,1},{9,13},{13,9},{2,6},{6,2},{1... | collective-permute-start | bytes 1671176 | tf_op jit(solution)/shard_map/ppermute | solution.py:30
  51.3 6.0 %collective-permute-done.4 = bf16[128,2048]{1,0:T(8,128)(2,1)S(1)} collective-permute-done((bf16[128,2048]{1,0:T(8,128)(2,1)S(1)}, bf16[128,2048]{1,0:T(8,128)(2,1)S(1)}, u32[]{:S(2)}, u32[]{:S(2)}) %collective-permute-start.4) | collective-permute-done | bytes 524320 | tf_op jit(solution)/shard_map/ppermute | solution.py:30
  57.3 1.3 convolution_convert_fusion.6
  58.6 0.8 fusion.20
  59.5 1.6 %collective-permute-start.9 = (bf16[128,1024]{1,0:T(8,128)(2,1)}, bf16[128,1024]{1,0:T(8,128)(2,1)S(1)}, u32[]{:S(2)}, u32[]{:S(2)}) collective-permute-start(bf16[128,1024]{1,0:T(8,128)(2,1)} %get-tuple-element.44), channel_id=1, source_target_pairs={{0,4},{4,0},{8,12},{12,8},{1,5},{5,1},{9,13},{13,9},{2,6},{6,2},{1... | collective-permute-start | bytes 786440 | tf_op jit(solution)/shard_map/ppermute | solution.py:30
  61.0 0.4 collective-permute-start.6
  61.5 10.1 %attend.3 = bf16[128,2048]{1,0:T(8,128)(2,1)S(1)} custom-call(s32[2]{0:T(128)S(1)} %copy-done.4, s32[2]{0:T(128)S(1)} %pad_add_fusion.1.meta_ref, bf16[256,2048]{1,0:T(8,128)(2,1)S(1)} %copy-done.3, bf16[2,2048,512]{2,1,0:T(8,128)(2,1)S(1)} %copy-done.1, bf16[256,512]{1,0:T(8,128)(2,1)S(1)} %copy-done.2, ...), custom_call_target="tpu_custom_call" | custom-call | flops 2281701376 | bytes 3276800 | tf_op jit(solution)/shard_map/attend/pallas_call | solution.py:258
  71.6 1.6 collective-permute-start.12
  73.2 4.6 %convolution_convert_fusion.1 = bf16[128,2048]{1,0:T(8,128)(2,1)S(1)} fusion(bf16[128,2048]{1,0:T(8,128)(2,1)S(1)} %attend.3, bf16[2048,2048]{1,0:T(8,128)(2,1)} %get-tuple-element.20), kind=kOutput, calls=%fused_computation.5 | convolution fusion | flops 1074003968 | bytes 9437184 | tf_op jit(solution)/shard_map/dot_general | solution.py:339
  77.9 1.3 convolution_convert_fusion.3
  79.2 1.3 convolution_convert_fusion.5
  80.5 0.5 fusion.23
  81.2 1.6 %collective-permute-start.13 = (bf16[128,2176]{1,0:T(8,128)(2,1)S(1)}, bf16[128,2176]{1,0:T(8,128)(2,1)S(1)}, u32[]{:S(2)}, u32[]{:S(2)}) collective-permute-start(bf16[128,2176]{1,0:T(8,128)(2,1)S(1)} %pad_maximum_fusion.1), channel_id=1, source_target_pairs={{0,4},{4,0},{8,12},{12,8},{1,5},{5,1},{9,13},{13,9},{2,6},{6,2},{1... | collective-permute-start | bytes 1671176 | tf_op jit(solution)/shard_map/ppermute | solution.py:30
  83.0 0.6 collective-permute-start.7
  83.6 1.6 collective-permute-start.10
  85.2 1.3 convolution_convert_fusion
  86.5 1.1 collective-permute-start.17
  87.6 4.4 %collective-permute-done.7 = bf16[128,1024]{1,0:T(8,128)(2,1)S(1)} collective-permute-done((bf16[128,1024]{1,0:T(8,128)(2,1)S(1)}, bf16[128,1024]{1,0:T(8,128)(2,1)S(1)}, u32[]{:S(2)}, u32[]{:S(2)}) %collective-permute-start.7) | collective-permute-done | bytes 262176 | tf_op jit(solution)/shard_map/ppermute | solution.py:30
  92.0 0.1 broadcast_select_fusion.5
  92.2 2.3 %collective-permute-start.8 = (bf16[128,1152]{1,0:T(8,128)(2,1)S(1)}, bf16[128,1152]{1,0:T(8,128)(2,1)S(1)}, u32[]{:S(2)}, u32[]{:S(2)}) collective-permute-start(bf16[128,1152]{1,0:T(8,128)(2,1)S(1)} %pad_maximum_fusion.2), channel_id=1, source_target_pairs={{0,8},{8,0},{4,12},{12,4},{1,9},{9,1},{5,13},{13,5},{2,10},{10,2},... | collective-permute-start | bytes 884744 | tf_op jit(solution)/shard_map/ppermute | solution.py:30
  94.5 0.4 collective-permute-done.10
  94.8 0.1 broadcast_select_fusion.4
  95.0 2.3 %collective-permute-start.11 = (bf16[128,1024]{1,0:T(8,128)(2,1)S(1)}, bf16[128,1024]{1,0:T(8,128)(2,1)S(1)}, u32[]{:S(2)}, u32[]{:S(2)}) collective-permute-start(bf16[128,1024]{1,0:T(8,128)(2,1)S(1)} %broadcast_select_fusion.4), channel_id=1, source_target_pairs={{0,8},{8,0},{4,12},{12,4},{1,9},{9,1},{5,13},{13,5},{2,10},{10,2},... | collective-permute-start | bytes 786440 | tf_op jit(solution)/shard_map/ppermute | solution.py:30
  97.3 1.6 collective-permute-start.14
  98.8 1.3 convolution_convert_fusion.2
  100.2 10.8 %collective-permute-done.17 = bf16[128,1024]{1,0:T(8,128)(2,1)S(1)} collective-permute-done((bf16[128,1024]{1,0:T(8,128)(2,1)S(1)}, bf16[128,1024]{1,0:T(8,128)(2,1)S(1)}, u32[]{:S(2)}, u32[]{:S(2)}) %collective-permute-start.17) | collective-permute-done | bytes 262176 | tf_op jit(solution)/shard_map/ppermute | solution.py:30
  110.9 5.5 %collective-permute-done.11 = bf16[128,1024]{1,0:T(8,128)(2,1)S(1)} collective-permute-done((bf16[128,1024]{1,0:T(8,128)(2,1)S(1)}, bf16[128,1024]{1,0:T(8,128)(2,1)S(1)}, u32[]{:S(2)}, u32[]{:S(2)}) %collective-permute-start.11) | collective-permute-done | bytes 262176 | tf_op jit(solution)/shard_map/ppermute | solution.py:30
  116.5 1.7 %collective-permute-start.15 = (bf16[128,1024]{1,0:T(8,128)(2,1)S(1)}, bf16[128,1024]{1,0:T(8,128)(2,1)S(1)}, u32[]{:S(2)}, u32[]{:S(2)}) collective-permute-start(bf16[128,1024]{1,0:T(8,128)(2,1)S(1)} %add_convert_fusion.4), channel_id=1, source_target_pairs={{0,2},{2,0},{1,3},{3,1},{4,6},{6,4},{5,7},{7,5},{8,10},{10,8},{9,1... | collective-permute-start | bytes 786440 | tf_op jit(solution)/shard_map/ppermute | solution.py:30
  118.2 0.5 collective-permute-start.18
  118.7 0.3 add_convert_fusion.6
  119.0 4.2 %collective-permute-done.15 = bf16[128,1024]{1,0:T(8,128)(2,1)S(1)} collective-permute-done((bf16[128,1024]{1,0:T(8,128)(2,1)S(1)}, bf16[128,1024]{1,0:T(8,128)(2,1)S(1)}, u32[]{:S(2)}, u32[]{:S(2)}) %collective-permute-start.15) | collective-permute-done | bytes 262176 | tf_op jit(solution)/shard_map/ppermute | solution.py:30
  123.2 0.1 broadcast_select_fusion.3
  123.3 3.6 %collective-permute-start.16 = (bf16[128,1152]{1,0:T(8,128)(2,1)S(1)}, bf16[128,1152]{1,0:T(8,128)(2,1)S(1)}, u32[]{:S(2)}, u32[]{:S(2)}) collective-permute-start(bf16[128,1152]{1,0:T(8,128)(2,1)S(1)} %pad_maximum_fusion.3), channel_id=1, source_target_pairs={{0,8},{8,0},{4,12},{12,4},{1,9},{9,1},{5,13},{13,5},{2,10},{10,2},... | collective-permute-start | bytes 884744 | tf_op jit(solution)/shard_map/ppermute | solution.py:30
  126.9 0.3 add_convert_fusion.9
  127.2 0.1 broadcast_select_fusion.2
  127.3 2.4 %collective-permute-start.19 = (bf16[128,1024]{1,0:T(8,128)(2,1)S(1)}, bf16[128,1024]{1,0:T(8,128)(2,1)S(1)}, u32[]{:S(2)}, u32[]{:S(2)}) collective-permute-start(bf16[128,1024]{1,0:T(8,128)(2,1)S(1)} %broadcast_select_fusion.2), channel_id=1, source_target_pairs={{0,8},{8,0},{4,12},{12,4},{1,9},{9,1},{5,13},{13,5},{2,10},{10,2},... | collective-permute-start | bytes 786440 | tf_op jit(solution)/shard_map/ppermute | solution.py:30
  129.7 13.3 %collective-permute-done.16 = bf16[128,1152]{1,0:T(8,128)(2,1)S(1)} collective-permute-done((bf16[128,1152]{1,0:T(8,128)(2,1)S(1)}, bf16[128,1152]{1,0:T(8,128)(2,1)S(1)}, u32[]{:S(2)}, u32[]{:S(2)}) %collective-permute-start.16) | collective-permute-done | bytes 294944 | tf_op jit(solution)/shard_map/ppermute | solution.py:30
  142.9 0.3 add_convert_fusion.3
  143.2 2.6 %collective-permute-done.19 = bf16[128,1024]{1,0:T(8,128)(2,1)S(1)} collective-permute-done((bf16[128,1024]{1,0:T(8,128)(2,1)S(1)}, bf16[128,1024]{1,0:T(8,128)(2,1)S(1)}, u32[]{:S(2)}, u32[]{:S(2)}) %collective-permute-start.19) | collective-permute-done | bytes 262176 | tf_op jit(solution)/shard_map/ppermute | solution.py:30
  145.8 0.3 add_convert_fusion
  146.1 0.3 fusion
  146.4 3.6 %collective-permute-start.22 = (f32[256]{0:T(256)S(1)}, f32[256]{0:T(256)S(1)}, u32[]{:S(2)}, u32[]{:S(2)}) collective-permute-start(f32[256]{0:T(256)S(1)} %get-tuple-element.34), channel_id=1, source_target_pairs={{0,12},{4,0},{8,4},{12,8},{1,13},{5,1},{9,5},{13,9},{2,14},{6,2},{... | collective-permute-start | bytes 3080 | tf_op jit(solution)/shard_map/ppermute | solution.py:292
  150.0 0.6 collective-permute-start.20
  150.6 0.7 collective-permute-done.22
  151.3 3.2 %collective-permute-done.21 = f32[256]{0:T(256)S(1)} collective-permute-done((f32[256]{0:T(256)S(1)}, f32[256]{0:T(256)S(1)}, u32[]{:S(2)}, u32[]{:S(2)}) %collective-permute-start.21) | collective-permute-done | bytes 1056 | tf_op jit(solution)/shard_map/ppermute | solution.py:292
  154.5 0.9 collective-permute-done.20
  155.4 1.3 fusion.2
  (56 shorter events, 0.8 us)
Async XLA Ops:
  0.6 47.9 %copy-start = (bf16[2048,4,64]{0,2,1:T(8,128)(2,1)S(1)}, bf16[2048,4,64]{0,2,1:T(8,128)(2,1)}, u32[]{:S(2)}) copy-start(bf16[2048,4,64]{0,2,1:T(8,128)(2,1)} %param.16) | copy-start | bytes 3145732
  0.6 18.4 %collective-permute-start = (bf16[2048,2048]{1,0:T(8,128)(2,1)}, bf16[2048,2048]{1,0:T(8,128)(2,1)}, u32[]{:S(2)}, u32[]{:S(2)}) collective-permute-start(bf16[2048,2048]{1,0:T(8,128)(2,1)} %param.15), channel_id=1, source_target_pairs={{0,1},{1,0},{2,3},{3,2},{4,5},{5,4},{6,7},{7,6},{8,9},{9,8},{10,11... | collective-permute-start | bytes 25165832 | tf_op jit(solution)/shard_map/ppermute | solution.py:30
  4.2 26.9 %collective-permute-start.1 = (bf16[2048,256]{1,0:T(8,128)(2,1)}, bf16[2048,256]{1,0:T(8,128)(2,1)S(1)}, u32[]{:S(2)}, u32[]{:S(2)}) collective-permute-start(bf16[2048,256]{1,0:T(8,128)(2,1)} %get-tuple-element.39), channel_id=1, source_target_pairs={{0,4},{4,0},{8,12},{12,8},{1,5},{5,1},{9,13},{13,9},{2,6},{6,2},{1... | collective-permute-start | bytes 3145736 | tf_op jit(solution)/shard_map/ppermute | solution.py:30
  8.4 25.5 %collective-permute-start.2 = (bf16[256,256]{1,0:T(8,128)(2,1)}, bf16[256,256]{1,0:T(8,128)(2,1)S(1)}, u32[]{:S(2)}, u32[]{:S(2)}) collective-permute-start(bf16[256,256]{1,0:T(8,128)(2,1)} %constant_dynamic-slice_fusion), channel_id=1, source_target_pairs={{0,4},{4,0},{8,12},{12,8},{1,5},{5,1},{9,13},{13,9},{2,6},{6,2},{1... | collective-permute-start | bytes 393224 | tf_op jit(solution)/shard_map/ppermute | solution.py:30
  8.4 53.1 %collective-permute-start.3 = (bf16[2048,256]{1,0:T(8,128)(2,1)}, bf16[2048,256]{1,0:T(8,128)(2,1)S(1)}, u32[]{:S(2)}, u32[]{:S(2)}) collective-permute-start(bf16[2048,256]{1,0:T(8,128)(2,1)} %get-tuple-element.38), channel_id=1, source_target_pairs={{0,4},{4,0},{8,12},{12,8},{1,5},{5,1},{9,13},{13,9},{2,6},{6,2},{1... | collective-permute-start | bytes 3145736 | tf_op jit(solution)/shard_map/ppermute | solution.py:30
  19.0 14.9 %copy-start.1 = (bf16[2,2048,512]{2,1,0:T(8,128)(2,1)S(1)}, bf16[2,2048,512]{2,1,0:T(8,128)(2,1)}, u32[]{:S(2)}) copy-start(bf16[2,2048,512]{2,1,0:T(8,128)(2,1)} %own_past.3) | copy-start | bytes 12582916
  19.0 14.9 %copy-start.2 = (bf16[256,512]{1,0:T(8,128)(2,1)S(1)}, bf16[256,512]{1,0:T(8,128)(2,1)}, u32[]{:S(2)}) copy-start(bf16[256,512]{1,0:T(8,128)(2,1)} %own_new.3) | copy-start | bytes 786436
  19.0 14.9 %copy-start.3 = (bf16[256,2048]{1,0:T(8,128)(2,1)S(1)}, bf16[256,2048]{1,0:T(8,128)(2,1)}, u32[]{:S(2)}) copy-start(bf16[256,2048]{1,0:T(8,128)(2,1)} %q_ref.3) | copy-start | bytes 3145732
  19.0 14.9 %copy-start.4 = (s32[2]{0:T(128)S(1)}, s32[2]{0:T(128)}, u32[]{:S(2)}) copy-start(s32[2]{0:T(128)} %length_ref.3) | copy-start | bytes 28
  43.9 3.4 %copy-start.5 = (bf16[2048,2048]{1,0:T(8,128)(2,1)S(1)}, bf16[2048,2048]{1,0:T(8,128)(2,1)}, u32[]{:S(2)}) copy-start(bf16[2048,2048]{1,0:T(8,128)(2,1)} %get-tuple-element.20) | copy-start | bytes 25165828
  43.9 13.4 %collective-permute-start.4 = (bf16[128,2048]{1,0:T(8,128)(2,1)S(1)}, bf16[128,2048]{1,0:T(8,128)(2,1)S(1)}, u32[]{:S(2)}, u32[]{:S(2)}) collective-permute-start(bf16[128,2048]{1,0:T(8,128)(2,1)S(1)} %attend.2), channel_id=1, source_target_pairs={{0,2},{2,0},{1,3},{3,1},{4,6},{6,4},{5,7},{7,5},{8,10},{10,8},{9,1... | collective-permute-start | bytes 1572872 | tf_op jit(solution)/shard_map/ppermute | solution.py:30
  49.2 33.6 %collective-permute-start.5 = (bf16[128,2176]{1,0:T(8,128)(2,1)S(1)}, bf16[128,2176]{1,0:T(8,128)(2,1)S(1)}, u32[]{:S(2)}, u32[]{:S(2)}) collective-permute-start(bf16[128,2176]{1,0:T(8,128)(2,1)S(1)} %pad_maximum_fusion), channel_id=1, source_target_pairs={{0,4},{4,0},{8,12},{12,8},{1,5},{5,1},{9,13},{13,9},{2,6},{6,2},{1... | collective-permute-start | bytes 1671176 | tf_op jit(solution)/shard_map/ppermute | solution.py:30
  59.5 24.1 %collective-permute-start.9 = (bf16[128,1024]{1,0:T(8,128)(2,1)}, bf16[128,1024]{1,0:T(8,128)(2,1)S(1)}, u32[]{:S(2)}, u32[]{:S(2)}) collective-permute-start(bf16[128,1024]{1,0:T(8,128)(2,1)} %get-tuple-element.44), channel_id=1, source_target_pairs={{0,4},{4,0},{8,12},{12,8},{1,5},{5,1},{9,13},{13,9},{2,6},{6,2},{1... | collective-permute-start | bytes 786440 | tf_op jit(solution)/shard_map/ppermute | solution.py:30
  61.0 21.8 %collective-permute-start.6 = (bf16[128,1024]{1,0:T(8,128)(2,1)}, bf16[128,1024]{1,0:T(8,128)(2,1)S(1)}, u32[]{:S(2)}, u32[]{:S(2)}) collective-permute-start(bf16[128,1024]{1,0:T(8,128)(2,1)} %get-tuple-element.45), channel_id=1, source_target_pairs={{0,4},{4,0},{8,12},{12,8},{1,5},{5,1},{9,13},{13,9},{2,6},{6,2},{1... | collective-permute-start | bytes 786440 | tf_op jit(solution)/shard_map/ppermute | solution.py:30
  71.6 13.5 %collective-permute-start.12 = (bf16[128,2048]{1,0:T(8,128)(2,1)S(1)}, bf16[128,2048]{1,0:T(8,128)(2,1)S(1)}, u32[]{:S(2)}, u32[]{:S(2)}) collective-permute-start(bf16[128,2048]{1,0:T(8,128)(2,1)S(1)} %attend.3), channel_id=1, source_target_pairs={{0,2},{2,0},{1,3},{3,1},{4,6},{6,4},{5,7},{7,5},{8,10},{10,8},{9,1... | collective-permute-start | bytes 1572872 | tf_op jit(solution)/shard_map/ppermute | solution.py:30
  77.9 7.3 %slice-start = ((s8[8388608]{0:T(1024)(128)(4,1)}), s8[4194304]{0:T(1024)(128)(4,1)S(1)}, s32[]{:S(2)}) async-start(s8[8388608]{0:T(1024)(128)(4,1)} %bitcast.34), calls=%async_computation | async-start | bytes 8388608
  79.2 6.0 %slice-start.1 = ((s8[8388608]{0:T(1024)(128)(4,1)}), s8[4194304]{0:T(1024)(128)(4,1)S(1)}, s32[]{:S(2)}) async-start(s8[8388608]{0:T(1024)(128)(4,1)} %bitcast.34), calls=%async_computation.1 | async-start | bytes 8388608
  81.2 35.2 %collective-permute-start.13 = (bf16[128,2176]{1,0:T(8,128)(2,1)S(1)}, bf16[128,2176]{1,0:T(8,128)(2,1)S(1)}, u32[]{:S(2)}, u32[]{:S(2)}) collective-permute-start(bf16[128,2176]{1,0:T(8,128)(2,1)S(1)} %pad_maximum_fusion.1), channel_id=1, source_target_pairs={{0,4},{4,0},{8,12},{12,8},{1,5},{5,1},{9,13},{13,9},{2,6},{6,2},{1... | collective-permute-start | bytes 1671176 | tf_op jit(solution)/shard_map/ppermute | solution.py:30
  83.0 9.1 %collective-permute-start.7 = (bf16[128,1024]{1,0:T(8,128)(2,1)S(1)}, bf16[128,1024]{1,0:T(8,128)(2,1)S(1)}, u32[]{:S(2)}, u32[]{:S(2)}) collective-permute-start(bf16[128,1024]{1,0:T(8,128)(2,1)S(1)} %add_convert_fusion.10), channel_id=1, source_target_pairs={{0,2},{2,0},{1,3},{3,1},{4,6},{6,4},{5,7},{7,5},{8,10},{10,8},{9,1... | collective-permute-start | bytes 786440 | tf_op jit(solution)/shard_map/ppermute | solution.py:30
  83.6 11.2 %collective-permute-start.10 = (bf16[128,1024]{1,0:T(8,128)(2,1)S(1)}, bf16[128,1024]{1,0:T(8,128)(2,1)S(1)}, u32[]{:S(2)}, u32[]{:S(2)}) collective-permute-start(bf16[128,1024]{1,0:T(8,128)(2,1)S(1)} %add_convert_fusion.7), channel_id=1, source_target_pairs={{0,2},{2,0},{1,3},{3,1},{4,6},{6,4},{5,7},{7,5},{8,10},{10,8},{9,1... | collective-permute-start | bytes 786440 | tf_op jit(solution)/shard_map/ppermute | solution.py:30
  86.5 24.4 %collective-permute-start.17 = (bf16[128,1024]{1,0:T(8,128)(2,1)S(1)}, bf16[128,1024]{1,0:T(8,128)(2,1)S(1)}, u32[]{:S(2)}, u32[]{:S(2)}) collective-permute-start(bf16[128,1024]{1,0:T(8,128)(2,1)S(1)} %get-tuple-element.43), channel_id=1, source_target_pairs={{0,4},{4,0},{8,12},{12,8},{1,5},{5,1},{9,13},{13,9},{2,6},{6,2},{1... | collective-permute-start | bytes 786440 | tf_op jit(solution)/shard_map/ppermute | solution.py:30
  92.2 24.2 %collective-permute-start.8 = (bf16[128,1152]{1,0:T(8,128)(2,1)S(1)}, bf16[128,1152]{1,0:T(8,128)(2,1)S(1)}, u32[]{:S(2)}, u32[]{:S(2)}) collective-permute-start(bf16[128,1152]{1,0:T(8,128)(2,1)S(1)} %pad_maximum_fusion.2), channel_id=1, source_target_pairs={{0,8},{8,0},{4,12},{12,4},{1,9},{9,1},{5,13},{13,5},{2,10},{10,2},... | collective-permute-start | bytes 884744 | tf_op jit(solution)/shard_map/ppermute | solution.py:30
  95.0 21.4 %collective-permute-start.11 = (bf16[128,1024]{1,0:T(8,128)(2,1)S(1)}, bf16[128,1024]{1,0:T(8,128)(2,1)S(1)}, u32[]{:S(2)}, u32[]{:S(2)}) collective-permute-start(bf16[128,1024]{1,0:T(8,128)(2,1)S(1)} %broadcast_select_fusion.4), channel_id=1, source_target_pairs={{0,8},{8,0},{4,12},{12,4},{1,9},{9,1},{5,13},{13,5},{2,10},{10,2},... | collective-permute-start | bytes 786440 | tf_op jit(solution)/shard_map/ppermute | solution.py:30
  97.2 21.5 %copy-start.7 = (bf16[64,2048]{1,0:T(8,128)(2,1)S(1)}, bf16[64,2048]{1,0:T(8,128)(2,1)}, u32[]{:S(2)}) copy-start(bf16[64,2048]{1,0:T(8,128)(2,1)} %get-tuple-element.40) | copy-start | bytes 786436
  97.3 21.5 %copy-start.9 = (bf16[256,2048]{1,0:T(8,128)(2,1)S(1)}, bf16[256,2048]{1,0:T(8,128)(2,1)}, u32[]{:S(2)}) copy-start(bf16[256,2048]{1,0:T(8,128)(2,1)} %param.18) | copy-start | bytes 3145732
  97.3 19.1 %collective-permute-start.14 = (bf16[128,1024]{1,0:T(8,128)(2,1)S(1)}, bf16[128,1024]{1,0:T(8,128)(2,1)S(1)}, u32[]{:S(2)}, u32[]{:S(2)}) collective-permute-start(bf16[128,1024]{1,0:T(8,128)(2,1)S(1)} %get-tuple-element.42), channel_id=1, source_target_pairs={{0,4},{4,0},{8,12},{12,8},{1,5},{5,1},{9,13},{13,9},{2,6},{6,2},{1... | collective-permute-start | bytes 786440 | tf_op jit(solution)/shard_map/ppermute | solution.py:30
  100.1 50.5 %copy-start.8 = (bf16[2048]{0:T(1024)(128)(2,1)S(1)}, bf16[2048]{0:T(1024)(128)(2,1)}, u32[]{:S(2)}) copy-start(bf16[2048]{0:T(1024)(128)(2,1)} %param.19) | copy-start | bytes 12292
  116.5 6.7 %collective-permute-start.15 = (bf16[128,1024]{1,0:T(8,128)(2,1)S(1)}, bf16[128,1024]{1,0:T(8,128)(2,1)S(1)}, u32[]{:S(2)}, u32[]{:S(2)}) collective-permute-start(bf16[128,1024]{1,0:T(8,128)(2,1)S(1)} %add_convert_fusion.4), channel_id=1, source_target_pairs={{0,2},{2,0},{1,3},{3,1},{4,6},{6,4},{5,7},{7,5},{8,10},{10,8},{9,1... | collective-permute-start | bytes 786440 | tf_op jit(solution)/shard_map/ppermute | solution.py:30
  118.2 9.0 %collective-permute-start.18 = (bf16[128,1024]{1,0:T(8,128)(2,1)S(1)}, bf16[128,1024]{1,0:T(8,128)(2,1)S(1)}, u32[]{:S(2)}, u32[]{:S(2)}) collective-permute-start(bf16[128,1024]{1,0:T(8,128)(2,1)S(1)} %add_convert_fusion.1), channel_id=1, source_target_pairs={{0,2},{2,0},{1,3},{3,1},{4,6},{6,4},{5,7},{7,5},{8,10},{10,8},{9,1... | collective-permute-start | bytes 786440 | tf_op jit(solution)/shard_map/ppermute | solution.py:30
  123.3 19.6 %collective-permute-start.16 = (bf16[128,1152]{1,0:T(8,128)(2,1)S(1)}, bf16[128,1152]{1,0:T(8,128)(2,1)S(1)}, u32[]{:S(2)}, u32[]{:S(2)}) collective-permute-start(bf16[128,1152]{1,0:T(8,128)(2,1)S(1)} %pad_maximum_fusion.3), channel_id=1, source_target_pairs={{0,8},{8,0},{4,12},{12,4},{1,9},{9,1},{5,13},{13,5},{2,10},{10,2},... | collective-permute-start | bytes 884744 | tf_op jit(solution)/shard_map/ppermute | solution.py:30
  127.3 18.5 %collective-permute-start.19 = (bf16[128,1024]{1,0:T(8,128)(2,1)S(1)}, bf16[128,1024]{1,0:T(8,128)(2,1)S(1)}, u32[]{:S(2)}, u32[]{:S(2)}) collective-permute-start(bf16[128,1024]{1,0:T(8,128)(2,1)S(1)} %broadcast_select_fusion.2), channel_id=1, source_target_pairs={{0,8},{8,0},{4,12},{12,4},{1,9},{9,1},{5,13},{13,5},{2,10},{10,2},... | collective-permute-start | bytes 786440 | tf_op jit(solution)/shard_map/ppermute | solution.py:30
  146.4 10.3 %copy-start.6 = (bf16[256,2048]{1,0:T(8,128)(2,1)}, bf16[256,2048]{1,0:T(8,128)(2,1)S(1)}, u32[]{:S(2)}) copy-start(bf16[256,2048]{1,0:T(8,128)(2,1)S(1)} %get-tuple-element.35) | copy-start | bytes 3145732
  146.4 4.9 %collective-permute-start.22 = (f32[256]{0:T(256)S(1)}, f32[256]{0:T(256)S(1)}, u32[]{:S(2)}, u32[]{:S(2)}) collective-permute-start(f32[256]{0:T(256)S(1)} %get-tuple-element.34), channel_id=1, source_target_pairs={{0,12},{4,0},{8,4},{12,8},{1,13},{5,1},{9,5},{13,9},{2,14},{6,2},{... | collective-permute-start | bytes 3080 | tf_op jit(solution)/shard_map/ppermute | solution.py:292
  150.0 4.5 %collective-permute-start.21 = (f32[256]{0:T(256)S(1)}, f32[256]{0:T(256)S(1)}, u32[]{:S(2)}, u32[]{:S(2)}) collective-permute-start(f32[256]{0:T(256)S(1)} %get-tuple-element.34), channel_id=1, source_target_pairs={{0,8},{4,12},{8,0},{12,4},{1,9},{5,13},{9,1},{13,5},{2,10},{6,14},... | collective-permute-start | bytes 3080 | tf_op jit(solution)/shard_map/ppermute | solution.py:292
  150.0 5.4 %collective-permute-start.20 = (f32[256]{0:T(256)S(1)}, f32[256]{0:T(256)S(1)}, u32[]{:S(2)}, u32[]{:S(2)}) collective-permute-start(f32[256]{0:T(256)S(1)} %get-tuple-element.34), channel_id=1, source_target_pairs={{0,4},{4,8},{8,12},{12,0},{1,5},{5,9},{9,13},{13,1},{2,6},{6,10},{... | collective-permute-start | bytes 3080 | tf_op jit(solution)/shard_map/ppermute | solution.py:292

commit v5 on v4

--- a/solution.py
+++ b/solution.py
@@ -382,7 +382,7 @@
             got_mine, got_theirs[0], _ = lax.optimization_barrier(
                 (got_mine, got_theirs[0], (before[0], payload))
             )
-            got_theirs[1], _ = lax.optimization_barrier((got_theirs[1], before[1]))
+            earlier = before[1]
         rank_pair = pair_sum(rank, got_mine[:, width:])
         kept, before = [], []
         for i, cut in enumerate(cuts):
@@ -392,6 +392,8 @@
             theirs = partner(crossing, "dp", 0)
             if i > 0:
                 theirs, _ = lax.optimization_barrier((theirs, payload))
+            elif r > 0:
+                theirs, _ = lax.optimization_barrier((theirs, earlier))
             mine = pair_sum(keep_mine[:, cut], got_mine[:, cut])
             kept.append(jnp.where(x == upper, mine, theirs))
             payload = jnp.where(x == upper, theirs, mine)

time: 157 us -> 164 us (1.045)
  waiting for transfers between devices: 56.7 us -> 69.9 us
  starting transfers between devices: 36.1 us -> 30.3 us
    ppermute x20, waiting for transfers between devices: 52 us -> 65.2 us  [partner(): return lax.ppermute(block, axis, route)]
    ppermute x20, starting transfers between devices: 31.9 us -> 27 us  [partner(): return lax.ppermute(block, axis, route)]
  transfers between devices with their start and end apart: 23 -> 23, of which waited for: 13 -> 14; matrix products, arithmetic and copies ran while one was open for 23% -> 21% of each run, Pallas kernels for 13% -> 12%
where the time goes in v5:
time: 164 us; the launch traced here: 163 us
  waiting for transfers between devices  69.9 us (43%)
  starting transfers between devices  30.3 us (18%)
  Pallas kernels  20.1 us (12%)
  matrix products  15.9 us (10%)
  other arithmetic  12.6 us (8%)
  local copies, waits for them, and re-layouts  8.31 us (5%)
  between operations  6.25 us (4%)
    ppermute x20, waiting for transfers between devices, partner(): return lax.ppermute(block, axis, route)  65.2 us
    ppermute x20, starting transfers between devices, partner(): return lax.ppermute(block, axis, route)  27 us
    pallas_call x2, Pallas kernels, attend(): pl.pallas_call(functools.partial(attend_kernel, heads_tile), out_shape=ja...  20.1 us
    dot_general x8, matrix products, product(): jnp.dot(rows, weight, preferred_element_type=jnp.float32)  13.8 us
    select_n x1, other arithmetic, shards_fast(): weight_send = jnp.where(keep_own, weight_partner, output_weight)  9.97 us
    ppermute x3, waiting for transfers between devices, from_others(): lax.ppermute(block, axis, [(i, (i + shift) % count) for i in range(count)])  4.72 us
    ppermute x3, starting transfers between devices, from_others(): lax.ppermute(block, axis, [(i, (i + shift) % count) for i in range(count)])  3.3 us
  transfers between devices with their start and end apart: 23, of which 14 were waited for; matrix products, arithmetic and copies ran while one was open for 21% of the time, Pallas kernels for 12%

profile of v5, /device:TPU:0, one launch (start us, length us, event | category | flops | bytes accessed | tf_op | source)
XLA Modules:
  0.0 163.4 jit_solution(1790710399039346543)
XLA Ops:
  0.6 0.5 collective-permute-start
  1.2 3.0 %dynamic-slice_bitcast_fusion = (bf16[2048,256]{1,0:T(8,128)(2,1)}, bf16[2048,256]{1,0:T(8,128)(2,1)}) fusion(bf16[2,2048,512]{2,1,0:T(8,128)(2,1)} %own_past.3, s32[]{:T(128)S(6)} %select_n.82), kind=kLoop, calls=%fused_computation.16 | loop fusion | bytes 4194308 | tf_op jit(solution)/shard_map/squeeze | solution.py:320
  4.2 2.7 %collective-permute-start.1 = (bf16[2048,256]{1,0:T(8,128)(2,1)}, bf16[2048,256]{1,0:T(8,128)(2,1)S(1)}, u32[]{:S(2)}, u32[]{:S(2)}) collective-permute-start(bf16[2048,256]{1,0:T(8,128)(2,1)} %get-tuple-element.39), channel_id=1, source_target_pairs={{0,4},{4,0},{8,12},{12,8},{1,5},{5,1},{9,13},{13,9},{2,6},{6,2},{1... | collective-permute-start | bytes 3145736 | tf_op jit(solution)/shard_map/ppermute | solution.py:30
  6.8 0.9 constant_dynamic-slice_fusion
  7.8 2.0 %collective-permute-start.3 = (bf16[2048,256]{1,0:T(8,128)(2,1)}, bf16[2048,256]{1,0:T(8,128)(2,1)S(1)}, u32[]{:S(2)}, u32[]{:S(2)}) collective-permute-start(bf16[2048,256]{1,0:T(8,128)(2,1)} %get-tuple-element.38), channel_id=1, source_target_pairs={{0,4},{4,0},{8,12},{12,8},{1,5},{5,1},{9,13},{13,9},{2,6},{6,2},{1... | collective-permute-start | bytes 3145736 | tf_op jit(solution)/shard_map/ppermute | solution.py:30
  9.8 1.3 fusion.21
  16.5 1.9 %dynamic-slice_bitcast_fusion.3 = (bf16[64,2048]{1,0:T(8,128)(2,1)}, bf16[64,2048]{1,0:T(8,128)(2,1)}) fusion(bf16[4,64,2048]{2,1,0:T(8,128)(2,1)} %param.17, s32[]{:T(128)S(6)} %select_n.86, s32[]{:T(128)S(6)} %select_n.92), kind=kLoop, calls=%fused_computation.35 | loop fusion | bytes 1048584 | tf_op jit(solution)/shard_map/squeeze | solution.py:404
  18.4 10.0 %broadcast_select_fusion = (bf16[2048,2048]{1,0:T(8,128)(2,1)}, bf16[2048,2048]{1,0:T(8,128)(2,1)S(1)}) fusion(bf16[2048,2048]{1,0:T(8,128)(2,1)} %collective-permute-done, bf16[2048,2048]{1,0:T(8,128)(2,1)} %param.15, pred[]{:T(512)S(6)} %eq.7), kind=kLoop, calls=%fused_computation | loop fusion | flops 8388608 | bytes 33554432 | tf_op jit(solution)/shard_map/jit(_where)/select_n | solution.py:333
  28.4 2.7 %collective-permute-done.1.recv_past = bf16[2048,256]{1,0:T(8,128)(2,1)S(1)} collective-permute-done((bf16[2048,256]{1,0:T(8,128)(2,1)}, bf16[2048,256]{1,0:T(8,128)(2,1)S(1)}, u32[]{:S(2)}, u32[]{:S(2)}) %collective-permute-start.1) | collective-permute-done | bytes 1048608 | tf_op jit(solution)/shard_map/ppermute | solution.py:30
  31.1 2.8 %collective-permute-done.2.recv_new = bf16[256,256]{1,0:T(8,128)(2,1)S(1)} collective-permute-done((bf16[256,256]{1,0:T(8,128)(2,1)S(1)}, bf16[256,256]{1,0:T(8,128)(2,1)S(1)}, u32[]{:S(2)}, u32[]{:S(2)}) %collective-permute-start.2) | collective-permute-done | bytes 131104 | tf_op jit(solution)/shard_map/ppermute | solution.py:30
  33.9 10.0 %attend.2 = bf16[128,2048]{1,0:T(8,128)(2,1)S(1)} custom-call(s32[2]{0:T(128)S(1)} %copy-done.4, s32[2]{0:T(128)S(1)} %pad_add_fusion.meta_ref, bf16[256,2048]{1,0:T(8,128)(2,1)S(1)} %copy-done.3, bf16[2,2048,512]{2,1,0:T(8,128)(2,1)S(1)} %copy-done.1, bf16[256,512]{1,0:T(8,128)(2,1)S(1)} %copy-done.2, ...), custom_call_target="tpu_custom_call" | custom-call | flops 2281701376 | bytes 3276800 | tf_op jit(solution)/shard_map/attend/pallas_call | solution.py:258
  43.9 1.9 %collective-permute-start.4 = (bf16[128,2048]{1,0:T(8,128)(2,1)S(1)}, bf16[128,2048]{1,0:T(8,128)(2,1)S(1)}, u32[]{:S(2)}, u32[]{:S(2)}) collective-permute-start(bf16[128,2048]{1,0:T(8,128)(2,1)S(1)} %attend.2), channel_id=1, source_target_pairs={{0,2},{2,0},{1,3},{3,1},{4,6},{6,4},{5,7},{7,5},{8,10},{10,8},{9,1... | collective-permute-start | bytes 1572872 | tf_op jit(solution)/shard_map/ppermute | solution.py:30
  45.8 1.3 convolution_convert_fusion.7
  47.1 0.1 copy-done.5
  47.2 1.3 convolution_convert_fusion.4
  48.6 0.5 fusion.22
  49.2 2.0 %collective-permute-start.5 = (bf16[128,2176]{1,0:T(8,128)(2,1)S(1)}, bf16[128,2176]{1,0:T(8,128)(2,1)S(1)}, u32[]{:S(2)}, u32[]{:S(2)}) collective-permute-start(bf16[128,2176]{1,0:T(8,128)(2,1)S(1)} %pad_maximum_fusion), channel_id=1, source_target_pairs={{0,4},{4,0},{8,12},{12,8},{1,5},{5,1},{9,13},{13,9},{2,6},{6,2},{1... | collective-permute-start | bytes 1671176 | tf_op jit(solution)/shard_map/ppermute | solution.py:30
  51.3 6.0 %collective-permute-done.4 = bf16[128,2048]{1,0:T(8,128)(2,1)S(1)} collective-permute-done((bf16[128,2048]{1,0:T(8,128)(2,1)S(1)}, bf16[128,2048]{1,0:T(8,128)(2,1)S(1)}, u32[]{:S(2)}, u32[]{:S(2)}) %collective-permute-start.4) | collective-permute-done | bytes 524320 | tf_op jit(solution)/shard_map/ppermute | solution.py:30
  57.3 1.3 convolution_convert_fusion.6
  58.6 0.8 fusion.20
  59.5 10.1 %attend.3 = bf16[128,2048]{1,0:T(8,128)(2,1)S(1)} custom-call(s32[2]{0:T(128)S(1)} %copy-done.4, s32[2]{0:T(128)S(1)} %pad_add_fusion.1.meta_ref, bf16[256,2048]{1,0:T(8,128)(2,1)S(1)} %copy-done.3, bf16[2,2048,512]{2,1,0:T(8,128)(2,1)S(1)} %copy-done.1, bf16[256,512]{1,0:T(8,128)(2,1)S(1)} %copy-done.2, ...), custom_call_target="tpu_custom_call" | custom-call | flops 2281701376 | bytes 3276800 | tf_op jit(solution)/shard_map/attend/pallas_call | solution.py:258
  69.6 1.6 collective-permute-start.12
  71.2 0.5 fusion.23
  71.7 4.6 %convolution_convert_fusion.1 = bf16[128,2048]{1,0:T(8,128)(2,1)S(1)} fusion(bf16[128,2048]{1,0:T(8,128)(2,1)S(1)} %attend.3, bf16[2048,2048]{1,0:T(8,128)(2,1)} %get-tuple-element.20), kind=kOutput, calls=%fused_computation.5 | convolution fusion | flops 1074003968 | bytes 9437184 | tf_op jit(solution)/shard_map/dot_general | solution.py:339
  76.3 1.6 %collective-permute-start.6 = (bf16[128,1024]{1,0:T(8,128)(2,1)}, bf16[128,1024]{1,0:T(8,128)(2,1)S(1)}, u32[]{:S(2)}, u32[]{:S(2)}) collective-permute-start(bf16[128,1024]{1,0:T(8,128)(2,1)} %get-tuple-element.45), channel_id=1, source_target_pairs={{0,4},{4,0},{8,12},{12,8},{1,5},{5,1},{9,13},{13,9},{2,6},{6,2},{1... | collective-permute-start | bytes 786440 | tf_op jit(solution)/shard_map/ppermute | solution.py:30
  77.9 0.4 collective-permute-start.9
  78.4 1.3 convolution_convert_fusion.3
  79.9 1.6 %collective-permute-start.13 = (bf16[128,2176]{1,0:T(8,128)(2,1)S(1)}, bf16[128,2176]{1,0:T(8,128)(2,1)S(1)}, u32[]{:S(2)}, u32[]{:S(2)}) collective-permute-start(bf16[128,2176]{1,0:T(8,128)(2,1)S(1)} %pad_maximum_fusion.1), channel_id=1, source_target_pairs={{0,4},{4,0},{8,12},{12,8},{1,5},{5,1},{9,13},{13,9},{2,6},{6,2},{1... | collective-permute-start | bytes 1671176 | tf_op jit(solution)/shard_map/ppermute | solution.py:30
  81.6 1.3 convolution_convert_fusion.5
  82.9 2.9 %collective-permute-done.6 = bf16[128,1024]{1,0:T(8,128)(2,1)S(1)} collective-permute-done((bf16[128,1024]{1,0:T(8,128)(2,1)}, bf16[128,1024]{1,0:T(8,128)(2,1)S(1)}, u32[]{:S(2)}, u32[]{:S(2)}) %collective-permute-start.6) | collective-permute-done | bytes 262176 | tf_op jit(solution)/shard_map/ppermute | solution.py:30
  85.9 0.6 collective-permute-start.7
  86.5 5.0 %collective-permute-done.9 = bf16[128,1024]{1,0:T(8,128)(2,1)S(1)} collective-permute-done((bf16[128,1024]{1,0:T(8,128)(2,1)}, bf16[128,1024]{1,0:T(8,128)(2,1)S(1)}, u32[]{:S(2)}, u32[]{:S(2)}) %collective-permute-start.9) | collective-permute-done | bytes 262176 | tf_op jit(solution)/shard_map/ppermute | solution.py:30
  91.5 0.6 collective-permute-start.10
  92.1 1.3 convolution_convert_fusion
  93.4 1.6 %collective-permute-start.17 = (bf16[128,1024]{1,0:T(8,128)(2,1)S(1)}, bf16[128,1024]{1,0:T(8,128)(2,1)S(1)}, u32[]{:S(2)}, u32[]{:S(2)}) collective-permute-start(bf16[128,1024]{1,0:T(8,128)(2,1)S(1)} %get-tuple-element.43), channel_id=1, source_target_pairs={{0,4},{4,0},{8,12},{12,8},{1,5},{5,1},{9,13},{13,9},{2,6},{6,2},{1... | collective-permute-start | bytes 786440 | tf_op jit(solution)/shard_map/ppermute | solution.py:30
  95.1 0.4 collective-permute-start.14
  95.5 0.1 broadcast_select_fusion.5
  95.7 2.7 %collective-permute-start.8 = (bf16[128,1152]{1,0:T(8,128)(2,1)S(1)}, bf16[128,1152]{1,0:T(8,128)(2,1)S(1)}, u32[]{:S(2)}, u32[]{:S(2)}) collective-permute-start(bf16[128,1152]{1,0:T(8,128)(2,1)S(1)} %pad_maximum_fusion.2), channel_id=1, source_target_pairs={{0,8},{8,0},{4,12},{12,4},{1,9},{9,1},{5,13},{13,5},{2,10},{10,2},... | collective-permute-start | bytes 884744 | tf_op jit(solution)/shard_map/ppermute | solution.py:30
  98.4 1.3 convolution_convert_fusion.2
  99.7 0.1 broadcast_select_fusion.4
  99.9 0.9 collective-permute-start.11
  100.7 14.6 %collective-permute-done.13 = bf16[128,2176]{1,0:T(8,128)(2,1)S(1)} collective-permute-done((bf16[128,2176]{1,0:T(8,128)(2,1)S(1)}, bf16[128,2176]{1,0:T(8,128)(2,1)S(1)}, u32[]{:S(2)}, u32[]{:S(2)}) %collective-permute-start.13) | collective-permute-done | bytes 557088 | tf_op jit(solution)/shard_map/ppermute | solution.py:30
  115.3 8.2 %collective-permute-done.14 = bf16[128,1024]{1,0:T(8,128)(2,1)S(1)} collective-permute-done((bf16[128,1024]{1,0:T(8,128)(2,1)S(1)}, bf16[128,1024]{1,0:T(8,128)(2,1)S(1)}, u32[]{:S(2)}, u32[]{:S(2)}) %collective-permute-start.14) | collective-permute-done | bytes 262176 | tf_op jit(solution)/shard_map/ppermute | solution.py:30
  123.6 1.0 collective-permute-start.15
  124.6 1.2 collective-permute-start.18
  125.8 0.3 add_convert_fusion.6
  126.1 5.6 %collective-permute-done.15 = bf16[128,1024]{1,0:T(8,128)(2,1)S(1)} collective-permute-done((bf16[128,1024]{1,0:T(8,128)(2,1)S(1)}, bf16[128,1024]{1,0:T(8,128)(2,1)S(1)}, u32[]{:S(2)}, u32[]{:S(2)}) %collective-permute-start.15) | collective-permute-done | bytes 262176 | tf_op jit(solution)/shard_map/ppermute | solution.py:30
  131.7 0.1 broadcast_select_fusion.3
  131.8 1.8 %collective-permute-start.16 = (bf16[128,1152]{1,0:T(8,128)(2,1)S(1)}, bf16[128,1152]{1,0:T(8,128)(2,1)S(1)}, u32[]{:S(2)}, u32[]{:S(2)}) collective-permute-start(bf16[128,1152]{1,0:T(8,128)(2,1)S(1)} %pad_maximum_fusion.3), channel_id=1, source_target_pairs={{0,8},{8,0},{4,12},{12,4},{1,9},{9,1},{5,13},{13,5},{2,10},{10,2},... | collective-permute-start | bytes 884744 | tf_op jit(solution)/shard_map/ppermute | solution.py:30
  133.6 0.3 add_convert_fusion.9
  133.9 0.6 collective-permute-done.18
  134.5 0.1 broadcast_select_fusion.2
  134.6 1.8 %collective-permute-start.19 = (bf16[128,1024]{1,0:T(8,128)(2,1)S(1)}, bf16[128,1024]{1,0:T(8,128)(2,1)S(1)}, u32[]{:S(2)}, u32[]{:S(2)}) collective-permute-start(bf16[128,1024]{1,0:T(8,128)(2,1)S(1)} %broadcast_select_fusion.2), channel_id=1, source_target_pairs={{0,8},{8,0},{4,12},{12,4},{1,9},{9,1},{5,13},{13,5},{2,10},{10,2},... | collective-permute-start | bytes 786440 | tf_op jit(solution)/shard_map/ppermute | solution.py:30
  136.4 14.2 %collective-permute-done.16 = bf16[128,1152]{1,0:T(8,128)(2,1)S(1)} collective-permute-done((bf16[128,1152]{1,0:T(8,128)(2,1)S(1)}, bf16[128,1152]{1,0:T(8,128)(2,1)S(1)}, u32[]{:S(2)}, u32[]{:S(2)}) %collective-permute-start.16) | collective-permute-done | bytes 294944 | tf_op jit(solution)/shard_map/ppermute | solution.py:30
  150.6 0.3 add_convert_fusion.3
  150.8 2.7 %collective-permute-done.19 = bf16[128,1024]{1,0:T(8,128)(2,1)S(1)} collective-permute-done((bf16[128,1024]{1,0:T(8,128)(2,1)S(1)}, bf16[128,1024]{1,0:T(8,128)(2,1)S(1)}, u32[]{:S(2)}, u32[]{:S(2)}) %collective-permute-start.19) | collective-permute-done | bytes 262176 | tf_op jit(solution)/shard_map/ppermute | solution.py:30
  153.5 0.3 add_convert_fusion
  153.8 0.3 fusion
  154.1 2.7 %collective-permute-start.22 = (f32[256]{0:T(256)S(1)}, f32[256]{0:T(256)S(1)}, u32[]{:S(2)}, u32[]{:S(2)}) collective-permute-start(f32[256]{0:T(256)S(1)} %get-tuple-element.34), channel_id=1, source_target_pairs={{0,12},{4,0},{8,4},{12,8},{1,13},{5,1},{9,5},{13,9},{2,14},{6,2},{... | collective-permute-start | bytes 3080 | tf_op jit(solution)/shard_map/ppermute | solution.py:292
  156.7 0.6 collective-permute-start.20
  157.4 0.7 collective-permute-done.22
  158.0 3.2 %collective-permute-done.21 = f32[256]{0:T(256)S(1)} collective-permute-done((f32[256]{0:T(256)S(1)}, f32[256]{0:T(256)S(1)}, u32[]{:S(2)}, u32[]{:S(2)}) %collective-permute-start.21) | collective-permute-done | bytes 1056 | tf_op jit(solution)/shard_map/ppermute | solution.py:292
  161.2 0.9 collective-permute-done.20
  162.1 1.3 fusion.2
  (58 shorter events, 1.0 us)
Async XLA Ops:
  0.6 47.9 %copy-start = (bf16[2048,4,64]{0,2,1:T(8,128)(2,1)S(1)}, bf16[2048,4,64]{0,2,1:T(8,128)(2,1)}, u32[]{:S(2)}) copy-start(bf16[2048,4,64]{0,2,1:T(8,128)(2,1)} %param.16) | copy-start | bytes 3145732
  0.6 17.7 %collective-permute-start = (bf16[2048,2048]{1,0:T(8,128)(2,1)}, bf16[2048,2048]{1,0:T(8,128)(2,1)}, u32[]{:S(2)}, u32[]{:S(2)}) collective-permute-start(bf16[2048,2048]{1,0:T(8,128)(2,1)} %param.15), channel_id=1, source_target_pairs={{0,1},{1,0},{2,3},{3,2},{4,5},{5,4},{6,7},{7,6},{8,9},{9,8},{10,11... | collective-permute-start | bytes 25165832 | tf_op jit(solution)/shard_map/ppermute | solution.py:30
  4.2 26.9 %collective-permute-start.1 = (bf16[2048,256]{1,0:T(8,128)(2,1)}, bf16[2048,256]{1,0:T(8,128)(2,1)S(1)}, u32[]{:S(2)}, u32[]{:S(2)}) collective-permute-start(bf16[2048,256]{1,0:T(8,128)(2,1)} %get-tuple-element.39), channel_id=1, source_target_pairs={{0,4},{4,0},{8,12},{12,8},{1,5},{5,1},{9,13},{13,9},{2,6},{6,2},{1... | collective-permute-start | bytes 3145736 | tf_op jit(solution)/shard_map/ppermute | solution.py:30
  7.8 26.1 %collective-permute-start.2 = (bf16[256,256]{1,0:T(8,128)(2,1)S(1)}, bf16[256,256]{1,0:T(8,128)(2,1)S(1)}, u32[]{:S(2)}, u32[]{:S(2)}) collective-permute-start(bf16[256,256]{1,0:T(8,128)(2,1)S(1)} %constant_dynamic-slice_fusion), channel_id=1, source_target_pairs={{0,4},{4,0},{8,12},{12,8},{1,5},{5,1},{9,13},{13,9},{2,6},{6,2},{1... | collective-permute-start | bytes 393224 | tf_op jit(solution)/shard_map/ppermute | solution.py:30
  7.8 51.6 %collective-permute-start.3 = (bf16[2048,256]{1,0:T(8,128)(2,1)}, bf16[2048,256]{1,0:T(8,128)(2,1)S(1)}, u32[]{:S(2)}, u32[]{:S(2)}) collective-permute-start(bf16[2048,256]{1,0:T(8,128)(2,1)} %get-tuple-element.38), channel_id=1, source_target_pairs={{0,4},{4,0},{8,12},{12,8},{1,5},{5,1},{9,13},{13,9},{2,6},{6,2},{1... | collective-permute-start | bytes 3145736 | tf_op jit(solution)/shard_map/ppermute | solution.py:30
  18.4 15.5 %copy-start.1 = (bf16[2,2048,512]{2,1,0:T(8,128)(2,1)S(1)}, bf16[2,2048,512]{2,1,0:T(8,128)(2,1)}, u32[]{:S(2)}) copy-start(bf16[2,2048,512]{2,1,0:T(8,128)(2,1)} %own_past.3) | copy-start | bytes 12582916
  18.4 15.5 %copy-start.2 = (bf16[256,512]{1,0:T(8,128)(2,1)S(1)}, bf16[256,512]{1,0:T(8,128)(2,1)}, u32[]{:S(2)}) copy-start(bf16[256,512]{1,0:T(8,128)(2,1)} %own_new.3) | copy-start | bytes 786436
  18.4 15.5 %copy-start.3 = (bf16[256,2048]{1,0:T(8,128)(2,1)S(1)}, bf16[256,2048]{1,0:T(8,128)(2,1)}, u32[]{:S(2)}) copy-start(bf16[256,2048]{1,0:T(8,128)(2,1)} %q_ref.3) | copy-start | bytes 3145732
  18.4 15.5 %copy-start.4 = (s32[2]{0:T(128)S(1)}, s32[2]{0:T(128)}, u32[]{:S(2)}) copy-start(s32[2]{0:T(128)} %length_ref.3) | copy-start | bytes 28
  43.9 3.4 %copy-start.5 = (bf16[2048,2048]{1,0:T(8,128)(2,1)S(1)}, bf16[2048,2048]{1,0:T(8,128)(2,1)}, u32[]{:S(2)}) copy-start(bf16[2048,2048]{1,0:T(8,128)(2,1)} %get-tuple-element.20) | copy-start | bytes 25165828
  43.9 13.4 %collective-permute-start.4 = (bf16[128,2048]{1,0:T(8,128)(2,1)S(1)}, bf16[128,2048]{1,0:T(8,128)(2,1)S(1)}, u32[]{:S(2)}, u32[]{:S(2)}) collective-permute-start(bf16[128,2048]{1,0:T(8,128)(2,1)S(1)} %attend.2), channel_id=1, source_target_pairs={{0,2},{2,0},{1,3},{3,1},{4,6},{6,4},{5,7},{7,5},{8,10},{10,8},{9,1... | collective-permute-start | bytes 1572872 | tf_op jit(solution)/shard_map/ppermute | solution.py:30
  49.2 33.7 %collective-permute-start.5 = (bf16[128,2176]{1,0:T(8,128)(2,1)S(1)}, bf16[128,2176]{1,0:T(8,128)(2,1)S(1)}, u32[]{:S(2)}, u32[]{:S(2)}) collective-permute-start(bf16[128,2176]{1,0:T(8,128)(2,1)S(1)} %pad_maximum_fusion), channel_id=1, source_target_pairs={{0,4},{4,0},{8,12},{12,8},{1,5},{5,1},{9,13},{13,9},{2,6},{6,2},{1... | collective-permute-start | bytes 1671176 | tf_op jit(solution)/shard_map/ppermute | solution.py:30
  69.6 22.5 %collective-permute-start.12 = (bf16[128,2048]{1,0:T(8,128)(2,1)S(1)}, bf16[128,2048]{1,0:T(8,128)(2,1)S(1)}, u32[]{:S(2)}, u32[]{:S(2)}) collective-permute-start(bf16[128,2048]{1,0:T(8,128)(2,1)S(1)} %attend.3), channel_id=1, source_target_pairs={{0,2},{2,0},{1,3},{3,1},{4,6},{6,4},{5,7},{7,5},{8,10},{10,8},{9,1... | collective-permute-start | bytes 1572872 | tf_op jit(solution)/shard_map/ppermute | solution.py:30
  76.3 9.5 %collective-permute-start.6 = (bf16[128,1024]{1,0:T(8,128)(2,1)}, bf16[128,1024]{1,0:T(8,128)(2,1)S(1)}, u32[]{:S(2)}, u32[]{:S(2)}) collective-permute-start(bf16[128,1024]{1,0:T(8,128)(2,1)} %get-tuple-element.45), channel_id=1, source_target_pairs={{0,4},{4,0},{8,12},{12,8},{1,5},{5,1},{9,13},{13,9},{2,6},{6,2},{1... | collective-permute-start | bytes 786440 | tf_op jit(solution)/shard_map/ppermute | solution.py:30
  77.9 13.5 %collective-permute-start.9 = (bf16[128,1024]{1,0:T(8,128)(2,1)}, bf16[128,1024]{1,0:T(8,128)(2,1)S(1)}, u32[]{:S(2)}, u32[]{:S(2)}) collective-permute-start(bf16[128,1024]{1,0:T(8,128)(2,1)} %get-tuple-element.44), channel_id=1, source_target_pairs={{0,4},{4,0},{8,12},{12,8},{1,5},{5,1},{9,13},{13,9},{2,6},{6,2},{1... | collective-permute-start | bytes 786440 | tf_op jit(solution)/shard_map/ppermute | solution.py:30
  79.8 12.3 %slice-start = ((s8[8388608]{0:T(1024)(128)(4,1)}), s8[4194304]{0:T(1024)(128)(4,1)S(1)}, s32[]{:S(2)}) async-start(s8[8388608]{0:T(1024)(128)(4,1)} %bitcast.34), calls=%async_computation | async-start | bytes 8388608
  79.9 12.2 %slice-start.1 = ((s8[8388608]{0:T(1024)(128)(4,1)}), s8[4194304]{0:T(1024)(128)(4,1)S(1)}, s32[]{:S(2)}) async-start(s8[8388608]{0:T(1024)(128)(4,1)} %bitcast.34), calls=%async_computation.1 | async-start | bytes 8388608
  79.9 35.4 %collective-permute-start.13 = (bf16[128,2176]{1,0:T(8,128)(2,1)S(1)}, bf16[128,2176]{1,0:T(8,128)(2,1)S(1)}, u32[]{:S(2)}, u32[]{:S(2)}) collective-permute-start(bf16[128,2176]{1,0:T(8,128)(2,1)S(1)} %pad_maximum_fusion.1), channel_id=1, source_target_pairs={{0,4},{4,0},{8,12},{12,8},{1,5},{5,1},{9,13},{13,9},{2,6},{6,2},{1... | collective-permute-start | bytes 1671176 | tf_op jit(solution)/shard_map/ppermute | solution.py:30
  85.9 9.6 %collective-permute-start.7 = (bf16[128,1024]{1,0:T(8,128)(2,1)S(1)}, bf16[128,1024]{1,0:T(8,128)(2,1)S(1)}, u32[]{:S(2)}, u32[]{:S(2)}) collective-permute-start(bf16[128,1024]{1,0:T(8,128)(2,1)S(1)} %add_convert_fusion.10), channel_id=1, source_target_pairs={{0,2},{2,0},{1,3},{3,1},{4,6},{6,4},{5,7},{7,5},{8,10},{10,8},{9,1... | collective-permute-start | bytes 786440 | tf_op jit(solution)/shard_map/ppermute | solution.py:30
  91.5 8.2 %collective-permute-start.10 = (bf16[128,1024]{1,0:T(8,128)(2,1)S(1)}, bf16[128,1024]{1,0:T(8,128)(2,1)S(1)}, u32[]{:S(2)}, u32[]{:S(2)}) collective-permute-start(bf16[128,1024]{1,0:T(8,128)(2,1)S(1)} %add_convert_fusion.7), channel_id=1, source_target_pairs={{0,2},{2,0},{1,3},{3,1},{4,6},{6,4},{5,7},{7,5},{8,10},{10,8},{9,1... | collective-permute-start | bytes 786440 | tf_op jit(solution)/shard_map/ppermute | solution.py:30
  93.4 31.1 %collective-permute-start.17 = (bf16[128,1024]{1,0:T(8,128)(2,1)S(1)}, bf16[128,1024]{1,0:T(8,128)(2,1)S(1)}, u32[]{:S(2)}, u32[]{:S(2)}) collective-permute-start(bf16[128,1024]{1,0:T(8,128)(2,1)S(1)} %get-tuple-element.43), channel_id=1, source_target_pairs={{0,4},{4,0},{8,12},{12,8},{1,5},{5,1},{9,13},{13,9},{2,6},{6,2},{1... | collective-permute-start | bytes 786440 | tf_op jit(solution)/shard_map/ppermute | solution.py:30
  95.1 28.4 %collective-permute-start.14 = (bf16[128,1024]{1,0:T(8,128)(2,1)S(1)}, bf16[128,1024]{1,0:T(8,128)(2,1)S(1)}, u32[]{:S(2)}, u32[]{:S(2)}) collective-permute-start(bf16[128,1024]{1,0:T(8,128)(2,1)S(1)} %get-tuple-element.42), channel_id=1, source_target_pairs={{0,4},{4,0},{8,12},{12,8},{1,5},{5,1},{9,13},{13,9},{2,6},{6,2},{1... | collective-permute-start | bytes 786440 | tf_op jit(solution)/shard_map/ppermute | solution.py:30
  95.7 30.1 %copy-start.8 = (bf16[64,2048]{1,0:T(8,128)(2,1)S(1)}, bf16[64,2048]{1,0:T(8,128)(2,1)}, u32[]{:S(2)}) copy-start(bf16[64,2048]{1,0:T(8,128)(2,1)} %get-tuple-element.40) | copy-start | bytes 786436
  95.7 30.1 %copy-start.10 = (bf16[256,2048]{1,0:T(8,128)(2,1)S(1)}, bf16[256,2048]{1,0:T(8,128)(2,1)}, u32[]{:S(2)}) copy-start(bf16[256,2048]{1,0:T(8,128)(2,1)} %param.18) | copy-start | bytes 3145732
  95.7 27.8 %collective-permute-start.8 = (bf16[128,1152]{1,0:T(8,128)(2,1)S(1)}, bf16[128,1152]{1,0:T(8,128)(2,1)S(1)}, u32[]{:S(2)}, u32[]{:S(2)}) collective-permute-start(bf16[128,1152]{1,0:T(8,128)(2,1)S(1)} %pad_maximum_fusion.2), channel_id=1, source_target_pairs={{0,8},{8,0},{4,12},{12,4},{1,9},{9,1},{5,13},{13,5},{2,10},{10,2},... | collective-permute-start | bytes 884744 | tf_op jit(solution)/shard_map/ppermute | solution.py:30
  99.7 50.9 %copy-start.7 = (bf16[64,2048]{1,0:T(8,128)(2,1)S(1)}, bf16[64,2048]{1,0:T(8,128)(2,1)}, u32[]{:S(2)}) copy-start(bf16[64,2048]{1,0:T(8,128)(2,1)} %get-tuple-element.41) | copy-start | bytes 786436
  99.7 57.6 %copy-start.9 = (bf16[2048]{0:T(1024)(128)(2,1)S(1)}, bf16[2048]{0:T(1024)(128)(2,1)}, u32[]{:S(2)}) copy-start(bf16[2048]{0:T(1024)(128)(2,1)} %param.19) | copy-start | bytes 12292
  99.9 26.0 %collective-permute-start.11 = (bf16[128,1024]{1,0:T(8,128)(2,1)S(1)}, bf16[128,1024]{1,0:T(8,128)(2,1)S(1)}, u32[]{:S(2)}, u32[]{:S(2)}) collective-permute-start(bf16[128,1024]{1,0:T(8,128)(2,1)S(1)} %broadcast_select_fusion.4), channel_id=1, source_target_pairs={{0,8},{8,0},{4,12},{12,4},{1,9},{9,1},{5,13},{13,5},{2,10},{10,2},... | collective-permute-start | bytes 786440 | tf_op jit(solution)/shard_map/ppermute | solution.py:30
  123.6 8.1 %collective-permute-start.15 = (bf16[128,1024]{1,0:T(8,128)(2,1)S(1)}, bf16[128,1024]{1,0:T(8,128)(2,1)S(1)}, u32[]{:S(2)}, u32[]{:S(2)}) collective-permute-start(bf16[128,1024]{1,0:T(8,128)(2,1)S(1)} %add_convert_fusion.4), channel_id=1, source_target_pairs={{0,2},{2,0},{1,3},{3,1},{4,6},{6,4},{5,7},{7,5},{8,10},{10,8},{9,1... | collective-permute-start | bytes 786440 | tf_op jit(solution)/shard_map/ppermute | solution.py:30
  124.6 9.9 %collective-permute-start.18 = (bf16[128,1024]{1,0:T(8,128)(2,1)S(1)}, bf16[128,1024]{1,0:T(8,128)(2,1)S(1)}, u32[]{:S(2)}, u32[]{:S(2)}) collective-permute-start(bf16[128,1024]{1,0:T(8,128)(2,1)S(1)} %add_convert_fusion.1), channel_id=1, source_target_pairs={{0,2},{2,0},{1,3},{3,1},{4,6},{6,4},{5,7},{7,5},{8,10},{10,8},{9,1... | collective-permute-start | bytes 786440 | tf_op jit(solution)/shard_map/ppermute | solution.py:30
  131.8 18.7 %collective-permute-start.16 = (bf16[128,1152]{1,0:T(8,128)(2,1)S(1)}, bf16[128,1152]{1,0:T(8,128)(2,1)S(1)}, u32[]{:S(2)}, u32[]{:S(2)}) collective-permute-start(bf16[128,1152]{1,0:T(8,128)(2,1)S(1)} %pad_maximum_fusion.3), channel_id=1, source_target_pairs={{0,8},{8,0},{4,12},{12,4},{1,9},{9,1},{5,13},{13,5},{2,10},{10,2},... | collective-permute-start | bytes 884744 | tf_op jit(solution)/shard_map/ppermute | solution.py:30
  134.6 18.9 %collective-permute-start.19 = (bf16[128,1024]{1,0:T(8,128)(2,1)S(1)}, bf16[128,1024]{1,0:T(8,128)(2,1)S(1)}, u32[]{:S(2)}, u32[]{:S(2)}) collective-permute-start(bf16[128,1024]{1,0:T(8,128)(2,1)S(1)} %broadcast_select_fusion.2), channel_id=1, source_target_pairs={{0,8},{8,0},{4,12},{12,4},{1,9},{9,1},{5,13},{13,5},{2,10},{10,2},... | collective-permute-start | bytes 786440 | tf_op jit(solution)/shard_map/ppermute | solution.py:30
  154.0 9.3 %copy-start.6 = (bf16[256,2048]{1,0:T(8,128)(2,1)}, bf16[256,2048]{1,0:T(8,128)(2,1)S(1)}, u32[]{:S(2)}) copy-start(bf16[256,2048]{1,0:T(8,128)(2,1)S(1)} %get-tuple-element.35) | copy-start | bytes 3145732
  154.1 4.0 %collective-permute-start.22 = (f32[256]{0:T(256)S(1)}, f32[256]{0:T(256)S(1)}, u32[]{:S(2)}, u32[]{:S(2)}) collective-permute-start(f32[256]{0:T(256)S(1)} %get-tuple-element.34), channel_id=1, source_target_pairs={{0,12},{4,0},{8,4},{12,8},{1,13},{5,1},{9,5},{13,9},{2,14},{6,2},{... | collective-permute-start | bytes 3080 | tf_op jit(solution)/shard_map/ppermute | solution.py:292
  156.7 4.5 %collective-permute-start.21 = (f32[256]{0:T(256)S(1)}, f32[256]{0:T(256)S(1)}, u32[]{:S(2)}, u32[]{:S(2)}) collective-permute-start(f32[256]{0:T(256)S(1)} %get-tuple-element.34), channel_id=1, source_target_pairs={{0,8},{4,12},{8,0},{12,4},{1,9},{5,13},{9,1},{13,5},{2,10},{6,14},... | collective-permute-start | bytes 3080 | tf_op jit(solution)/shard_map/ppermute | solution.py:292
  156.7 5.4 %collective-permute-start.20 = (f32[256]{0:T(256)S(1)}, f32[256]{0:T(256)S(1)}, u32[]{:S(2)}, u32[]{:S(2)}) collective-permute-start(f32[256]{0:T(256)S(1)} %get-tuple-element.34), channel_id=1, source_target_pairs={{0,4},{4,8},{8,12},{12,0},{1,5},{5,9},{9,13},{13,1},{2,6},{6,10},{... | collective-permute-start | bytes 3080 | tf_op jit(solution)/shard_map/ppermute | solution.py:292
